TPU v7x, 256 devices: a whole 4x4x8 slice. The times are simulated.
256 devices in a mesh: dp: 8 (over x, core), tensor: 32 (over z, y).
Axes of the slice: x: 4, y: 4, z: 8, core: 2. Of those that a mesh axis runs over, the one named last changes fastest.
Arguments:
- inputs: bfloat16 [4, 128, 8192], P(None, 'tensor', 'dp'), may hold values from -6 to 6
- grad_out: bfloat16 [4, 128, 8192], P(None, 'tensor', 'dp'), may hold values from -6 to 6
- gate_pre: bfloat16 [4, 128, 28672], P(None, 'dp', 'tensor'), may hold values from -6 to 6
- up_pre: bfloat16 [4, 128, 28672], P(None, 'dp', 'tensor'), may hold values from -6 to 6
- gate_weight: bfloat16 [8192, 28672], P('dp', 'tensor'), may hold values from -0.0625 to 0.0625
- up_weight: bfloat16 [8192, 28672], P('dp', 'tensor'), may hold values from -0.0625 to 0.0625
- down_weight: bfloat16 [8192, 28672], P('dp', 'tensor'), may hold values from -0.03125 to 0.03125
Outputs:
- input_grads: bfloat16 [4, 128, 8192], P(None, 'tensor', 'dp')
- gate_grad: bfloat16 [8192, 28672], P('dp', 'tensor')
- up_grad: bfloat16 [8192, 28672], P('dp', 'tensor')
- down_grad: bfloat16 [8192, 28672], P('dp', 'tensor')
All inputs are finite; a program needn't handle non-finite values.
Results may differ from a plain program's by a relative error of at most 0.0049.
Values may be sent and summed in bfloat16 or wider, within the bound.
No kernel may reach another device: no remote copies, remote signals or barrier semaphores. Data moves between devices by JAX's collectives and lax.ppermute only.
A program may use at most 128 MiB of HBM per device.

v0:
```python
import jax
import jax.numpy as jnp
from jax import lax
from jax.sharding import PartitionSpec as P

FF = 28672
G = 4


def swish_terms(d_hidden, gate_part, up_part):
    gate_float = gate_part.astype(jnp.float32)
    up_float = up_part.astype(jnp.float32)
    sigmoid_val = jax.nn.sigmoid(gate_float)
    active = gate_float * sigmoid_val
    d_gate = (d_hidden * up_float * sigmoid_val * (1.0 + gate_float * (1.0 - sigmoid_val))).astype(
        jnp.bfloat16
    )
    d_up = (d_hidden * active).astype(jnp.bfloat16)
    hidden = (active * up_float).astype(jnp.bfloat16)
    return (d_gate, d_up, hidden)


def contract_rows(left_arr, right_arr):
    return lax.dot_general(
        left_arr, right_arr, (((0,), (0,)), ((), ())), preferred_element_type=jnp.float32
    )


def contract_cols(left_arr, right_arr):
    return lax.dot_general(
        left_arr, right_arr, (((1,), (1,)), ((), ())), preferred_element_type=jnp.float32
    )


def guarded(is_live, work, shapes):
    return lax.cond(
        is_live, work, lambda: tuple((jnp.zeros(shape_one, jnp.float32) for shape_one in shapes))
    )


def shards(inputs, grad_out, gate_pre, up_pre, gate_weight, up_weight, down_weight):
    width_rows = gate_weight.shape[0]
    columns = gate_weight.shape[1]
    whole_in, whole_grad = (
        lax.all_gather(inputs, "tensor", axis=1, tiled=True),
        lax.all_gather(grad_out, "tensor", axis=1, tiled=True),
    )
    tokens_all = whole_in.shape[1]
    prefixes = [FF // 2 ** (G - 1 - granule) for granule in range(G)]
    column_start = lax.axis_index("tensor") * columns
    widths = [columns] * G
    lives = [column_start < prefix_cols for prefix_cols in prefixes]
    d_gates = []
    d_ups = []
    hiddens = []
    in_grads = []
    for granule in range(G):
        width_now = widths[granule]
        is_live = lives[granule]
        grad_rows = whole_grad[granule]
        partial_sum = guarded(
            is_live,
            lambda: (jnp.dot(grad_rows, down_weight, preferred_element_type=jnp.float32),),
            [(tokens_all, width_now)],
        )[0]
        d_share = lax.psum_scatter(partial_sum, "dp", scatter_dimension=0, tiled=True)
        share_gate, share_up, share_hidden = swish_terms(
            d_share, gate_pre[granule], up_pre[granule]
        )
        d_gate = lax.all_gather(share_gate, "dp", axis=0, tiled=True)
        d_up = lax.all_gather(share_up, "dp", axis=0, tiled=True)
        hidden = lax.all_gather(share_hidden, "dp", axis=0, tiled=True)
        input_term = guarded(
            is_live,
            lambda: (contract_cols(d_gate, gate_weight) + contract_cols(d_up, up_weight),),
            [(tokens_all, width_rows)],
        )[0]
        in_grads.append(
            lax.psum_scatter(input_term, "tensor", scatter_dimension=0, tiled=True).astype(
                jnp.bfloat16
            )
        )
        d_gates.append(d_gate)
        d_ups.append(d_up)
        hiddens.append(hidden)
    gate_blocks = []
    up_blocks = []
    down_blocks = []
    start_col = 0
    for granule in range(G):
        stop_col = widths[granule]
        if stop_col > start_col:
            span_cols = stop_col - start_col
            totals = tuple(
                (jnp.zeros((width_rows, span_cols), jnp.float32) for copy_index in range(3))
            )
            for later_granule in range(granule, G):
                in_rows = whole_in[later_granule]
                out_rows = whole_grad[later_granule]
                gate_part = d_gates[later_granule]
                up_part = d_ups[later_granule]
                hidden_part = hiddens[later_granule]
                terms = guarded(
                    lives[later_granule],
                    lambda: (
                        contract_rows(in_rows, gate_part),
                        contract_rows(in_rows, up_part),
                        contract_rows(out_rows, hidden_part),
                    ),
                    [(width_rows, span_cols)] * 3,
                )
                totals = tuple((total_one + term_one for total_one, term_one in zip(totals, terms)))
            gate_blocks.append(totals[0])
            up_blocks.append(totals[1])
            down_blocks.append(totals[2])
            start_col = stop_col
    gate_grad = gate_blocks[0].astype(jnp.bfloat16)
    up_grad = up_blocks[0].astype(jnp.bfloat16)
    down_grad = down_blocks[0].astype(jnp.bfloat16)
    return (jnp.stack(in_grads), gate_grad, up_grad, down_grad)


def solution(mesh):
    in_specs = (
        P(None, "tensor", "dp"),
        P(None, "tensor", "dp"),
        P(None, "dp", "tensor"),
        P(None, "dp", "tensor"),
        P("dp", "tensor"),
        P("dp", "tensor"),
        P("dp", "tensor"),
    )
    out_specs = (P(None, "tensor", "dp"), P("dp", "tensor"), P("dp", "tensor"), P("dp", "tensor"))
    return jax.shard_map(shards, mesh=mesh, in_specs=in_specs, out_specs=out_specs, check_vma=False)
```

profile of v0, /device:TPU:40, one launch (start us, length us, event | category | flops | bytes accessed | tf_op | source)
XLA Modules:
  0.0 622.5 jit_solution(5947939000728880707)
XLA Ops:
  8.8 79.6 %all-gather.3.cloned.1.call-done = bf16[4,128,1024]{2,0,1:T(4,128)(2,1)} async-done(((bf16[4,4,1024]{2,0,1:T(4,128)(2,1)}), bf16[4,128,1024]{2,0,1:T(4,128)(2,1)}) %all-gather.3.cloned.1.call-update) | async-done | bytes 1048592 | tf_op jit(solution)/shard_map/all_gather | solution.py:46
  88.4 5.0 fusion.44
  102.5 24.6 %reduce-scatter.5.cloned.1.call-done = f32[16,896]{1,0:T(8,128)} async-done(((f32[128,896]{1,0:T(8,128)}), f32[16,896]{1,0:T(8,128)}) %reduce-scatter.5.cloned.1.call-update) | async-done | bytes 57360 | tf_op jit(solution)/shard_map/reduce_scatter | solution.py:66
  127.1 35.5 %reduce-scatter.7.cloned.1.call-done = f32[16,896]{1,0:T(8,128)} async-done(((f32[128,896]{1,0:T(8,128)}), f32[16,896]{1,0:T(8,128)}) %reduce-scatter.7.cloned.1.call-update) | async-done | bytes 57360 | tf_op jit(solution)/shard_map/reduce_scatter | solution.py:66
  162.6 34.6 %reduce-scatter.11.cloned.1.call-done = f32[16,896]{1,0:T(8,128)} async-done(((f32[128,896]{1,0:T(8,128)}), f32[16,896]{1,0:T(8,128)}) %reduce-scatter.11.cloned.1.call-update) | async-done | bytes 57360 | tf_op jit(solution)/shard_map/reduce_scatter | solution.py:66
  198.9 12.8 %all_gather.49 = bf16[128,896]{1,0:T(8,128)(2,1)S(1)} all-gather(bf16[16,896]{1,0:T(8,128)(2,1)S(1)} %get-tuple-element.246), channel_id=1, replica_groups=mesh['dp'=8,'tensor'=32] {'dp'}, dimensions={0}, use_global_device_ids=true | all-gather | bytes 258048 | tf_op jit(solution)/shard_map/all_gather | solution.py:70
  211.7 20.9 %reduce-scatter.9.cloned.1.call-done = f32[16,896]{1,0:T(8,128)} async-done(((f32[128,896]{1,0:T(8,128)}), f32[16,896]{1,0:T(8,128)}) %reduce-scatter.9.cloned.1.call-update) | async-done | bytes 57360 | tf_op jit(solution)/shard_map/reduce_scatter | solution.py:66
  233.5 13.9 %all_gather.50 = bf16[128,896]{1,0:T(8,128)(2,1)} all-gather(bf16[16,896]{1,0:T(8,128)(2,1)S(1)} %get-tuple-element.251), channel_id=1, replica_groups=mesh['dp'=8,'tensor'=32] {'dp'}, dimensions={0}, use_global_device_ids=true | all-gather | bytes 258048 | tf_op jit(solution)/shard_map/all_gather | solution.py:71
  247.4 4.6 conditional.19
  249.6 2.4 convolution_add_fusion.3
  252.0 13.9 %all_gather.48 = bf16[128,896]{1,0:T(8,128)(2,1)} all-gather(bf16[16,896]{1,0:T(8,128)(2,1)S(1)} %get-tuple-element.249), channel_id=1, replica_groups=mesh['dp'=8,'tensor'=32] {'dp'}, dimensions={0}, use_global_device_ids=true | all-gather | bytes 258048 | tf_op jit(solution)/shard_map/all_gather | solution.py:71
  265.9 13.9 %all_gather.47 = bf16[128,896]{1,0:T(8,128)(2,1)} all-gather(bf16[16,896]{1,0:T(8,128)(2,1)S(1)} %get-tuple-element.250), channel_id=1, replica_groups=mesh['dp'=8,'tensor'=32] {'dp'}, dimensions={0}, use_global_device_ids=true | all-gather | bytes 258048 | tf_op jit(solution)/shard_map/all_gather | solution.py:70
  279.7 4.8 conditional.17
  282.1 2.4 convolution_add_fusion.2
  284.5 13.9 %all_gather.45 = bf16[128,896]{1,0:T(8,128)(2,1)} all-gather(bf16[16,896]{1,0:T(8,128)(2,1)S(1)} %get-tuple-element.244), channel_id=1, replica_groups=mesh['dp'=8,'tensor'=32] {'dp'}, dimensions={0}, use_global_device_ids=true | all-gather | bytes 258048 | tf_op jit(solution)/shard_map/all_gather | solution.py:70
  298.4 13.9 %all_gather.46 = bf16[128,896]{1,0:T(8,128)(2,1)} all-gather(bf16[16,896]{1,0:T(8,128)(2,1)S(1)} %get-tuple-element.248), channel_id=1, replica_groups=mesh['dp'=8,'tensor'=32] {'dp'}, dimensions={0}, use_global_device_ids=true | all-gather | bytes 258048 | tf_op jit(solution)/shard_map/all_gather | solution.py:71
  312.3 4.7 conditional.15
  312.3 2.3 fusion.50
  314.6 2.4 convolution_add_fusion.1
  317.0 13.9 %all_gather.43 = bf16[128,896]{1,0:T(8,128)(2,1)} all-gather(bf16[16,896]{1,0:T(8,128)(2,1)S(1)} %get-tuple-element.245), channel_id=1, replica_groups=mesh['dp'=8,'tensor'=32] {'dp'}, dimensions={0}, use_global_device_ids=true | all-gather | bytes 258048 | tf_op jit(solution)/shard_map/all_gather | solution.py:70
  330.9 13.9 %all_gather.44 = bf16[128,896]{1,0:T(8,128)(2,1)} all-gather(bf16[16,896]{1,0:T(8,128)(2,1)S(1)} %get-tuple-element.247), channel_id=1, replica_groups=mesh['dp'=8,'tensor'=32] {'dp'}, dimensions={0}, use_global_device_ids=true | all-gather | bytes 258048 | tf_op jit(solution)/shard_map/all_gather | solution.py:71
  344.9 14.1 %all_gather.53 = bf16[128,896]{1,0:T(8,128)(2,1)} all-gather(bf16[16,896]{1,0:T(8,128)(2,1)S(1)} %copy-done.29), channel_id=1, replica_groups=mesh['dp'=8,'tensor'=32] {'dp'}, dimensions={0}, use_global_device_ids=true | all-gather | bytes 258048 | tf_op jit(solution)/shard_map/all_gather | solution.py:72
  358.9 13.9 %all_gather.52 = bf16[128,896]{1,0:T(8,128)(2,1)} all-gather(bf16[16,896]{1,0:T(8,128)(2,1)S(1)} %copy-done.28), channel_id=1, replica_groups=mesh['dp'=8,'tensor'=32] {'dp'}, dimensions={0}, use_global_device_ids=true | all-gather | bytes 258048 | tf_op jit(solution)/shard_map/all_gather | solution.py:72
  372.8 13.9 %all_gather.54 = bf16[128,896]{1,0:T(8,128)(2,1)} all-gather(bf16[16,896]{1,0:T(8,128)(2,1)S(1)} %copy-done.27), channel_id=1, replica_groups=mesh['dp'=8,'tensor'=32] {'dp'}, dimensions={0}, use_global_device_ids=true | all-gather | bytes 258048 | tf_op jit(solution)/shard_map/all_gather | solution.py:72
  386.7 13.9 %all_gather.55 = bf16[128,896]{1,0:T(8,128)(2,1)} all-gather(bf16[16,896]{1,0:T(8,128)(2,1)S(1)} %get-tuple-element.243), channel_id=1, replica_groups=mesh['dp'=8,'tensor'=32] {'dp'}, dimensions={0}, use_global_device_ids=true | all-gather | bytes 258048 | tf_op jit(solution)/shard_map/all_gather | solution.py:72
  400.5 160.4 %all-reduce.6 = (bf16[128,1024]{1,0:T(8,128)(2,1)}, bf16[128,1024]{1,0:T(8,128)(2,1)}, bf16[128,1024]{1,0:T(8,128)(2,1)}, bf16[128,1024]{1,0:T(8,128)(2,1)}) all-reduce(f32[128,1024]{1,0:T(8,128)S(1)} %get-tuple-element.285, f32[128,1024]{1,0:T(8,128)S(1)} %get-tuple-element.283, ...), channel_id=9, replica_groups=mesh['dp'=8,'tensor'=32] {'tensor'}, use_global_device_ids=true, to_apply=%region_23.0.clone | all-reduce | flops 524288 | bytes 3145728
  568.8 5.4 conditional.21
  578.4 5.6 conditional.22
  588.1 4.5 conditional.23
  596.6 7.3 %add_convert_fusion = bf16[1024,896]{1,0:T(8,128)(2,1)} fusion(f32[1024,896]{1,0:T(8,128)} %copy-done.15, f32[1024,896]{1,0:T(8,128)} %copy-done.11, f32[1024,896]{1,0:T(8,128)} %copy-done.1, f32[1024,896]{1,0:T(8,128)} %copy-done.6), kind=kLoop, calls=%fused_computation.16 | loop fusion | flops 3670016 | bytes 16515072 | tf_op jit(solution)/shard_map/convert_element_type | solution.py:119
  605.7 4.4 add_convert_fusion.1
  610.1 5.5 add_convert_fusion.2
  (112 shorter events, 57.8 us)
Async XLA Ops:
  7.2 86.4 %copy-start = (bf16[1024,896]{1,0:T(8,128)(2,1)S(1)}, bf16[1024,896]{1,0:T(8,128)(2,1)}, u32[]{:S(2)}) copy-start(bf16[1024,896]{1,0:T(8,128)(2,1)} %param.37) | copy-start | bytes 5505028
  7.2 81.2 %all-gather.3.cloned.1.call-start = ((), (), s32[]{:S(2)}) async-start(), calls=%async_computation.4 | async-start | bytes 1081344 | tf_op jit(solution)/shard_map/all_gather | solution.py:46
  8.8 118.3 %reduce-scatter.5.cloned.1.call-start = ((), (), s32[]{:S(2)}) async-start(), calls=%async_computation.5 | async-start | bytes 516096 | tf_op jit(solution)/shard_map/reduce_scatter | solution.py:66
  94.4 68.2 %reduce-scatter.7.cloned.1.call-start = ((), (), s32[]{:S(2)}) async-start(), calls=%async_computation.6 | async-start | bytes 516096 | tf_op jit(solution)/shard_map/reduce_scatter | solution.py:66
  95.7 2.7 copy-start.18
  96.9 100.3 %reduce-scatter.11.cloned.1.call-start = ((), (), s32[]{:S(2)}) async-start(), calls=%async_computation.8 | async-start | bytes 516096 | tf_op jit(solution)/shard_map/reduce_scatter | solution.py:66
  97.0 2.8 copy-start.30
  97.0 100.2 %copy-start.26 = (bf16[4,16,896]{2,1,0:T(8,128)(2,1)S(1)}, bf16[4,16,896]{2,1,0:T(8,128)(2,1)}, u32[]{:S(2)}) copy-start(bf16[4,16,896]{2,1,0:T(8,128)(2,1)} %param.33) | copy-start | bytes 344068
  98.3 134.3 %reduce-scatter.9.cloned.1.call-start = ((), (), s32[]{:S(2)}) async-start(), calls=%async_computation.7 | async-start | bytes 516096 | tf_op jit(solution)/shard_map/reduce_scatter | solution.py:66
  99.7 464.1 %all-gather.5.cloned.1.call-start = ((), (), s32[]{:S(2)}) async-start(), calls=%async_computation.9 | async-start | bytes 1081344 | tf_op jit(solution)/shard_map/all_gather | solution.py:45
  317.0 27.9 %copy-start.29 = (bf16[16,896]{1,0:T(8,128)(2,1)S(1)}, bf16[16,896]{1,0:T(8,128)(2,1)}, u32[]{:S(2)}) copy-start(bf16[16,896]{1,0:T(8,128)(2,1)} %get-tuple-element.240) | copy-start | bytes 86020
  317.0 41.9 %copy-start.28 = (bf16[16,896]{1,0:T(8,128)(2,1)S(1)}, bf16[16,896]{1,0:T(8,128)(2,1)}, u32[]{:S(2)}) copy-start(bf16[16,896]{1,0:T(8,128)(2,1)} %get-tuple-element.241) | copy-start | bytes 86020
  317.0 55.8 %copy-start.27 = (bf16[16,896]{1,0:T(8,128)(2,1)S(1)}, bf16[16,896]{1,0:T(8,128)(2,1)}, u32[]{:S(2)}) copy-start(bf16[16,896]{1,0:T(8,128)(2,1)} %get-tuple-element.242) | copy-start | bytes 86020
  564.8 1.8 copy-start.1
  564.8 2.9 copy-start.2
  564.8 4.0 copy-start.4
  564.8 9.4 %copy-start.24 = (bf16[128,896]{1,0:T(8,128)(2,1)S(1)}, bf16[128,896]{1,0:T(8,128)(2,1)}, u32[]{:S(2)}) copy-start(bf16[128,896]{1,0:T(8,128)(2,1)} %all_gather.54) | copy-start | bytes 688132
  574.2 1.9 copy-start.6
  574.2 3.0 copy-start.7
  574.2 4.2 copy-start.9
  574.2 9.8 %copy-start.23 = (bf16[128,896]{1,0:T(8,128)(2,1)S(1)}, bf16[128,896]{1,0:T(8,128)(2,1)}, u32[]{:S(2)}) copy-start(bf16[128,896]{1,0:T(8,128)(2,1)} %all_gather.55) | copy-start | bytes 688132
  584.1 1.9 copy-start.11
  584.1 3.0 copy-start.12
  584.1 4.0 copy-start.14
  592.6 1.8 copy-start.15
  592.6 3.0 copy-start.16
  592.6 4.0 copy-start.17
  596.6 7.3 %copy-start.3 = (f32[1024,896]{1,0:T(8,128)S(1)}, f32[1024,896]{1,0:T(8,128)}, u32[]{:S(2)}) copy-start(f32[1024,896]{1,0:T(8,128)} %copy-done.2) | copy-start | bytes 11010052
  596.6 8.1 %copy-start.8 = (f32[1024,896]{1,0:T(8,128)S(1)}, f32[1024,896]{1,0:T(8,128)}, u32[]{:S(2)}) copy-start(f32[1024,896]{1,0:T(8,128)} %copy-done.7) | copy-start | bytes 11010052
  596.6 9.1 %copy-start.13 = (f32[1024,896]{1,0:T(8,128)S(1)}, f32[1024,896]{1,0:T(8,128)}, u32[]{:S(2)}) copy-start(f32[1024,896]{1,0:T(8,128)} %copy-done.12) | copy-start | bytes 11010052
  605.7 4.4 copy-start.5
  605.7 4.4 copy-start.10
  (3 other events, 2.5 us)
Sparse Core Ops, SparseCore 0:
  11.2 77.1 all-gather.2
  94.5 32.5 reduce-scatter.4
  130.3 32.2 reduce-scatter.6
  164.9 32.1 reduce-scatter.10
  200.3 32.2 reduce-scatter.8
  235.6 73.5 all-gather.4
where the time goes:
time: 635 us; the launch traced here: 622 us
  blocking collectives  326 us (51%)
  waiting for transfers between devices  195 us (31%)
  local copies, waits for them, and re-layouts  37.2 us (6%)
  matrix products  27.6 us (4%)
  other arithmetic  20.5 us (3%)
  between operations  15.2 us (2%)
    unnamed x1, blocking collectives  160 us
    reduce_scatter x4, waiting for transfers between devices, shards(): lax.psum_scatter(partial_sum, 'dp', scatter_dimension=0, tiled=True)  116 us
    all_gather x1, waiting for transfers between devices, shards(): lax.all_gather(grad_out, 'tensor', axis=1, tiled=True)  79.6 us
    all_gather x4, blocking collectives, shards(): hidden = lax.all_gather(share_hidden, 'dp', axis=0, tiled=True)  55.7 us
    all_gather x4, blocking collectives, shards(): d_up = lax.all_gather(share_up, 'dp', axis=0, tiled=True)  55.5 us
    all_gather x4, blocking collectives, shards(): d_gate = lax.all_gather(share_gate, 'dp', axis=0, tiled=True)  54.4 us
    unnamed x63, local copies, waits for them, and re-layouts  22.7 us
    dot_general x6, matrix products, contract_cols(): lax.dot_general(left_arr, right_arr, (((1,), (1,)), ((), ())), preferred_...  14 us
  transfers between devices with their start and end apart: 6, of which 5 were waited for; matrix products, arithmetic and copies ran while one was open for 4% of the time, Pallas kernels for 0%

commit v1 on v0

v1 whole, which is shorter than its diff:
```python
import functools

import jax
import jax.numpy as jnp
from jax import lax
from jax.experimental import pallas as pl
from jax.experimental.pallas import tpu as pltpu
from jax.sharding import PartitionSpec as P

FF = 28672
G = 4
X, C, Y, Z = 4, 2, 4, 8
BF = jnp.bfloat16
F32 = jnp.float32
VMEM_BYTES = 32 * 1024 * 1024
Z_GROUPS = [
    [(x * C + c) * Y * Z + ((x + dx) % X * C + (c ^ dc)) * Y + y for dc in range(C) for dx in range(X)]
    for x in range(X)
    for c in range(C)
    for y in range(Y)
]
CORE_SWAP = [(d, d ^ 1) for d in range(X * C)]


def from_x(block, step):
    return lax.ppermute(block, "dp", [((d // C + step) % X * C + d % C, d) for d in range(X * C)])


def from_y(block, step):
    return lax.ppermute(block, "tensor", [(t // Y * Y + (t % Y + step) % Y, t) for t in range(Y * Z)])


def swap_core(block):
    return lax.ppermute(block, "dp", CORE_SWAP)


def exchange_z(blocks):
    return lax.all_to_all(blocks, ("dp", "tensor"), 0, 0, axis_index_groups=Z_GROUPS)


def rows_dot(left, right):
    return lax.dot_general(left, right, (((0,), (0,)), ((), ())), preferred_element_type=F32)


def cols_dot(left, right):
    return lax.dot_general(left, right, (((1,), (1,)), ((), ())), preferred_element_type=F32)


def own_tokens(part, y):
    cols = part.shape[-1]
    part = part.reshape(G, Y, 4, cols).transpose(1, 0, 2, 3).reshape(Y, 16, cols)
    return lax.dynamic_slice_in_dim(jnp.concatenate([part, part]), y, Y, 0)


def half_kernel(core, *refs):
    pieces, weight_ref = refs[:Y], refs[Y]
    rows = [p[core * X : core * X + X].reshape(X * 16, p.shape[-1]) for p in pieces]
    part = jnp.dot(jnp.concatenate(rows), weight_ref[...], preferred_element_type=F32)
    if core == 1:
        refs[Y + 1][...] = part
        return
    theirs_ref, own_ref, sent_refs = refs[Y + 1], refs[Y + 2], refs[Y + 3 :]
    part = (part + theirs_ref[...]).reshape(Y, X, 16, part.shape[-1])
    own_ref[...] = part[:, 0]
    for j in range(1, X):
        sent_refs[j - 1][...] = part[:, j].astype(BF)


def half_dot(core, pieces, weight, theirs=()):
    width, cols = weight.shape
    shape = jax.ShapeDtypeStruct((256, cols), F32)
    if core == 0:
        block = (Y, 16, cols)
        shape = [jax.ShapeDtypeStruct(block, F32)] + [jax.ShapeDtypeStruct(block, BF)] * (X - 1)
    vmem = pl.BlockSpec(memory_space=pltpu.VMEM)
    return pl.pallas_call(
        functools.partial(half_kernel, core),
        out_shape=shape,
        in_specs=[vmem] * (Y + 1 + len(theirs)),
        out_specs=jax.tree.map(lambda _: vmem, shape),
        compiler_params=pltpu.CompilerParams(vmem_limit_bytes=VMEM_BYTES),
        cost_estimate=pl.CostEstimate(
            flops=2 * 256 * width * cols, bytes_accessed=2 * width * cols, transcendentals=0
        ),
        name=f"half_{core}",
    )(*pieces, weight, *theirs)


def input_kernel(*refs):
    pieces, (gate_ref, up_ref), (rows_ref, own_ref), sent_refs = (
        refs[:Z],
        refs[Z : Z + 2],
        refs[Z + 2 : Z + 4],
        refs[Z + 4 :],
    )
    for k in range(Z):
        for array in range(2):
            for j in range(Y):
                rows_ref[array, pl.ds((j * Z + k) * 16, 16), :] = pieces[k][array, j]
    for start in range(0, own_ref.shape[1], 256):
        lanes = pl.ds(start, 256)
        term = cols_dot(rows_ref[0], gate_ref[lanes, :]) + cols_dot(rows_ref[1], up_ref[lanes, :])
        own_ref[:, lanes] = term[:128]
        for j in range(1, Y):
            sent_refs[j - 1][:, lanes] = term[128 * j : 128 * j + 128].astype(BF)


def input_terms(pieces, gate_weight, up_weight):
    width, cols = gate_weight.shape
    vmem = pl.BlockSpec(memory_space=pltpu.VMEM)
    return pl.pallas_call(
        input_kernel,
        out_shape=[
            jax.ShapeDtypeStruct((2, 512, cols), BF),
            jax.ShapeDtypeStruct((128, width), F32),
        ]
        + [jax.ShapeDtypeStruct((128, width), BF)] * (Y - 1),
        in_specs=[vmem] * (Z + 2),
        out_specs=[vmem] * (Y + 1),
        compiler_params=pltpu.CompilerParams(vmem_limit_bytes=VMEM_BYTES),
        cost_estimate=pl.CostEstimate(
            flops=4 * 512 * width * cols, bytes_accessed=4 * width * cols, transcendentals=0
        ),
        name="input_terms",
    )(*pieces, gate_weight, up_weight)


def shards(inputs, grad_out, gate_pre, up_pre, gate_weight, up_weight, down_weight):
    width, cols = gate_weight.shape
    tensor = lax.axis_index("tensor")
    prefixes = jnp.array([FF // 2 ** (G - 1 - g) for g in range(G)], jnp.int32)
    live = jnp.repeat(tensor * cols < prefixes, 4)[None, :, None]

    both = jnp.stack([grad_out, inputs]).reshape(2, 16, width)
    both = exchange_z(jnp.broadcast_to(both, (Z, 2, 16, width)))
    gate = own_tokens(gate_pre, tensor % Y).astype(F32)
    up = own_tokens(up_pre, tensor % Y).astype(F32)
    sig = jax.nn.sigmoid(gate)
    gate_factor = jnp.where(live, up * sig * (1.0 + gate * (1.0 - sig)), 0.0)
    up_factor = jnp.where(live, gate * sig, 0.0)
    hidden = (up_factor * up).astype(BF)
    hidden = [hidden] + [from_x(hidden, j) for j in range(1, X)]
    both, hidden = lax.optimization_barrier((both, hidden))
    grad_z, in_z = both[:, 0], both[:, 1]
    grad_y = [grad_z] + [from_y(grad_z, j) for j in range(1, Y)]

    theirs = swap_core(half_dot(1, grad_y, down_weight))
    dhid, *blocks = half_dot(0, grad_y, down_weight, (theirs,))
    for j in range(1, X):
        dhid = dhid + from_x(blocks[j - 1], -j).astype(F32)

    d_own = jnp.stack([dhid * gate_factor, dhid * up_factor]).astype(BF)
    d_x = [d_own] + [from_x(d_own, j) for j in range(1, X)]
    d_other = [swap_core(d) for d in d_x]
    d_other[0], in_z = lax.optimization_barrier((d_other[0], in_z))
    in_y = [in_z] + [from_y(in_z, j) for j in range(1, Y)]
    hidden = jnp.stack(hidden)
    hidden = [hidden, swap_core(hidden)]

    rows, own, *sent = input_terms(d_x + d_other, gate_weight, up_weight)
    sent, grad_y, hidden = lax.optimization_barrier((sent, grad_y, hidden))
    got = [from_y(sent[j - 1], -j) for j in range(1, Y)]
    in_rows = jnp.stack(in_y).reshape(512, width)
    grad_rows = jnp.stack(grad_y).reshape(512, width)
    hidden = jnp.stack(hidden).reshape(Z, Y, 16, cols).transpose(1, 0, 2, 3).reshape(512, cols)
    total = own
    for g in got:
        total = total + g.astype(F32)
    total, rows, in_rows, grad_rows, hidden = lax.optimization_barrier(
        (total.astype(BF), rows, in_rows, grad_rows, hidden)
    )
    total = exchange_z(total.reshape(Z, 16, width))
    gate_grad = rows_dot(in_rows, rows[0]).astype(BF)
    up_grad = rows_dot(in_rows, rows[1]).astype(BF)
    down_grad = rows_dot(grad_rows, hidden).astype(BF)
    in_grads = total.astype(F32).sum(0).astype(BF).reshape(G, 4, width)
    return in_grads, gate_grad, up_grad, down_grad


def solution(mesh):
    tokens = P(None, "tensor", "dp")
    hidden = P(None, "dp", "tensor")
    weight = P("dp", "tensor")
    return jax.shard_map(
        shards,
        mesh=mesh,
        in_specs=(tokens, tokens, hidden, hidden, weight, weight, weight),
        out_specs=(tokens, weight, weight, weight),
        check_vma=False,
    )
```

time: 635 us -> 116 us (0.18); the launches traced: 622 us -> 116 us
  blocking collectives: 326 us -> 0 us
  waiting for transfers between devices: 195 us -> 46.8 us
  starting transfers between devices: 0.25 us -> 48.1 us
  local copies, waits for them, and re-layouts: 37.2 us -> 4.53 us
  matrix products: 27.6 us -> 8.89 us
  other arithmetic: 20.5 us -> 2.71 us
  between operations: 15.2 us -> 0.84 us
    all_gather x12 -> x0, blocking collectives: 166 us -> none  [the longest x4 55.7 us: shards(): hidden = lax.all_gather(share_hidden, 'dp', axis=0, tiled=True)]
    unnamed x1 -> x0, blocking collectives: 160 us -> none
    reduce_scatter x4 -> x0, waiting for transfers between devices: 116 us -> none  [shards(): lax.psum_scatter(partial_sum, 'dp', scatter_dimension=0, tiled=True)]
    all_gather x2 -> x0, waiting for transfers between devices: 79.6 us -> none  [the longest x1 79.6 us: shards(): lax.all_gather(grad_out, 'tensor', axis=1, tiled=True)]
    ppermute x0 -> x24, waiting for transfers between devices: none -> 41.3 us  [the longest x9 24.1 us: from_y(): lax.ppermute(block, 'tensor', [(t // Y * Y + (t % Y + step) % Y, t) for t...]
    ppermute x0 -> x24, starting transfers between devices: none -> 33.2 us  [the longest x9 19 us: from_x(): lax.ppermute(block, 'dp', [((d // C + step) % X * C + d % C, d) for d in...]
    unnamed x63 -> x16, local copies, waits for them, and re-layouts: 22.7 us -> 0.04 us
    convert_element_type x5 -> x2, other arithmetic: 19.7 us -> 1.01 us  [the longest x1 0.84 us: shards(): total.astype(BF)]
  transfers between devices with their start and end apart: 6 -> 26, of which waited for: 5 -> 19; matrix products, arithmetic and copies ran while one was open for 4% -> 10% of each run, Pallas kernels for 0% -> 2%
where the time goes in v1:
time: 116 us
  starting transfers between devices  48.1 us (41%)
  waiting for transfers between devices  46.8 us (40%)
  matrix products  8.89 us (8%)
  local copies, waits for them, and re-layouts  4.53 us (4%)
  Pallas kernels  3.79 us (3%)
  other arithmetic  2.71 us (2%)
    ppermute x9, waiting for transfers between devices, from_y(): lax.ppermute(block, 'tensor', [(t // Y * Y + (t % Y + step) % Y, t) for t...  24.1 us
    ppermute x9, starting transfers between devices, from_x(): lax.ppermute(block, 'dp', [((d // C + step) % X * C + d % C, d) for d in...  19 us
    all_to_all x2, starting transfers between devices, exchange_z(): lax.all_to_all(blocks, ('dp', 'tensor'), 0, 0, axis_index_groups=Z_GROUPS)  14.9 us
    ppermute x9, waiting for transfers between devices, from_x(): lax.ppermute(block, 'dp', [((d // C + step) % X * C + d % C, d) for d in...  14.7 us
    ppermute x9, starting transfers between devices, from_y(): lax.ppermute(block, 'tensor', [(t // Y * Y + (t % Y + step) % Y, t) for t...  13.2 us
    dot_general x3, matrix products, rows_dot(): lax.dot_general(left, right, (((0,), (0,)), ((), ())), preferred_element_...  8.89 us
    all_to_all x2, waiting for transfers between devices, exchange_z(): lax.all_to_all(blocks, ('dp', 'tensor'), 0, 0, axis_index_groups=Z_GROUPS)  5.46 us
    ppermute x6, waiting for transfers between devices, swap_core(): return lax.ppermute(block, 'dp', CORE_SWAP)  2.47 us
  transfers between devices with their start and end apart: 26, of which 19 were waited for; matrix products, arithmetic and copies ran while one was open for 10% of the time, Pallas kernels for 2%

profile of v1, /device:TPU:40, one launch (start us, length us, event | category | flops | bytes accessed | tf_op | source)
XLA Modules:
  0.0 115.6 jit_solution(6255839627327412328)
XLA Ops:
  3.1 8.7 %all-to-all-start = ((bf16[8,2,16,1024]{3,2,1,0:T(8,128)(2,1)}), bf16[8,2,16,1024]{3,2,1,0:T(8,128)(2,1)S(1)}, u32[]{:S(2)}, u32[]{:S(2)}) async-start(bf16[8,2,16,1024]{3,2,1,0:T(8,128)(2,1)} %broadcast_in_dim.24), calls=%async_computation | async-start | bytes 1048576 | tf_op jit(solution)/shard_map/all_to_all | solution.py:38
  12.4 1.6 %collective-permute-start.2 = (bf16[4,16,896]{2,1,0:T(8,128)(2,1)S(1)}, bf16[4,16,896]{2,1,0:T(8,128)(2,1)S(1)}, u32[]{:S(2)}, u32[]{:S(2)}) collective-permute-start(bf16[4,16,896]{2,1,0:T(8,128)(2,1)S(1)} %get-tuple-element.44), channel_id=1, source_target_pairs={{192,0},{224,32},{0,64},{32,96},{64,128},{96,160},{128,192},{160,2... | collective-permute-start | bytes 344072 | tf_op jit(solution)/shard_map/ppermute | solution.py:26
  14.0 3.4 %collective-permute-start.1 = (bf16[4,16,896]{2,1,0:T(8,128)(2,1)S(1)}, bf16[4,16,896]{2,1,0:T(8,128)(2,1)S(1)}, u32[]{:S(2)}, u32[]{:S(2)}) collective-permute-start(bf16[4,16,896]{2,1,0:T(8,128)(2,1)S(1)} %get-tuple-element.44), channel_id=1, source_target_pairs={{128,0},{160,32},{192,64},{224,96},{0,128},{32,160},{64,192},{96,2... | collective-permute-start | bytes 344072 | tf_op jit(solution)/shard_map/ppermute | solution.py:26
  17.4 1.4 %collective-permute-start = (bf16[4,16,896]{2,1,0:T(8,128)(2,1)S(1)}, bf16[4,16,896]{2,1,0:T(8,128)(2,1)S(1)}, u32[]{:S(2)}, u32[]{:S(2)}) collective-permute-start(bf16[4,16,896]{2,1,0:T(8,128)(2,1)S(1)} %get-tuple-element.44), channel_id=1, source_target_pairs={{64,0},{96,32},{128,64},{160,96},{192,128},{224,160},{0,192},{32,2... | collective-permute-start | bytes 344072 | tf_op jit(solution)/shard_map/ppermute | solution.py:26
  19.9 2.1 %collective-permute-done.1 = bf16[4,16,896]{2,1,0:T(8,128)(2,1)S(1)} collective-permute-done((bf16[4,16,896]{2,1,0:T(8,128)(2,1)S(1)}, bf16[4,16,896]{2,1,0:T(8,128)(2,1)S(1)}, u32[]{:S(2)}, u32[]{:S(2)}) %collective-permute-start.1) | collective-permute-done | bytes 114720 | tf_op jit(solution)/shard_map/ppermute | solution.py:26
  22.2 4.3 %all-to-all-done = bf16[8,2,16,1024]{3,2,1,0:T(8,128)(2,1)S(1)} async-done(((bf16[8,2,16,1024]{3,2,1,0:T(8,128)(2,1)}), bf16[8,2,16,1024]{3,2,1,0:T(8,128)(2,1)S(1)}, u32[]{:S(2)}, u32[]{:S(2)}) %all-to-all-start) | async-done | bytes 524320 | tf_op jit(solution)/shard_map/all_to_all | solution.py:38
  26.5 1.7 %collective-permute-start.5 = (bf16[8,16,1024]{2,1,0:T(8,128)(2,1)S(1)}, bf16[8,16,1024]{2,1,0:T(8,128)(2,1)S(1)}, u32[]{:S(2)}, u32[]{:S(2)}) collective-permute-start(bf16[8,16,1024]{2,1,0:T(8,128)(2,1)S(1)} %slice_bitcast_fusion.refs_0_), channel_id=1, source_target_pairs={{3,0},{0,1},{1,2},{2,3},{7,4},{4,5},{5,6},{6,7},{11,8},{8,9},{9,10... | collective-permute-start | bytes 786440 | tf_op jit(solution)/shard_map/ppermute | solution.py:30
  29.1 2.4 %collective-permute-start.3 = (bf16[8,16,1024]{2,1,0:T(8,128)(2,1)S(1)}, bf16[8,16,1024]{2,1,0:T(8,128)(2,1)S(1)}, u32[]{:S(2)}, u32[]{:S(2)}) collective-permute-start(bf16[8,16,1024]{2,1,0:T(8,128)(2,1)S(1)} %slice_bitcast_fusion.refs_0_), channel_id=1, source_target_pairs={{1,0},{2,1},{3,2},{0,3},{5,4},{6,5},{7,6},{4,7},{9,8},{10,9},{11,1... | collective-permute-start | bytes 786440 | tf_op jit(solution)/shard_map/ppermute | solution.py:30
  31.5 4.3 %collective-permute-done.5.refs_3_ = bf16[8,16,1024]{2,1,0:T(8,128)(2,1)S(1)} collective-permute-done((bf16[8,16,1024]{2,1,0:T(8,128)(2,1)S(1)}, bf16[8,16,1024]{2,1,0:T(8,128)(2,1)S(1)}, u32[]{:S(2)}, u32[]{:S(2)}) %collective-permute-start.5) | collective-permute-done | bytes 262176 | tf_op jit(solution)/shard_map/ppermute | solution.py:30
  35.8 3.1 %collective-permute-done.4.refs_2_ = bf16[8,16,1024]{2,1,0:T(8,128)(2,1)S(1)} collective-permute-done((bf16[8,16,1024]{2,1,0:T(8,128)(2,1)S(1)}, bf16[8,16,1024]{2,1,0:T(8,128)(2,1)S(1)}, u32[]{:S(2)}, u32[]{:S(2)}) %collective-permute-start.4) | collective-permute-done | bytes 262176 | tf_op jit(solution)/shard_map/ppermute | solution.py:30
  38.9 2.1 %collective-permute-done.3.refs_1_ = bf16[8,16,1024]{2,1,0:T(8,128)(2,1)S(1)} collective-permute-done((bf16[8,16,1024]{2,1,0:T(8,128)(2,1)S(1)}, bf16[8,16,1024]{2,1,0:T(8,128)(2,1)S(1)}, u32[]{:S(2)}, u32[]{:S(2)}) %collective-permute-start.3) | collective-permute-done | bytes 262176 | tf_op jit(solution)/shard_map/ppermute | solution.py:30
  41.9 2.5 %collective-permute-done.6.refs_5_ = f32[256,896]{1,0:T(8,128)S(1)} collective-permute-done((f32[256,896]{1,0:T(8,128)S(1)}, f32[256,896]{1,0:T(8,128)S(1)}, u32[]{:S(2)}, u32[]{:S(2)}) %collective-permute-start.6) | collective-permute-done | bytes 917536 | tf_op jit(solution)/shard_map/ppermute | solution.py:34
  45.1 4.0 %collective-permute-start.7 = (bf16[4,16,896]{2,1,0:T(8,128)(2,1)S(1)}, bf16[4,16,896]{2,1,0:T(8,128)(2,1)S(1)}, u32[]{:S(2)}, u32[]{:S(2)}) collective-permute-start(bf16[4,16,896]{2,1,0:T(8,128)(2,1)S(1)} %get-tuple-element.36), channel_id=1, source_target_pairs={{192,0},{224,32},{0,64},{32,96},{64,128},{96,160},{128,192},{160,2... | collective-permute-start | bytes 344072 | tf_op jit(solution)/shard_map/ppermute | solution.py:26
  50.3 1.6 %collective-permute-start.9 = (bf16[4,16,896]{2,1,0:T(8,128)(2,1)S(1)}, bf16[4,16,896]{2,1,0:T(8,128)(2,1)S(1)}, u32[]{:S(2)}, u32[]{:S(2)}) collective-permute-start(bf16[4,16,896]{2,1,0:T(8,128)(2,1)S(1)} %get-tuple-element.38), channel_id=1, source_target_pairs={{64,0},{96,32},{128,64},{160,96},{192,128},{224,160},{0,192},{32,2... | collective-permute-start | bytes 344072 | tf_op jit(solution)/shard_map/ppermute | solution.py:26
  52.6 3.3 %collective-permute-done.8 = bf16[4,16,896]{2,1,0:T(8,128)(2,1)S(1)} collective-permute-done((bf16[4,16,896]{2,1,0:T(8,128)(2,1)S(1)}, bf16[4,16,896]{2,1,0:T(8,128)(2,1)S(1)}, u32[]{:S(2)}, u32[]{:S(2)}) %collective-permute-start.8) | collective-permute-done | bytes 114720 | tf_op jit(solution)/shard_map/ppermute | solution.py:26
  56.2 2.1 %collective-permute-start.12 = (bf16[2,4,16,896]{3,2,1,0:T(8,128)(2,1)S(1)}, bf16[2,4,16,896]{3,2,1,0:T(8,128)(2,1)S(1)}, u32[]{:S(2)}, u32[]{:S(2)}) collective-permute-start(bf16[2,4,16,896]{3,2,1,0:T(8,128)(2,1)S(1)} %pad_maximum_fusion.4.refs_0_), channel_id=1, source_target_pairs={{192,0},{224,32},{0,64},{32,96},{64,128},{96,160},{128,192},{160,2... | collective-permute-start | bytes 688136 | tf_op jit(solution)/shard_map/ppermute | solution.py:26
  58.2 1.8 %collective-permute-start.11 = (bf16[2,4,16,896]{3,2,1,0:T(8,128)(2,1)S(1)}, bf16[2,4,16,896]{3,2,1,0:T(8,128)(2,1)S(1)}, u32[]{:S(2)}, u32[]{:S(2)}) collective-permute-start(bf16[2,4,16,896]{3,2,1,0:T(8,128)(2,1)S(1)} %pad_maximum_fusion.4.refs_0_), channel_id=1, source_target_pairs={{128,0},{160,32},{192,64},{224,96},{0,128},{32,160},{64,192},{96,2... | collective-permute-start | bytes 688136 | tf_op jit(solution)/shard_map/ppermute | solution.py:26
  60.0 1.9 %collective-permute-start.10 = (bf16[2,4,16,896]{3,2,1,0:T(8,128)(2,1)S(1)}, bf16[2,4,16,896]{3,2,1,0:T(8,128)(2,1)S(1)}, u32[]{:S(2)}, u32[]{:S(2)}) collective-permute-start(bf16[2,4,16,896]{3,2,1,0:T(8,128)(2,1)S(1)} %pad_maximum_fusion.4.refs_0_), channel_id=1, source_target_pairs={{64,0},{96,32},{128,64},{160,96},{192,128},{224,160},{0,192},{32,2... | collective-permute-start | bytes 688136 | tf_op jit(solution)/shard_map/ppermute | solution.py:26
  62.6 3.1 %collective-permute-done.12.refs_3_ = bf16[2,4,16,896]{3,2,1,0:T(8,128)(2,1)S(1)} collective-permute-done((bf16[2,4,16,896]{3,2,1,0:T(8,128)(2,1)S(1)}, bf16[2,4,16,896]{3,2,1,0:T(8,128)(2,1)S(1)}, u32[]{:S(2)}, u32[]{:S(2)}) %collective-permute-start.12) | collective-permute-done | bytes 229408 | tf_op jit(solution)/shard_map/ppermute | solution.py:26
  65.7 4.0 %collective-permute-done.11.refs_2_ = bf16[2,4,16,896]{3,2,1,0:T(8,128)(2,1)S(1)} collective-permute-done((bf16[2,4,16,896]{3,2,1,0:T(8,128)(2,1)S(1)}, bf16[2,4,16,896]{3,2,1,0:T(8,128)(2,1)S(1)}, u32[]{:S(2)}, u32[]{:S(2)}) %collective-permute-start.11) | collective-permute-done | bytes 229408 | tf_op jit(solution)/shard_map/ppermute | solution.py:26
  71.6 1.6 %collective-permute-start.22 = (bf16[8,16,1024]{2,1,0:T(8,128)(2,1)S(1)}, bf16[8,16,1024]{2,1,0:T(8,128)(2,1)S(1)}, u32[]{:S(2)}, u32[]{:S(2)}) collective-permute-start(bf16[8,16,1024]{2,1,0:T(8,128)(2,1)S(1)} %slice_bitcast_fusion.1), channel_id=1, source_target_pairs={{2,0},{3,1},{0,2},{1,3},{6,4},{7,5},{4,6},{5,7},{10,8},{11,9},{8,1... | collective-permute-start | bytes 786440 | tf_op jit(solution)/shard_map/ppermute | solution.py:30
  73.2 1.6 %collective-permute-start.21 = (bf16[8,16,1024]{2,1,0:T(8,128)(2,1)S(1)}, bf16[8,16,1024]{2,1,0:T(8,128)(2,1)S(1)}, u32[]{:S(2)}, u32[]{:S(2)}) collective-permute-start(bf16[8,16,1024]{2,1,0:T(8,128)(2,1)S(1)} %slice_bitcast_fusion.1), channel_id=1, source_target_pairs={{1,0},{2,1},{3,2},{0,3},{5,4},{6,5},{7,6},{4,7},{9,8},{10,9},{11,1... | collective-permute-start | bytes 786440 | tf_op jit(solution)/shard_map/ppermute | solution.py:30
  74.8 2.4 %input_terms.1 = (bf16[2,512,896]{2,1,0:T(8,128)(2,1)S(1)}, f32[128,1024]{1,0:T(8,128)S(1)}, bf16[128,1024]{1,0:T(8,128)(2,1)S(1)}, bf16[128,1024]{1,0:T(8,128)(2,1)S(1)}, bf16[128,1024]{1,0:T(8,128)(2,1)S(1)}) custom-call(bf16[2,4,16,896]{3,2,1,0:T(8,128)(2,1)S(1)} %pad_maximum_fusion.4.refs_0_, ...), custom_call_target="tpu_custom_call" | custom-call | flops 1879048192 | bytes 3670016 | tf_op jit(solution)/shard_map/input_terms/pallas_call | solution.py:111
  77.7 3.2 %collective-permute-start.19 = (bf16[128,1024]{1,0:T(8,128)(2,1)S(1)}, bf16[128,1024]{1,0:T(8,128)(2,1)S(1)}, u32[]{:S(2)}, u32[]{:S(2)}) collective-permute-start(bf16[128,1024]{1,0:T(8,128)(2,1)S(1)} %get-tuple-element.49), channel_id=1, source_target_pairs={{2,0},{3,1},{0,2},{1,3},{6,4},{7,5},{4,6},{5,7},{10,8},{11,9},{8,1... | collective-permute-start | bytes 786440 | tf_op jit(solution)/shard_map/ppermute | solution.py:30
  82.3 5.7 %collective-permute-done.21 = bf16[8,16,1024]{2,1,0:T(8,128)(2,1)S(1)} collective-permute-done((bf16[8,16,1024]{2,1,0:T(8,128)(2,1)S(1)}, bf16[8,16,1024]{2,1,0:T(8,128)(2,1)S(1)}, u32[]{:S(2)}, u32[]{:S(2)}) %collective-permute-start.21) | collective-permute-done | bytes 262176 | tf_op jit(solution)/shard_map/ppermute | solution.py:30
  89.1 1.7 %collective-permute-done.18 = bf16[128,1024]{1,0:T(8,128)(2,1)S(1)} collective-permute-done((bf16[128,1024]{1,0:T(8,128)(2,1)S(1)}, bf16[128,1024]{1,0:T(8,128)(2,1)S(1)}, u32[]{:S(2)}, u32[]{:S(2)}) %collective-permute-start.18) | collective-permute-done | bytes 262176 | tf_op jit(solution)/shard_map/ppermute | solution.py:30
  90.8 2.8 %collective-permute-done.19 = bf16[128,1024]{1,0:T(8,128)(2,1)S(1)} collective-permute-done((bf16[128,1024]{1,0:T(8,128)(2,1)S(1)}, bf16[128,1024]{1,0:T(8,128)(2,1)S(1)}, u32[]{:S(2)}, u32[]{:S(2)}) %collective-permute-start.19) | collective-permute-done | bytes 262176 | tf_op jit(solution)/shard_map/ppermute | solution.py:30
  93.6 4.2 %collective-permute-done.20 = bf16[128,1024]{1,0:T(8,128)(2,1)S(1)} collective-permute-done((bf16[128,1024]{1,0:T(8,128)(2,1)S(1)}, bf16[128,1024]{1,0:T(8,128)(2,1)S(1)}, u32[]{:S(2)}, u32[]{:S(2)}) %collective-permute-start.20) | collective-permute-done | bytes 262176 | tf_op jit(solution)/shard_map/ppermute | solution.py:30
  98.7 6.2 %all-to-all-start.1 = ((bf16[8,16,1024]{2,1,0:T(8,128)(2,1)}), bf16[8,16,1024]{2,1,0:T(8,128)(2,1)S(1)}, u32[]{:S(2)}, u32[]{:S(2)}) async-start(bf16[8,16,1024]{2,1,0:T(8,128)(2,1)} %bitcast.54), calls=%async_computation.1 | async-start | bytes 524288 | tf_op jit(solution)/shard_map/all_to_all | solution.py:38
  104.9 3.8 %convolution_convert_fusion.1 = bf16[1024,896]{1,0:T(8,128)(2,1)} fusion(bf16[512,1024]{1,0:T(8,128)(2,1)} %bitcast.52, bf16[2,512,896]{2,1,0:T(8,128)(2,1)S(1)} %get-tuple-element.61), kind=kOutput, calls=%fused_computation.1 | convolution fusion | flops 940441600 | bytes 3801088 | tf_op jit(solution)/shard_map/dot_general | solution.py:42
  108.7 2.5 %convolution_convert_fusion.2 = bf16[1024,896]{1,0:T(8,128)(2,1)} fusion(bf16[512,1024]{1,0:T(8,128)(2,1)S(1)} %bitcast.53, bf16[2,512,896]{2,1,0:T(8,128)(2,1)S(1)} %get-tuple-element.61), kind=kOutput, calls=%fused_computation.2 | convolution fusion | flops 940441600 | bytes 3801088 | tf_op jit(solution)/shard_map/dot_general | solution.py:42
  111.2 2.5 %convolution_convert_fusion = bf16[1024,896]{1,0:T(8,128)(2,1)} fusion(bf16[512,1024]{1,0:T(8,128)(2,1)S(1)} %bitcast.51, bf16[512,896]{1,0:T(8,128)(2,1)S(1)} %bitcast.56), kind=kOutput, calls=%fused_computation | convolution fusion | flops 940441600 | bytes 3801088 | tf_op jit(solution)/shard_map/dot_general | solution.py:42
  (68 shorter events, 17.3 us)
Async XLA Ops:
  0.6 11.2 %copy-start.7 = (s32[4]{0:T(128)S(1)}, s32[4]{0:T(128)}, u32[]{:S(2)}) copy-start(s32[4]{0:T(128)} %constant.32.clone) | copy-start | bytes 52
  0.6 11.4 %copy-start.5 = (bf16[4,16,896]{2,1,0:T(8,128)(2,1)S(1)}, bf16[4,16,896]{2,1,0:T(8,128)(2,1)}, u32[]{:S(2)}) copy-start(bf16[4,16,896]{2,1,0:T(8,128)(2,1)} %param.10) | copy-start | bytes 344068
  0.7 11.5 %copy-start.6 = (bf16[4,16,896]{2,1,0:T(8,128)(2,1)S(1)}, bf16[4,16,896]{2,1,0:T(8,128)(2,1)}, u32[]{:S(2)}) copy-start(bf16[4,16,896]{2,1,0:T(8,128)(2,1)} %param.11) | copy-start | bytes 344068
  3.1 37.9 %copy-start = (bf16[1024,896]{1,0:T(8,128)(2,1)S(1)}, bf16[1024,896]{1,0:T(8,128)(2,1)}, u32[]{:S(2)}) copy-start(bf16[1024,896]{1,0:T(8,128)(2,1)} %refs_4_.3) | copy-start | bytes 5505028
  3.1 23.4 %all-to-all-start = ((bf16[8,2,16,1024]{3,2,1,0:T(8,128)(2,1)}), bf16[8,2,16,1024]{3,2,1,0:T(8,128)(2,1)S(1)}, u32[]{:S(2)}, u32[]{:S(2)}) async-start(bf16[8,2,16,1024]{3,2,1,0:T(8,128)(2,1)} %broadcast_in_dim.24), calls=%async_computation | async-start | bytes 1048576 | tf_op jit(solution)/shard_map/all_to_all | solution.py:38
  12.4 7.5 %collective-permute-start.2 = (bf16[4,16,896]{2,1,0:T(8,128)(2,1)S(1)}, bf16[4,16,896]{2,1,0:T(8,128)(2,1)S(1)}, u32[]{:S(2)}, u32[]{:S(2)}) collective-permute-start(bf16[4,16,896]{2,1,0:T(8,128)(2,1)S(1)} %get-tuple-element.44), channel_id=1, source_target_pairs={{192,0},{224,32},{0,64},{32,96},{64,128},{96,160},{128,192},{160,2... | collective-permute-start | bytes 344072 | tf_op jit(solution)/shard_map/ppermute | solution.py:26
  14.0 8.0 %collective-permute-start.1 = (bf16[4,16,896]{2,1,0:T(8,128)(2,1)S(1)}, bf16[4,16,896]{2,1,0:T(8,128)(2,1)S(1)}, u32[]{:S(2)}, u32[]{:S(2)}) collective-permute-start(bf16[4,16,896]{2,1,0:T(8,128)(2,1)S(1)} %get-tuple-element.44), channel_id=1, source_target_pairs={{128,0},{160,32},{192,64},{224,96},{0,128},{32,160},{64,192},{96,2... | collective-permute-start | bytes 344072 | tf_op jit(solution)/shard_map/ppermute | solution.py:26
  17.4 4.8 %collective-permute-start = (bf16[4,16,896]{2,1,0:T(8,128)(2,1)S(1)}, bf16[4,16,896]{2,1,0:T(8,128)(2,1)S(1)}, u32[]{:S(2)}, u32[]{:S(2)}) collective-permute-start(bf16[4,16,896]{2,1,0:T(8,128)(2,1)S(1)} %get-tuple-element.44), channel_id=1, source_target_pairs={{64,0},{96,32},{128,64},{160,96},{192,128},{224,160},{0,192},{32,2... | collective-permute-start | bytes 344072 | tf_op jit(solution)/shard_map/ppermute | solution.py:26
  26.5 9.3 %collective-permute-start.5 = (bf16[8,16,1024]{2,1,0:T(8,128)(2,1)S(1)}, bf16[8,16,1024]{2,1,0:T(8,128)(2,1)S(1)}, u32[]{:S(2)}, u32[]{:S(2)}) collective-permute-start(bf16[8,16,1024]{2,1,0:T(8,128)(2,1)S(1)} %slice_bitcast_fusion.refs_0_), channel_id=1, source_target_pairs={{3,0},{0,1},{1,2},{2,3},{7,4},{4,5},{5,6},{6,7},{11,8},{8,9},{9,10... | collective-permute-start | bytes 786440 | tf_op jit(solution)/shard_map/ppermute | solution.py:30
  28.2 10.8 %collective-permute-start.4 = (bf16[8,16,1024]{2,1,0:T(8,128)(2,1)S(1)}, bf16[8,16,1024]{2,1,0:T(8,128)(2,1)S(1)}, u32[]{:S(2)}, u32[]{:S(2)}) collective-permute-start(bf16[8,16,1024]{2,1,0:T(8,128)(2,1)S(1)} %slice_bitcast_fusion.refs_0_), channel_id=1, source_target_pairs={{2,0},{3,1},{0,2},{1,3},{6,4},{7,5},{4,6},{5,7},{10,8},{11,9},{8,1... | collective-permute-start | bytes 786440 | tf_op jit(solution)/shard_map/ppermute | solution.py:30
  29.1 11.9 %collective-permute-start.3 = (bf16[8,16,1024]{2,1,0:T(8,128)(2,1)S(1)}, bf16[8,16,1024]{2,1,0:T(8,128)(2,1)S(1)}, u32[]{:S(2)}, u32[]{:S(2)}) collective-permute-start(bf16[8,16,1024]{2,1,0:T(8,128)(2,1)S(1)} %slice_bitcast_fusion.refs_0_), channel_id=1, source_target_pairs={{1,0},{2,1},{3,2},{0,3},{5,4},{6,5},{7,6},{4,7},{9,8},{10,9},{11,1... | collective-permute-start | bytes 786440 | tf_op jit(solution)/shard_map/ppermute | solution.py:30
  41.8 2.6 %collective-permute-start.6 = (f32[256,896]{1,0:T(8,128)S(1)}, f32[256,896]{1,0:T(8,128)S(1)}, u32[]{:S(2)}, u32[]{:S(2)}) collective-permute-start(f32[256,896]{1,0:T(8,128)S(1)} %half_1.1), channel_id=1, source_target_pairs={{0,32},{32,0},{64,96},{96,64},{128,160},{160,128},{192,224},{224,1... | collective-permute-start | bytes 2752520 | tf_op jit(solution)/shard_map/ppermute | solution.py:34
  44.3 30.4 %copy-start.2 = (bf16[1024,896]{1,0:T(8,128)(2,1)S(1)}, bf16[1024,896]{1,0:T(8,128)(2,1)}, u32[]{:S(2)}) copy-start(bf16[1024,896]{1,0:T(8,128)(2,1)} %refs_9_.1) | copy-start | bytes 5505028
  45.0 29.7 %copy-start.1 = (bf16[1024,896]{1,0:T(8,128)(2,1)S(1)}, bf16[1024,896]{1,0:T(8,128)(2,1)}, u32[]{:S(2)}) copy-start(bf16[1024,896]{1,0:T(8,128)(2,1)} %refs_8_.1) | copy-start | bytes 5505028
  45.1 7.5 %collective-permute-start.7 = (bf16[4,16,896]{2,1,0:T(8,128)(2,1)S(1)}, bf16[4,16,896]{2,1,0:T(8,128)(2,1)S(1)}, u32[]{:S(2)}, u32[]{:S(2)}) collective-permute-start(bf16[4,16,896]{2,1,0:T(8,128)(2,1)S(1)} %get-tuple-element.36), channel_id=1, source_target_pairs={{192,0},{224,32},{0,64},{32,96},{64,128},{96,160},{128,192},{160,2... | collective-permute-start | bytes 344072 | tf_op jit(solution)/shard_map/ppermute | solution.py:26
  49.1 6.8 %collective-permute-start.8 = (bf16[4,16,896]{2,1,0:T(8,128)(2,1)S(1)}, bf16[4,16,896]{2,1,0:T(8,128)(2,1)S(1)}, u32[]{:S(2)}, u32[]{:S(2)}) collective-permute-start(bf16[4,16,896]{2,1,0:T(8,128)(2,1)S(1)} %get-tuple-element.37), channel_id=1, source_target_pairs={{128,0},{160,32},{192,64},{224,96},{0,128},{32,160},{64,192},{96,2... | collective-permute-start | bytes 344072 | tf_op jit(solution)/shard_map/ppermute | solution.py:26
  50.3 5.6 %collective-permute-start.9 = (bf16[4,16,896]{2,1,0:T(8,128)(2,1)S(1)}, bf16[4,16,896]{2,1,0:T(8,128)(2,1)S(1)}, u32[]{:S(2)}, u32[]{:S(2)}) collective-permute-start(bf16[4,16,896]{2,1,0:T(8,128)(2,1)S(1)} %get-tuple-element.38), channel_id=1, source_target_pairs={{64,0},{96,32},{128,64},{160,96},{192,128},{224,160},{0,192},{32,2... | collective-permute-start | bytes 344072 | tf_op jit(solution)/shard_map/ppermute | solution.py:26
  56.2 9.5 %collective-permute-start.12 = (bf16[2,4,16,896]{3,2,1,0:T(8,128)(2,1)S(1)}, bf16[2,4,16,896]{3,2,1,0:T(8,128)(2,1)S(1)}, u32[]{:S(2)}, u32[]{:S(2)}) collective-permute-start(bf16[2,4,16,896]{3,2,1,0:T(8,128)(2,1)S(1)} %pad_maximum_fusion.4.refs_0_), channel_id=1, source_target_pairs={{192,0},{224,32},{0,64},{32,96},{64,128},{96,160},{128,192},{160,2... | collective-permute-start | bytes 688136 | tf_op jit(solution)/shard_map/ppermute | solution.py:26
  58.2 11.5 %collective-permute-start.11 = (bf16[2,4,16,896]{3,2,1,0:T(8,128)(2,1)S(1)}, bf16[2,4,16,896]{3,2,1,0:T(8,128)(2,1)S(1)}, u32[]{:S(2)}, u32[]{:S(2)}) collective-permute-start(bf16[2,4,16,896]{3,2,1,0:T(8,128)(2,1)S(1)} %pad_maximum_fusion.4.refs_0_), channel_id=1, source_target_pairs={{128,0},{160,32},{192,64},{224,96},{0,128},{32,160},{64,192},{96,2... | collective-permute-start | bytes 688136 | tf_op jit(solution)/shard_map/ppermute | solution.py:26
  60.0 9.8 %collective-permute-start.10 = (bf16[2,4,16,896]{3,2,1,0:T(8,128)(2,1)S(1)}, bf16[2,4,16,896]{3,2,1,0:T(8,128)(2,1)S(1)}, u32[]{:S(2)}, u32[]{:S(2)}) collective-permute-start(bf16[2,4,16,896]{3,2,1,0:T(8,128)(2,1)S(1)} %pad_maximum_fusion.4.refs_0_), channel_id=1, source_target_pairs={{64,0},{96,32},{128,64},{160,96},{192,128},{224,160},{0,192},{32,2... | collective-permute-start | bytes 688136 | tf_op jit(solution)/shard_map/ppermute | solution.py:26
  62.0 15.2 %collective-permute-start.17 = (bf16[4,4,16,896]{3,2,1,0:T(8,128)(2,1)S(1)}, bf16[4,4,16,896]{3,2,1,0:T(8,128)(2,1)S(1)}, u32[]{:S(2)}, u32[]{:S(2)}) collective-permute-start(bf16[4,4,16,896]{3,2,1,0:T(8,128)(2,1)S(1)} %pad_maximum_fusion.3), channel_id=1, source_target_pairs={{0,32},{32,0},{64,96},{96,64},{128,160},{160,128},{192,224},{224,1... | collective-permute-start | bytes 1376264 | tf_op jit(solution)/shard_map/ppermute | solution.py:34
  62.1 8.2 %collective-permute-start.13 = (bf16[2,4,16,896]{3,2,1,0:T(8,128)(2,1)S(1)}, bf16[2,4,16,896]{3,2,1,0:T(8,128)(2,1)S(1)}, u32[]{:S(2)}, u32[]{:S(2)}) collective-permute-start(bf16[2,4,16,896]{3,2,1,0:T(8,128)(2,1)S(1)} %pad_maximum_fusion.4.refs_0_), channel_id=1, source_target_pairs={{0,32},{32,0},{64,96},{96,64},{128,160},{160,128},{192,224},{224,1... | collective-permute-start | bytes 688136 | tf_op jit(solution)/shard_map/ppermute | solution.py:34
  65.7 5.9 %collective-permute-start.16 = (bf16[2,4,16,896]{3,2,1,0:T(8,128)(2,1)S(1)}, bf16[2,4,16,896]{3,2,1,0:T(8,128)(2,1)S(1)}, u32[]{:S(2)}, u32[]{:S(2)}) collective-permute-start(bf16[2,4,16,896]{3,2,1,0:T(8,128)(2,1)S(1)} %collective-permute-done.12.refs_3_), channel_id=1, source_target_pairs={{0,32},{32,0},{64,96},{96,64},{128,160},{160,128},{192,224},{224,1... | collective-permute-start | bytes 688136 | tf_op jit(solution)/shard_map/ppermute | solution.py:34
  69.7 3.5 %collective-permute-start.15 = (bf16[2,4,16,896]{3,2,1,0:T(8,128)(2,1)S(1)}, bf16[2,4,16,896]{3,2,1,0:T(8,128)(2,1)S(1)}, u32[]{:S(2)}, u32[]{:S(2)}) collective-permute-start(bf16[2,4,16,896]{3,2,1,0:T(8,128)(2,1)S(1)} %collective-permute-done.11.refs_2_), channel_id=1, source_target_pairs={{0,32},{32,0},{64,96},{96,64},{128,160},{160,128},{192,224},{224,1... | collective-permute-start | bytes 688136 | tf_op jit(solution)/shard_map/ppermute | solution.py:34
  69.9 4.9 %collective-permute-start.14 = (bf16[2,4,16,896]{3,2,1,0:T(8,128)(2,1)S(1)}, bf16[2,4,16,896]{3,2,1,0:T(8,128)(2,1)S(1)}, u32[]{:S(2)}, u32[]{:S(2)}) collective-permute-start(bf16[2,4,16,896]{3,2,1,0:T(8,128)(2,1)S(1)} %collective-permute-done.10.refs_1_), channel_id=1, source_target_pairs={{0,32},{32,0},{64,96},{96,64},{128,160},{160,128},{192,224},{224,1... | collective-permute-start | bytes 688136 | tf_op jit(solution)/shard_map/ppermute | solution.py:34
  70.3 11.7 %collective-permute-start.23 = (bf16[8,16,1024]{2,1,0:T(8,128)(2,1)S(1)}, bf16[8,16,1024]{2,1,0:T(8,128)(2,1)S(1)}, u32[]{:S(2)}, u32[]{:S(2)}) collective-permute-start(bf16[8,16,1024]{2,1,0:T(8,128)(2,1)S(1)} %slice_bitcast_fusion.1), channel_id=1, source_target_pairs={{3,0},{0,1},{1,2},{2,3},{7,4},{4,5},{5,6},{6,7},{11,8},{8,9},{9,10... | collective-permute-start | bytes 786440 | tf_op jit(solution)/shard_map/ppermute | solution.py:30
  71.6 10.7 %collective-permute-start.22 = (bf16[8,16,1024]{2,1,0:T(8,128)(2,1)S(1)}, bf16[8,16,1024]{2,1,0:T(8,128)(2,1)S(1)}, u32[]{:S(2)}, u32[]{:S(2)}) collective-permute-start(bf16[8,16,1024]{2,1,0:T(8,128)(2,1)S(1)} %slice_bitcast_fusion.1), channel_id=1, source_target_pairs={{2,0},{3,1},{0,2},{1,3},{6,4},{7,5},{4,6},{5,7},{10,8},{11,9},{8,1... | collective-permute-start | bytes 786440 | tf_op jit(solution)/shard_map/ppermute | solution.py:30
  73.2 14.8 %collective-permute-start.21 = (bf16[8,16,1024]{2,1,0:T(8,128)(2,1)S(1)}, bf16[8,16,1024]{2,1,0:T(8,128)(2,1)S(1)}, u32[]{:S(2)}, u32[]{:S(2)}) collective-permute-start(bf16[8,16,1024]{2,1,0:T(8,128)(2,1)S(1)} %slice_bitcast_fusion.1), channel_id=1, source_target_pairs={{1,0},{2,1},{3,2},{0,3},{5,4},{6,5},{7,6},{4,7},{9,8},{10,9},{11,1... | collective-permute-start | bytes 786440 | tf_op jit(solution)/shard_map/ppermute | solution.py:30
  77.2 13.6 %collective-permute-start.18 = (bf16[128,1024]{1,0:T(8,128)(2,1)S(1)}, bf16[128,1024]{1,0:T(8,128)(2,1)S(1)}, u32[]{:S(2)}, u32[]{:S(2)}) collective-permute-start(bf16[128,1024]{1,0:T(8,128)(2,1)S(1)} %get-tuple-element.48), channel_id=1, source_target_pairs={{3,0},{0,1},{1,2},{2,3},{7,4},{4,5},{5,6},{6,7},{11,8},{8,9},{9,10... | collective-permute-start | bytes 786440 | tf_op jit(solution)/shard_map/ppermute | solution.py:30
  77.7 15.9 %collective-permute-start.19 = (bf16[128,1024]{1,0:T(8,128)(2,1)S(1)}, bf16[128,1024]{1,0:T(8,128)(2,1)S(1)}, u32[]{:S(2)}, u32[]{:S(2)}) collective-permute-start(bf16[128,1024]{1,0:T(8,128)(2,1)S(1)} %get-tuple-element.49), channel_id=1, source_target_pairs={{2,0},{3,1},{0,2},{1,3},{6,4},{7,5},{4,6},{5,7},{10,8},{11,9},{8,1... | collective-permute-start | bytes 786440 | tf_op jit(solution)/shard_map/ppermute | solution.py:30
  82.0 15.8 %collective-permute-start.20 = (bf16[128,1024]{1,0:T(8,128)(2,1)S(1)}, bf16[128,1024]{1,0:T(8,128)(2,1)S(1)}, u32[]{:S(2)}, u32[]{:S(2)}) collective-permute-start(bf16[128,1024]{1,0:T(8,128)(2,1)S(1)} %get-tuple-element.50), channel_id=1, source_target_pairs={{1,0},{2,1},{3,2},{0,3},{5,4},{6,5},{7,6},{4,7},{9,8},{10,9},{11,1... | collective-permute-start | bytes 786440 | tf_op jit(solution)/shard_map/ppermute | solution.py:30
  98.7 16.2 %all-to-all-start.1 = ((bf16[8,16,1024]{2,1,0:T(8,128)(2,1)}), bf16[8,16,1024]{2,1,0:T(8,128)(2,1)S(1)}, u32[]{:S(2)}, u32[]{:S(2)}) async-start(bf16[8,16,1024]{2,1,0:T(8,128)(2,1)} %bitcast.54), calls=%async_computation.1 | async-start | bytes 524288 | tf_op jit(solution)/shard_map/all_to_all | solution.py:38
  (2 other events, 6.4 us)

commit v2 on v1

v2 whole, which is shorter than its diff:
```python
import functools

import jax
import jax.numpy as jnp
from jax import lax
from jax.experimental import pallas as pl
from jax.experimental.pallas import tpu as pltpu
from jax.sharding import PartitionSpec as P

FF = 28672
G = 4
X, C, Y, Z = 4, 2, 4, 8
BF = jnp.bfloat16
F32 = jnp.float32
MIB = 1024 * 1024
BAND = 256
Z_GROUPS = [
    [(x * C + c) * Y * Z + ((x + dx) % X * C + (c ^ dc)) * Y + y for dc in range(C) for dx in range(X)]
    for x in range(X)
    for c in range(C)
    for y in range(Y)
]
CORE_SWAP = [(d, d ^ 1) for d in range(X * C)]


def from_x(block, step):
    return lax.ppermute(block, "dp", [((d // C + step) % X * C + d % C, d) for d in range(X * C)])


def from_y(block, step):
    return lax.ppermute(block, "tensor", [(t // Y * Y + (t % Y + step) % Y, t) for t in range(Y * Z)])


def swap_core(block):
    return lax.ppermute(block, "dp", CORE_SWAP)


def exchange_z(blocks):
    return lax.all_to_all(blocks, ("dp", "tensor"), 0, 0, axis_index_groups=Z_GROUPS)


def rows_dot(left, right):
    return lax.dot_general(left, right, (((0,), (0,)), ((), ())), preferred_element_type=F32)


def cols_dot(left, right):
    return lax.dot_general(left, right, (((1,), (1,)), ((), ())), preferred_element_type=F32)


def own_tokens(part, y):
    cols = part.shape[-1]
    part = part.reshape(G, Y, 4, cols).transpose(1, 0, 2, 3).reshape(Y, 16, cols)
    return lax.dynamic_slice_in_dim(jnp.concatenate([part, part]), y, Y, 0)


def half_kernel(core, *refs):
    pieces, weight_ref = refs[:Y], refs[Y]
    rows = [p[core * X : core * X + X].reshape(X * 16, p.shape[-1]) for p in pieces]
    part = jnp.dot(jnp.concatenate(rows), weight_ref[...], preferred_element_type=F32)
    if core == 1:
        refs[Y + 1][...] = part
        return
    theirs_ref, own_ref, sent_refs = refs[Y + 1], refs[Y + 2], refs[Y + 3 :]
    part = (part + theirs_ref[...]).reshape(Y, X, 16, part.shape[-1])
    own_ref[...] = part[:, 0]
    for j in range(1, X):
        sent_refs[j - 1][...] = part[:, j].astype(BF)


def half_dot(core, pieces, weight, theirs=()):
    width, cols = weight.shape
    shape = jax.ShapeDtypeStruct((256, cols), F32)
    if core == 0:
        block = (Y, 16, cols)
        shape = [jax.ShapeDtypeStruct(block, F32)] + [jax.ShapeDtypeStruct(block, BF)] * (X - 1)
    vmem = pl.BlockSpec(memory_space=pltpu.VMEM)
    return pl.pallas_call(
        functools.partial(half_kernel, core),
        out_shape=shape,
        in_specs=[vmem] * (Y + 1 + len(theirs)),
        out_specs=jax.tree.map(lambda _: vmem, shape),
        compiler_params=pltpu.CompilerParams(vmem_limit_bytes=8 * MIB),
        cost_estimate=pl.CostEstimate(
            flops=2 * 256 * width * cols, bytes_accessed=2 * width * cols, transcendentals=0
        ),
        name=f"half_{core}",
    )(*pieces, weight, *theirs)


def gate_kernel(mine_ref, other_ref, factor_ref, hidden_ref):
    cols = hidden_ref.shape[-1]
    start = lax.axis_index("tensor") * cols
    granule = lax.broadcasted_iota(jnp.int32, (16, cols), 0) // 4
    live = start < lax.shift_right_logical(FF, G - 1 - granule)

    def step(i, carry):
        x, j = i // Y, lax.rem(i, Y)
        for c, ref in enumerate((mine_ref, other_ref)):
            gate, up = ref[x, 0, j].astype(F32), ref[x, 1, j].astype(F32)
            sig = 1.0 / (1.0 + jnp.exp(-gate))
            active = jnp.where(live, gate * sig, 0.0)
            rows = pl.ds(pl.multiple_of((j * Z + c * X + x) * 16, 16), 16)
            factor_ref[0, rows, :] = jnp.where(live, up * sig * (1.0 + gate * (1.0 - sig)), 0.0)
            factor_ref[1, rows, :] = active
            hidden_ref[rows, :] = (active * up).astype(BF)
        return carry

    lax.fori_loop(0, X * Y, step, 0)


def gate_terms(mine, other):
    cols = mine.shape[-1]
    vmem = pl.BlockSpec(memory_space=pltpu.VMEM)
    return pl.pallas_call(
        gate_kernel,
        out_shape=[jax.ShapeDtypeStruct((2, 512, cols), F32), jax.ShapeDtypeStruct((512, cols), BF)],
        in_specs=[vmem] * 2,
        out_specs=[vmem] * 2,
        compiler_params=pltpu.CompilerParams(vmem_limit_bytes=4 * MIB),
        cost_estimate=pl.CostEstimate(
            flops=16 * 512 * cols, bytes_accessed=12 * 512 * cols, transcendentals=512 * cols
        ),
        name="gate_terms",
    )(mine, other)


def input_kernel(*refs):
    pieces, (factor_ref, gate_ref, up_ref), (rows_ref, own_ref), sent_refs = (
        refs[:Z],
        refs[Z : Z + 3],
        refs[Z + 3 : Z + 5],
        refs[Z + 5 :],
    )
    for k in range(Z):
        for j in range(Y):
            rows = pl.ds((j * Z + k) * 16, 16)
            dhid = pieces[k][j].astype(F32)
            for array in range(2):
                rows_ref[array, rows, :] = (dhid * factor_ref[array, rows, :]).astype(BF)
    for start in range(0, own_ref.shape[1], 256):
        lanes = pl.ds(start, 256)
        term = cols_dot(rows_ref[0], gate_ref[lanes, :]) + cols_dot(rows_ref[1], up_ref[lanes, :])
        own_ref[:, lanes] = term[:128]
        for j in range(1, Y):
            sent_refs[j - 1][:, lanes] = term[128 * j : 128 * j + 128].astype(BF)


def input_terms(pieces, factors, gate_weight, up_weight):
    width, cols = gate_weight.shape
    vmem = pl.BlockSpec(memory_space=pltpu.VMEM)
    return pl.pallas_call(
        input_kernel,
        out_shape=[
            jax.ShapeDtypeStruct((2, 512, cols), BF),
            jax.ShapeDtypeStruct((128, width), F32),
        ]
        + [jax.ShapeDtypeStruct((128, width), BF)] * (Y - 1),
        in_specs=[vmem] * (Z + 3),
        out_specs=[vmem] * (Y + 1),
        compiler_params=pltpu.CompilerParams(vmem_limit_bytes=10 * MIB),
        cost_estimate=pl.CostEstimate(
            flops=4 * 512 * width * cols, bytes_accessed=4 * width * cols, transcendentals=0
        ),
        name="input_terms",
    )(*pieces, factors, gate_weight, up_weight)


def weight_kernel(*refs):
    in_refs, grad_refs, (hidden_ref, rows_ref) = refs[:Y], refs[Y : 2 * Y], refs[2 * Y : 2 * Y + 2]
    outs, (blocks, sems) = refs[2 * Y + 2 : 2 * Y + 5], refs[2 * Y + 5 :]
    def copy(k, i):
        band = pl.ds(pl.multiple_of(i * BAND, BAND), BAND)
        return pltpu.make_async_copy(blocks.at[k, band], outs[k].at[band], sems.at[k, i])

    def step(i, carry):
        band = pl.ds(pl.multiple_of(i * BAND, BAND), BAND)
        ins, grads = (
            jnp.concatenate([r[:, :, band].reshape(Z * 16, BAND) for r in pieces])
            for pieces in (in_refs, grad_refs)
        )
        for k, (left, right) in enumerate(((ins, rows_ref[0]), (ins, rows_ref[1]), (grads, hidden_ref[...]))):
            blocks[k, band, :] = rows_dot(left, right).astype(BF)
            copy(k, i).start()
        return carry

    bands = in_refs[0].shape[-1] // BAND
    lax.fori_loop(0, bands, step, 0)
    for i in range(bands):
        for k in range(3):
            copy(k, i).wait()


def weight_grads(in_y, grad_y, hidden, rows):
    width, cols = in_y[0].shape[-1], rows.shape[-1]
    vmem = pl.BlockSpec(memory_space=pltpu.VMEM)
    return pl.pallas_call(
        weight_kernel,
        out_shape=[jax.ShapeDtypeStruct((width, cols), BF)] * 3,
        in_specs=[vmem] * (2 * Y + 2),
        out_specs=[pl.BlockSpec(memory_space=pl.ANY)] * 3,
        scratch_shapes=[
            pltpu.VMEM((3, width, cols), BF),
            pltpu.SemaphoreType.DMA((3, width // BAND)),
        ],
        compiler_params=pltpu.CompilerParams(vmem_limit_bytes=14 * MIB),
        cost_estimate=pl.CostEstimate(
            flops=6 * 512 * width * cols, bytes_accessed=6 * width * cols, transcendentals=0
        ),
        name="weight_grads",
    )(*in_y, *grad_y, hidden, rows)


def shards(inputs, grad_out, gate_pre, up_pre, gate_weight, up_weight, down_weight):
    width, cols = gate_weight.shape
    tensor = lax.axis_index("tensor")
    both = exchange_z(jnp.broadcast_to(jnp.stack([grad_out, inputs]), (Z, 2, G, 4, width)))
    both = both.reshape(Z, 2, 16, width)

    pre = jnp.stack([own_tokens(gate_pre, tensor % Y), own_tokens(up_pre, tensor % Y)])
    pre = [pre] + [from_x(pre, j) for j in range(1, X)]
    both, pre = lax.optimization_barrier((both, pre))
    grad_z, in_z = both[:, 0], both[:, 1]
    grad_y = [grad_z] + [from_y(grad_z, j) for j in range(1, Y)]

    pre = jnp.stack(pre)
    factors, hidden = gate_terms(pre, swap_core(pre))
    theirs, in_z = lax.optimization_barrier((half_dot(1, grad_y, down_weight), in_z))
    theirs = swap_core(theirs)
    dhid, *blocks = half_dot(0, grad_y, down_weight, (theirs,))
    blocks = [from_x(blocks[j - 1], -j) for j in range(1, X)]
    in_y = [in_z] + [from_y(in_z, j) for j in range(1, Y)]
    blocks, factors, hidden, in_y[1] = lax.optimization_barrier((blocks, factors, hidden, in_y[1]))
    for block in blocks:
        dhid = dhid + block.astype(F32)

    d_own = dhid.astype(BF)
    d_x = [d_own] + [from_x(d_own, j) for j in range(1, X)]
    d_other = [swap_core(d) for d in d_x]
    d_other, in_y = lax.optimization_barrier((d_other, in_y))

    rows, own, *sent = input_terms(d_x + d_other, factors, gate_weight, up_weight)
    sent, hidden = lax.optimization_barrier((sent, hidden))
    total = own
    for j in range(1, Y):
        total = total + from_y(sent[j - 1], -j).astype(F32)
    total, rows, grad_y, in_y, hidden = lax.optimization_barrier(
        (total.astype(BF), rows, grad_y, in_y, hidden)
    )
    total = exchange_z(total.reshape(Z, 16, width))
    gate_grad, up_grad, down_grad = weight_grads(in_y, grad_y, hidden, rows)
    in_grads = total.astype(F32).sum(0).astype(BF).reshape(G, 4, width)
    return in_grads, gate_grad, up_grad, down_grad


def solution(mesh):
    tokens = P(None, "tensor", "dp")
    hidden = P(None, "dp", "tensor")
    weight = P("dp", "tensor")
    return jax.shard_map(
        shards,
        mesh=mesh,
        in_specs=(tokens, tokens, hidden, hidden, weight, weight, weight),
        out_specs=(tokens, weight, weight, weight),
        check_vma=False,
    )
```

time: 116 us -> 106 us (0.914)
  waiting for transfers between devices: 46.8 us -> 36.6 us
  matrix products: 8.89 us -> 0 us
  Pallas kernels: 3.79 us -> 10.2 us
  local copies, waits for them, and re-layouts: 4.53 us -> 6.77 us
  starting transfers between devices: 48.1 us -> 46.2 us
  other arithmetic: 2.71 us -> 4.19 us
    ppermute x9, waiting for transfers between devices: 14.7 us -> 3.69 us  [from_x(): lax.ppermute(block, 'dp', [((d // C + step) % X * C + d % C, d) for d in...]
    dot_general x3 -> x0, matrix products: 8.89 us -> none  [rows_dot(): lax.dot_general(left, right, (((0,), (0,)), ((), ())), preferred_element_...]
    pallas_call x0 -> x2, Pallas kernels: none -> 6.37 us  [the longest x1 4.98 us: weight_grads(): pl.pallas_call(weight_kernel, out_shape=[jax.ShapeDtypeStruct((width, col...]
    unnamed x16 -> x22, local copies, waits for them, and re-layouts: 0.04 us -> 4.73 us
    all_to_all x2, waiting for transfers between devices: 5.46 us -> 10.1 us  [exchange_z(): lax.all_to_all(blocks, ('dp', 'tensor'), 0, 0, axis_index_groups=Z_GROUPS)]
    ppermute x9, waiting for transfers between devices: 24.1 us -> 21.6 us  [from_y(): lax.ppermute(block, 'tensor', [(t // Y * Y + (t % Y + step) % Y, t) for t...]
    ppermute x9, starting transfers between devices: 19 us -> 16.9 us  [from_x(): lax.ppermute(block, 'dp', [((d // C + step) % X * C + d % C, d) for d in...]
    ppermute x9, starting transfers between devices: 13.2 us -> 15 us  [from_y(): lax.ppermute(block, 'tensor', [(t // Y * Y + (t % Y + step) % Y, t) for t...]
  transfers between devices with their start and end apart: 26 -> 26, of which waited for: 19 -> 14; matrix products, arithmetic and copies ran while one was open for 10% -> 2% of each run, Pallas kernels for 2% -> 7%
where the time goes in v2:
time: 106 us; the launch traced here: 105 us
  starting transfers between devices  46.2 us (44%)
  waiting for transfers between devices  36.6 us (35%)
  Pallas kernels  10.2 us (10%)
  local copies, waits for them, and re-layouts  6.77 us (6%)
  other arithmetic  4.19 us (4%)
    ppermute x9, waiting for transfers between devices, from_y(): lax.ppermute(block, 'tensor', [(t // Y * Y + (t % Y + step) % Y, t) for t...  21.6 us
    ppermute x9, starting transfers between devices, from_x(): lax.ppermute(block, 'dp', [((d // C + step) % X * C + d % C, d) for d in...  16.9 us
    ppermute x9, starting transfers between devices, from_y(): lax.ppermute(block, 'tensor', [(t // Y * Y + (t % Y + step) % Y, t) for t...  15 us
    all_to_all x2, starting transfers between devices, exchange_z(): lax.all_to_all(blocks, ('dp', 'tensor'), 0, 0, axis_index_groups=Z_GROUPS)  13.2 us
    all_to_all x2, waiting for transfers between devices, exchange_z(): lax.all_to_all(blocks, ('dp', 'tensor'), 0, 0, axis_index_groups=Z_GROUPS)  10.1 us
    pallas_call x1, Pallas kernels, weight_grads(): pl.pallas_call(weight_kernel, out_shape=[jax.ShapeDtypeStruct((width, col...  4.98 us
    unnamed x22, local copies, waits for them, and re-layouts  4.73 us
    ppermute x9, waiting for transfers between devices, from_x(): lax.ppermute(block, 'dp', [((d // C + step) % X * C + d % C, d) for d in...  3.69 us
  transfers between devices with their start and end apart: 26, of which 14 were waited for; matrix products, arithmetic and copies ran while one was open for 2% of the time, Pallas kernels for 7%

profile of v2, /device:TPU:40, one launch (start us, length us, event | category | flops | bytes accessed | tf_op | source)
XLA Modules:
  0.0 104.8 jit_solution(14014694150849355257)
XLA Ops:
  1.5 1.0 broadcast_in_dim.3
  2.5 8.6 %all-to-all-start = ((bf16[8,2,4,4,1024]{4,3,2,1,0:T(4,128)(2,1)}), bf16[8,2,4,4,1024]{4,3,2,1,0:T(4,128)(2,1)S(1)}, u32[]{:S(2)}, u32[]{:S(2)}) async-start(bf16[8,2,4,4,1024]{4,3,2,1,0:T(4,128)(2,1)} %broadcast_in_dim.3), calls=%async_computation | async-start | bytes 1048576 | tf_op jit(solution)/shard_map/all_to_all | solution.py:39
  11.5 1.6 %collective-permute-start.2 = (bf16[2,4,16,896]{3,2,1,0:T(8,128)(2,1)S(1)}, bf16[2,4,16,896]{3,2,1,0:T(8,128)(2,1)}, u32[]{:S(2)}, u32[]{:S(2)}) collective-permute-start(bf16[2,4,16,896]{3,2,1,0:T(8,128)(2,1)S(1)} %pad_maximum_fusion.1), channel_id=1, source_target_pairs={{192,0},{224,32},{0,64},{32,96},{64,128},{96,160},{128,192},{160,2... | collective-permute-start | bytes 688136 | tf_op jit(solution)/shard_map/ppermute | solution.py:27
  13.1 3.4 %collective-permute-start.1 = (bf16[2,4,16,896]{3,2,1,0:T(8,128)(2,1)S(1)}, bf16[2,4,16,896]{3,2,1,0:T(8,128)(2,1)}, u32[]{:S(2)}, u32[]{:S(2)}) collective-permute-start(bf16[2,4,16,896]{3,2,1,0:T(8,128)(2,1)S(1)} %pad_maximum_fusion.1), channel_id=1, source_target_pairs={{128,0},{160,32},{192,64},{224,96},{0,128},{32,160},{64,192},{96,2... | collective-permute-start | bytes 688136 | tf_op jit(solution)/shard_map/ppermute | solution.py:27
  16.5 1.4 %collective-permute-start = (bf16[2,4,16,896]{3,2,1,0:T(8,128)(2,1)S(1)}, bf16[2,4,16,896]{3,2,1,0:T(8,128)(2,1)}, u32[]{:S(2)}, u32[]{:S(2)}) collective-permute-start(bf16[2,4,16,896]{3,2,1,0:T(8,128)(2,1)S(1)} %pad_maximum_fusion.1), channel_id=1, source_target_pairs={{64,0},{96,32},{128,64},{160,96},{192,128},{224,160},{0,192},{32,2... | collective-permute-start | bytes 688136 | tf_op jit(solution)/shard_map/ppermute | solution.py:27
  17.9 7.8 %all-to-all-done = bf16[8,2,4,4,1024]{4,3,2,1,0:T(4,128)(2,1)S(1)} async-done(((bf16[8,2,4,4,1024]{4,3,2,1,0:T(4,128)(2,1)}), bf16[8,2,4,4,1024]{4,3,2,1,0:T(4,128)(2,1)S(1)}, u32[]{:S(2)}, u32[]{:S(2)}) %all-to-all-start) | async-done | bytes 524320 | tf_op jit(solution)/shard_map/all_to_all | solution.py:39
  26.1 1.7 %collective-permute-start.5 = (bf16[8,16,1024]{2,1,0:T(8,128)(2,1)S(1)}, bf16[8,16,1024]{2,1,0:T(8,128)(2,1)S(1)}, u32[]{:S(2)}, u32[]{:S(2)}) collective-permute-start(bf16[8,16,1024]{2,1,0:T(8,128)(2,1)S(1)} %get-tuple-element.95.refs_0_.refs_4_), channel_id=1, source_target_pairs={{3,0},{0,1},{1,2},{2,3},{7,4},{4,5},{5,6},{6,7},{11,8},{8,9},{9,10... | collective-permute-start | bytes 786440 | tf_op jit(solution)/shard_map/ppermute | solution.py:31
  28.7 2.4 %collective-permute-start.3 = (bf16[8,16,1024]{2,1,0:T(8,128)(2,1)S(1)}, bf16[8,16,1024]{2,1,0:T(8,128)(2,1)S(1)}, u32[]{:S(2)}, u32[]{:S(2)}) collective-permute-start(bf16[8,16,1024]{2,1,0:T(8,128)(2,1)S(1)} %get-tuple-element.95.refs_0_.refs_4_), channel_id=1, source_target_pairs={{1,0},{2,1},{3,2},{0,3},{5,4},{6,5},{7,6},{4,7},{9,8},{10,9},{11,1... | collective-permute-start | bytes 786440 | tf_op jit(solution)/shard_map/ppermute | solution.py:31
  31.1 4.3 %collective-permute-done.5.refs_3_.refs_7_ = bf16[8,16,1024]{2,1,0:T(8,128)(2,1)S(1)} collective-permute-done((bf16[8,16,1024]{2,1,0:T(8,128)(2,1)S(1)}, bf16[8,16,1024]{2,1,0:T(8,128)(2,1)S(1)}, u32[]{:S(2)}, u32[]{:S(2)}) %collective-permute-start.5) | collective-permute-done | bytes 262176 | tf_op jit(solution)/shard_map/ppermute | solution.py:31
  35.5 3.0 %collective-permute-done.4.refs_2_.refs_6_ = bf16[8,16,1024]{2,1,0:T(8,128)(2,1)S(1)} collective-permute-done((bf16[8,16,1024]{2,1,0:T(8,128)(2,1)S(1)}, bf16[8,16,1024]{2,1,0:T(8,128)(2,1)S(1)}, u32[]{:S(2)}, u32[]{:S(2)}) %collective-permute-start.4) | collective-permute-done | bytes 262176 | tf_op jit(solution)/shard_map/ppermute | solution.py:31
  38.5 2.1 %collective-permute-done.3.refs_1_.refs_5_ = bf16[8,16,1024]{2,1,0:T(8,128)(2,1)S(1)} collective-permute-done((bf16[8,16,1024]{2,1,0:T(8,128)(2,1)S(1)}, bf16[8,16,1024]{2,1,0:T(8,128)(2,1)S(1)}, u32[]{:S(2)}, u32[]{:S(2)}) %collective-permute-start.3) | collective-permute-done | bytes 262176 | tf_op jit(solution)/shard_map/ppermute | solution.py:31
  41.4 1.3 %pad_maximum_fusion.mine_ref = bf16[4,2,4,16,896]{4,3,2,1,0:T(8,128)(2,1)S(1)} fusion(bf16[1,2,4,16,896]{4,3,2,1,0:T(8,128)(2,1)} %bitcast.11, bf16[1,2,4,16,896]{4,3,2,1,0:T(8,128)(2,1)} %bitcast.10, bf16[1,2,4,16,896]{4,3,2,1,0:T(8,128)(2,1)} %bitcast.9, bf16[1,2,4,16,896]{4,3,2,1,0:T(8,128)(2,1)S(1)} %bitcast.18), kind=kLoop, calls=%fused_computation | loop fusion | flops 1376256 | bytes 1835008 | tf_op jit(solution)/shard_map/stack | solution.py:225
  44.8 4.0 %collective-permute-start.7 = (bf16[4,16,896]{2,1,0:T(8,128)(2,1)S(1)}, bf16[4,16,896]{2,1,0:T(8,128)(2,1)S(1)}, u32[]{:S(2)}, u32[]{:S(2)}) collective-permute-start(bf16[4,16,896]{2,1,0:T(8,128)(2,1)S(1)} %get-tuple-element.57), channel_id=1, source_target_pairs={{192,0},{224,32},{0,64},{32,96},{64,128},{96,160},{128,192},{160,2... | collective-permute-start | bytes 344072 | tf_op jit(solution)/shard_map/ppermute | solution.py:27
  48.8 1.2 %collective-permute-start.8 = (bf16[4,16,896]{2,1,0:T(8,128)(2,1)S(1)}, bf16[4,16,896]{2,1,0:T(8,128)(2,1)S(1)}, u32[]{:S(2)}, u32[]{:S(2)}) collective-permute-start(bf16[4,16,896]{2,1,0:T(8,128)(2,1)S(1)} %get-tuple-element.58), channel_id=1, source_target_pairs={{128,0},{160,32},{192,64},{224,96},{0,128},{32,160},{64,192},{96,2... | collective-permute-start | bytes 344072 | tf_op jit(solution)/shard_map/ppermute | solution.py:27
  50.0 1.6 %collective-permute-start.9 = (bf16[4,16,896]{2,1,0:T(8,128)(2,1)S(1)}, bf16[4,16,896]{2,1,0:T(8,128)(2,1)S(1)}, u32[]{:S(2)}, u32[]{:S(2)}) collective-permute-start(bf16[4,16,896]{2,1,0:T(8,128)(2,1)S(1)} %get-tuple-element.59), channel_id=1, source_target_pairs={{64,0},{96,32},{128,64},{160,96},{192,128},{224,160},{0,192},{32,2... | collective-permute-start | bytes 344072 | tf_op jit(solution)/shard_map/ppermute | solution.py:27
  51.5 1.2 %collective-permute-start.20 = (bf16[8,16,1024]{2,1,0:T(8,128)(2,1)S(1)}, bf16[8,16,1024]{2,1,0:T(8,128)(2,1)S(1)}, u32[]{:S(2)}, u32[]{:S(2)}) collective-permute-start(bf16[8,16,1024]{2,1,0:T(8,128)(2,1)S(1)} %get-tuple-element.91.refs_0_), channel_id=1, source_target_pairs={{3,0},{0,1},{1,2},{2,3},{7,4},{4,5},{5,6},{6,7},{11,8},{8,9},{9,10... | collective-permute-start | bytes 786440 | tf_op jit(solution)/shard_map/ppermute | solution.py:31
  52.8 1.4 %gate_terms.1 = (f32[2,512,896]{2,1,0:T(8,128)S(1)}, bf16[512,896]{1,0:T(8,128)(2,1)S(1)}) custom-call(bf16[4,2,4,16,896]{4,3,2,1,0:T(8,128)(2,1)S(1)} %pad_maximum_fusion.mine_ref, bf16[4,2,4,16,896]{4,3,2,1,0:T(8,128)(2,1)S(1)} %collective-permute-done.10.other_ref), custom_call_target="tpu_custom_call" | custom-call | flops 7340032 | bytes 5505024 | tf_op jit(solution)/shard_map/gate_terms/pallas_call | solution.py:114
  55.1 3.0 %collective-permute-start.19 = (bf16[8,16,1024]{2,1,0:T(8,128)(2,1)S(1)}, bf16[8,16,1024]{2,1,0:T(8,128)(2,1)S(1)}, u32[]{:S(2)}, u32[]{:S(2)}) collective-permute-start(bf16[8,16,1024]{2,1,0:T(8,128)(2,1)S(1)} %get-tuple-element.91.refs_0_), channel_id=1, source_target_pairs={{2,0},{3,1},{0,2},{1,3},{6,4},{7,5},{4,6},{5,7},{10,8},{11,9},{8,1... | collective-permute-start | bytes 786440 | tf_op jit(solution)/shard_map/ppermute | solution.py:31
  58.9 2.3 %collective-permute-start.13 = (bf16[4,16,896]{2,1,0:T(8,128)(2,1)S(1)}, bf16[4,16,896]{2,1,0:T(8,128)(2,1)S(1)}, u32[]{:S(2)}, u32[]{:S(2)}) collective-permute-start(bf16[4,16,896]{2,1,0:T(8,128)(2,1)S(1)} %add_convert_fusion.1.refs_0_), channel_id=1, source_target_pairs={{128,0},{160,32},{192,64},{224,96},{0,128},{32,160},{64,192},{96,2... | collective-permute-start | bytes 344072 | tf_op jit(solution)/shard_map/ppermute | solution.py:27
  62.5 3.3 %collective-permute-done.14.refs_3_ = bf16[4,16,896]{2,1,0:T(8,128)(2,1)S(1)} collective-permute-done((bf16[4,16,896]{2,1,0:T(8,128)(2,1)S(1)}, bf16[4,16,896]{2,1,0:T(8,128)(2,1)S(1)}, u32[]{:S(2)}, u32[]{:S(2)}) %collective-permute-start.14) | collective-permute-done | bytes 114720 | tf_op jit(solution)/shard_map/ppermute | solution.py:27
  67.9 2.4 %input_terms.1 = (bf16[2,512,896]{2,1,0:T(8,128)(2,1)S(1)}, f32[128,1024]{1,0:T(8,128)S(1)}, bf16[128,1024]{1,0:T(8,128)(2,1)S(1)}, bf16[128,1024]{1,0:T(8,128)(2,1)S(1)}, bf16[128,1024]{1,0:T(8,128)(2,1)S(1)}) custom-call(bf16[4,16,896]{2,1,0:T(8,128)(2,1)S(1)} %add_convert_fusion.1.refs_0_, bf16[4,16,896]{2,1,0:T(8,128)(2,1)S(1)} %collective-permute-done.12.refs_1_, ...), custom_call_target="tpu_custom_call" | custom-call | flops 1879048192 | bytes 3670016 | tf_op jit(solution)/shard_map/input_terms/pallas_call | solution.py:151
  70.5 4.8 %collective-permute-start.22 = (bf16[128,1024]{1,0:T(8,128)(2,1)S(1)}, bf16[128,1024]{1,0:T(8,128)(2,1)S(1)}, u32[]{:S(2)}, u32[]{:S(2)}) collective-permute-start(bf16[128,1024]{1,0:T(8,128)(2,1)S(1)} %get-tuple-element.82), channel_id=1, source_target_pairs={{2,0},{3,1},{0,2},{1,3},{6,4},{7,5},{4,6},{5,7},{10,8},{11,9},{8,1... | collective-permute-start | bytes 786440 | tf_op jit(solution)/shard_map/ppermute | solution.py:31
  75.3 5.1 %collective-permute-done.21 = bf16[128,1024]{1,0:T(8,128)(2,1)S(1)} collective-permute-done((bf16[128,1024]{1,0:T(8,128)(2,1)S(1)}, bf16[128,1024]{1,0:T(8,128)(2,1)S(1)}, u32[]{:S(2)}, u32[]{:S(2)}) %collective-permute-start.21) | collective-permute-done | bytes 262176 | tf_op jit(solution)/shard_map/ppermute | solution.py:31
  80.3 2.1 %collective-permute-done.22 = bf16[128,1024]{1,0:T(8,128)(2,1)S(1)} collective-permute-done((bf16[128,1024]{1,0:T(8,128)(2,1)S(1)}, bf16[128,1024]{1,0:T(8,128)(2,1)S(1)}, u32[]{:S(2)}, u32[]{:S(2)}) %collective-permute-start.22) | collective-permute-done | bytes 262176 | tf_op jit(solution)/shard_map/ppermute | solution.py:31
  82.4 5.0 %collective-permute-done.23 = bf16[128,1024]{1,0:T(8,128)(2,1)S(1)} collective-permute-done((bf16[128,1024]{1,0:T(8,128)(2,1)S(1)}, bf16[128,1024]{1,0:T(8,128)(2,1)S(1)}, u32[]{:S(2)}, u32[]{:S(2)}) %collective-permute-start.23) | collective-permute-done | bytes 262176 | tf_op jit(solution)/shard_map/ppermute | solution.py:31
  88.2 4.6 %all-to-all-start.1 = ((bf16[8,16,1024]{2,1,0:T(8,128)(2,1)}), bf16[8,16,1024]{2,1,0:T(8,128)(2,1)}, u32[]{:S(2)}, u32[]{:S(2)}) async-start(bf16[8,16,1024]{2,1,0:T(8,128)(2,1)} %bitcast.17), calls=%async_computation.1 | async-start | bytes 524288 | tf_op jit(solution)/shard_map/all_to_all | solution.py:39
  92.9 1.2 %copy-done.4 = bf16[512,896]{1,0:T(8,128)(2,1)S(1)} copy-done((bf16[512,896]{1,0:T(8,128)(2,1)S(1)}, bf16[512,896]{1,0:T(8,128)(2,1)}, u32[]{:S(2)}) %copy-start.4) | copy-done | bytes 917528
  94.0 0.9 copy-done.6
  95.0 0.9 copy-done.8
  95.9 5.0 %weight_grads.1 = (bf16[1024,896]{1,0:T(8,128)(2,1)}, bf16[1024,896]{1,0:T(8,128)(2,1)}, bf16[1024,896]{1,0:T(8,128)(2,1)}) custom-call(bf16[8,16,1024]{2,1,0:T(8,128)(2,1)S(1)} %get-tuple-element.91.refs_0_, bf16[8,16,1024]{2,1,0:T(8,128)(2,1)S(1)} %collective-permute-done.11.refs_1_, bf16[8,16,1024]{2,1,0:T(8,128)(2,1)S(1)} %copy-done.8, ...), custom_call_target="tpu_custom_call" | custom-call | flops 2818572288 | bytes 5505024 | tf_op jit(solution)/shard_map/weight_grads/pallas_call | solution.py:196
  100.9 2.3 %all-to-all-done.1 = bf16[8,16,1024]{2,1,0:T(8,128)(2,1)} async-done(((bf16[8,16,1024]{2,1,0:T(8,128)(2,1)}), bf16[8,16,1024]{2,1,0:T(8,128)(2,1)}, u32[]{:S(2)}, u32[]{:S(2)}) %all-to-all-start.1) | async-done | bytes 262176 | tf_op jit(solution)/shard_map/all_to_all | solution.py:39
  103.2 1.0 reduce_sum.12
  (65 shorter events, 12.2 us)
Async XLA Ops:
  0.6 10.5 %copy-start.9 = (bf16[4,16,896]{2,1,0:T(8,128)(2,1)S(1)}, bf16[4,16,896]{2,1,0:T(8,128)(2,1)}, u32[]{:S(2)}) copy-start(bf16[4,16,896]{2,1,0:T(8,128)(2,1)} %param.9) | copy-start | bytes 344068
  0.6 10.6 %copy-start.10 = (bf16[4,16,896]{2,1,0:T(8,128)(2,1)S(1)}, bf16[4,16,896]{2,1,0:T(8,128)(2,1)}, u32[]{:S(2)}) copy-start(bf16[4,16,896]{2,1,0:T(8,128)(2,1)} %param.10) | copy-start | bytes 344068
  2.5 23.2 %all-to-all-start = ((bf16[8,2,4,4,1024]{4,3,2,1,0:T(4,128)(2,1)}), bf16[8,2,4,4,1024]{4,3,2,1,0:T(4,128)(2,1)S(1)}, u32[]{:S(2)}, u32[]{:S(2)}) async-start(bf16[8,2,4,4,1024]{4,3,2,1,0:T(4,128)(2,1)} %broadcast_in_dim.3), calls=%async_computation | async-start | bytes 1048576 | tf_op jit(solution)/shard_map/all_to_all | solution.py:39
  11.5 29.1 %copy-start = (bf16[1024,896]{1,0:T(8,128)(2,1)S(1)}, bf16[1024,896]{1,0:T(8,128)(2,1)}, u32[]{:S(2)}) copy-start(bf16[1024,896]{1,0:T(8,128)(2,1)} %refs_4_.3) | copy-start | bytes 5505028
  11.5 14.4 %collective-permute-start.2 = (bf16[2,4,16,896]{3,2,1,0:T(8,128)(2,1)S(1)}, bf16[2,4,16,896]{3,2,1,0:T(8,128)(2,1)}, u32[]{:S(2)}, u32[]{:S(2)}) collective-permute-start(bf16[2,4,16,896]{3,2,1,0:T(8,128)(2,1)S(1)} %pad_maximum_fusion.1), channel_id=1, source_target_pairs={{192,0},{224,32},{0,64},{32,96},{64,128},{96,160},{128,192},{160,2... | collective-permute-start | bytes 688136 | tf_op jit(solution)/shard_map/ppermute | solution.py:27
  13.1 13.0 %collective-permute-start.1 = (bf16[2,4,16,896]{3,2,1,0:T(8,128)(2,1)S(1)}, bf16[2,4,16,896]{3,2,1,0:T(8,128)(2,1)}, u32[]{:S(2)}, u32[]{:S(2)}) collective-permute-start(bf16[2,4,16,896]{3,2,1,0:T(8,128)(2,1)S(1)} %pad_maximum_fusion.1), channel_id=1, source_target_pairs={{128,0},{160,32},{192,64},{224,96},{0,128},{32,160},{64,192},{96,2... | collective-permute-start | bytes 688136 | tf_op jit(solution)/shard_map/ppermute | solution.py:27
  16.5 9.6 %collective-permute-start = (bf16[2,4,16,896]{3,2,1,0:T(8,128)(2,1)S(1)}, bf16[2,4,16,896]{3,2,1,0:T(8,128)(2,1)}, u32[]{:S(2)}, u32[]{:S(2)}) collective-permute-start(bf16[2,4,16,896]{3,2,1,0:T(8,128)(2,1)S(1)} %pad_maximum_fusion.1), channel_id=1, source_target_pairs={{64,0},{96,32},{128,64},{160,96},{192,128},{224,160},{0,192},{32,2... | collective-permute-start | bytes 688136 | tf_op jit(solution)/shard_map/ppermute | solution.py:27
  26.1 9.3 %collective-permute-start.5 = (bf16[8,16,1024]{2,1,0:T(8,128)(2,1)S(1)}, bf16[8,16,1024]{2,1,0:T(8,128)(2,1)S(1)}, u32[]{:S(2)}, u32[]{:S(2)}) collective-permute-start(bf16[8,16,1024]{2,1,0:T(8,128)(2,1)S(1)} %get-tuple-element.95.refs_0_.refs_4_), channel_id=1, source_target_pairs={{3,0},{0,1},{1,2},{2,3},{7,4},{4,5},{5,6},{6,7},{11,8},{8,9},{9,10... | collective-permute-start | bytes 786440 | tf_op jit(solution)/shard_map/ppermute | solution.py:31
  27.8 10.7 %collective-permute-start.4 = (bf16[8,16,1024]{2,1,0:T(8,128)(2,1)S(1)}, bf16[8,16,1024]{2,1,0:T(8,128)(2,1)S(1)}, u32[]{:S(2)}, u32[]{:S(2)}) collective-permute-start(bf16[8,16,1024]{2,1,0:T(8,128)(2,1)S(1)} %get-tuple-element.95.refs_0_.refs_4_), channel_id=1, source_target_pairs={{2,0},{3,1},{0,2},{1,3},{6,4},{7,5},{4,6},{5,7},{10,8},{11,9},{8,1... | collective-permute-start | bytes 786440 | tf_op jit(solution)/shard_map/ppermute | solution.py:31
  28.7 11.8 %collective-permute-start.3 = (bf16[8,16,1024]{2,1,0:T(8,128)(2,1)S(1)}, bf16[8,16,1024]{2,1,0:T(8,128)(2,1)S(1)}, u32[]{:S(2)}, u32[]{:S(2)}) collective-permute-start(bf16[8,16,1024]{2,1,0:T(8,128)(2,1)S(1)} %get-tuple-element.95.refs_0_.refs_4_), channel_id=1, source_target_pairs={{1,0},{2,1},{3,2},{0,3},{5,4},{6,5},{7,6},{4,7},{9,8},{10,9},{11,1... | collective-permute-start | bytes 786440 | tf_op jit(solution)/shard_map/ppermute | solution.py:31
  41.3 2.8 %collective-permute-start.6 = (f32[256,896]{1,0:T(8,128)S(1)}, f32[256,896]{1,0:T(8,128)S(1)}, u32[]{:S(2)}, u32[]{:S(2)}) collective-permute-start(f32[256,896]{1,0:T(8,128)S(1)} %half_1.1), channel_id=1, source_target_pairs={{0,32},{32,0},{64,96},{96,64},{128,160},{160,128},{192,224},{224,1... | collective-permute-start | bytes 2752520 | tf_op jit(solution)/shard_map/ppermute | solution.py:35
  42.7 8.9 %collective-permute-start.10 = (bf16[4,2,4,16,896]{4,3,2,1,0:T(8,128)(2,1)S(1)}, bf16[4,2,4,16,896]{4,3,2,1,0:T(8,128)(2,1)S(1)}, u32[]{:S(2)}, u32[]{:S(2)}) collective-permute-start(bf16[4,2,4,16,896]{4,3,2,1,0:T(8,128)(2,1)S(1)} %pad_maximum_fusion.mine_ref), channel_id=1, source_target_pairs={{0,32},{32,0},{64,96},{96,64},{128,160},{160,128},{192,224},{224,1... | collective-permute-start | bytes 2752520 | tf_op jit(solution)/shard_map/ppermute | solution.py:35
  43.2 11.9 %collective-permute-start.11 = (bf16[8,16,1024]{2,1,0:T(8,128)(2,1)S(1)}, bf16[8,16,1024]{2,1,0:T(8,128)(2,1)S(1)}, u32[]{:S(2)}, u32[]{:S(2)}) collective-permute-start(bf16[8,16,1024]{2,1,0:T(8,128)(2,1)S(1)} %get-tuple-element.91.refs_0_), channel_id=1, source_target_pairs={{1,0},{2,1},{3,2},{0,3},{5,4},{6,5},{7,6},{4,7},{9,8},{10,9},{11,1... | collective-permute-start | bytes 786440 | tf_op jit(solution)/shard_map/ppermute | solution.py:31
  44.0 23.9 %copy-start.2 = (bf16[1024,896]{1,0:T(8,128)(2,1)S(1)}, bf16[1024,896]{1,0:T(8,128)(2,1)}, u32[]{:S(2)}) copy-start(bf16[1024,896]{1,0:T(8,128)(2,1)} %refs_10_.1) | copy-start | bytes 5505028
  44.8 23.2 %copy-start.1 = (bf16[1024,896]{1,0:T(8,128)(2,1)S(1)}, bf16[1024,896]{1,0:T(8,128)(2,1)}, u32[]{:S(2)}) copy-start(bf16[1024,896]{1,0:T(8,128)(2,1)} %refs_9_.1) | copy-start | bytes 5505028
  44.8 13.3 %collective-permute-start.7 = (bf16[4,16,896]{2,1,0:T(8,128)(2,1)S(1)}, bf16[4,16,896]{2,1,0:T(8,128)(2,1)S(1)}, u32[]{:S(2)}, u32[]{:S(2)}) collective-permute-start(bf16[4,16,896]{2,1,0:T(8,128)(2,1)S(1)} %get-tuple-element.57), channel_id=1, source_target_pairs={{192,0},{224,32},{0,64},{32,96},{64,128},{96,160},{128,192},{160,2... | collective-permute-start | bytes 344072 | tf_op jit(solution)/shard_map/ppermute | solution.py:27
  48.8 9.3 %collective-permute-start.8 = (bf16[4,16,896]{2,1,0:T(8,128)(2,1)S(1)}, bf16[4,16,896]{2,1,0:T(8,128)(2,1)S(1)}, u32[]{:S(2)}, u32[]{:S(2)}) collective-permute-start(bf16[4,16,896]{2,1,0:T(8,128)(2,1)S(1)} %get-tuple-element.58), channel_id=1, source_target_pairs={{128,0},{160,32},{192,64},{224,96},{0,128},{32,160},{64,192},{96,2... | collective-permute-start | bytes 344072 | tf_op jit(solution)/shard_map/ppermute | solution.py:27
  50.0 8.1 %collective-permute-start.9 = (bf16[4,16,896]{2,1,0:T(8,128)(2,1)S(1)}, bf16[4,16,896]{2,1,0:T(8,128)(2,1)S(1)}, u32[]{:S(2)}, u32[]{:S(2)}) collective-permute-start(bf16[4,16,896]{2,1,0:T(8,128)(2,1)S(1)} %get-tuple-element.59), channel_id=1, source_target_pairs={{64,0},{96,32},{128,64},{160,96},{192,128},{224,160},{0,192},{32,2... | collective-permute-start | bytes 344072 | tf_op jit(solution)/shard_map/ppermute | solution.py:27
  51.5 10.3 %collective-permute-start.20 = (bf16[8,16,1024]{2,1,0:T(8,128)(2,1)S(1)}, bf16[8,16,1024]{2,1,0:T(8,128)(2,1)S(1)}, u32[]{:S(2)}, u32[]{:S(2)}) collective-permute-start(bf16[8,16,1024]{2,1,0:T(8,128)(2,1)S(1)} %get-tuple-element.91.refs_0_), channel_id=1, source_target_pairs={{3,0},{0,1},{1,2},{2,3},{7,4},{4,5},{5,6},{6,7},{11,8},{8,9},{9,10... | collective-permute-start | bytes 786440 | tf_op jit(solution)/shard_map/ppermute | solution.py:31
  55.1 11.5 %collective-permute-start.19 = (bf16[8,16,1024]{2,1,0:T(8,128)(2,1)S(1)}, bf16[8,16,1024]{2,1,0:T(8,128)(2,1)S(1)}, u32[]{:S(2)}, u32[]{:S(2)}) collective-permute-start(bf16[8,16,1024]{2,1,0:T(8,128)(2,1)S(1)} %get-tuple-element.91.refs_0_), channel_id=1, source_target_pairs={{2,0},{3,1},{0,2},{1,3},{6,4},{7,5},{4,6},{5,7},{10,8},{11,9},{8,1... | collective-permute-start | bytes 786440 | tf_op jit(solution)/shard_map/ppermute | solution.py:31
  58.2 7.7 %collective-permute-start.14 = (bf16[4,16,896]{2,1,0:T(8,128)(2,1)S(1)}, bf16[4,16,896]{2,1,0:T(8,128)(2,1)S(1)}, u32[]{:S(2)}, u32[]{:S(2)}) collective-permute-start(bf16[4,16,896]{2,1,0:T(8,128)(2,1)S(1)} %add_convert_fusion.1.refs_0_), channel_id=1, source_target_pairs={{192,0},{224,32},{0,64},{32,96},{64,128},{96,160},{128,192},{160,2... | collective-permute-start | bytes 344072 | tf_op jit(solution)/shard_map/ppermute | solution.py:27
  58.9 6.9 %collective-permute-start.13 = (bf16[4,16,896]{2,1,0:T(8,128)(2,1)S(1)}, bf16[4,16,896]{2,1,0:T(8,128)(2,1)S(1)}, u32[]{:S(2)}, u32[]{:S(2)}) collective-permute-start(bf16[4,16,896]{2,1,0:T(8,128)(2,1)S(1)} %add_convert_fusion.1.refs_0_), channel_id=1, source_target_pairs={{128,0},{160,32},{192,64},{224,96},{0,128},{32,160},{64,192},{96,2... | collective-permute-start | bytes 344072 | tf_op jit(solution)/shard_map/ppermute | solution.py:27
  61.2 5.4 %collective-permute-start.12 = (bf16[4,16,896]{2,1,0:T(8,128)(2,1)S(1)}, bf16[4,16,896]{2,1,0:T(8,128)(2,1)S(1)}, u32[]{:S(2)}, u32[]{:S(2)}) collective-permute-start(bf16[4,16,896]{2,1,0:T(8,128)(2,1)S(1)} %add_convert_fusion.1.refs_0_), channel_id=1, source_target_pairs={{64,0},{96,32},{128,64},{160,96},{192,128},{224,160},{0,192},{32,2... | collective-permute-start | bytes 344072 | tf_op jit(solution)/shard_map/ppermute | solution.py:27
  62.5 4.1 %collective-permute-start.15 = (bf16[4,16,896]{2,1,0:T(8,128)(2,1)S(1)}, bf16[4,16,896]{2,1,0:T(8,128)(2,1)S(1)}, u32[]{:S(2)}, u32[]{:S(2)}) collective-permute-start(bf16[4,16,896]{2,1,0:T(8,128)(2,1)S(1)} %add_convert_fusion.1.refs_0_), channel_id=1, source_target_pairs={{0,32},{32,0},{64,96},{96,64},{128,160},{160,128},{192,224},{224,1... | collective-permute-start | bytes 344072 | tf_op jit(solution)/shard_map/ppermute | solution.py:35
  65.8 1.3 %collective-permute-start.18 = (bf16[4,16,896]{2,1,0:T(8,128)(2,1)S(1)}, bf16[4,16,896]{2,1,0:T(8,128)(2,1)S(1)}, u32[]{:S(2)}, u32[]{:S(2)}) collective-permute-start(bf16[4,16,896]{2,1,0:T(8,128)(2,1)S(1)} %collective-permute-done.14.refs_3_), channel_id=1, source_target_pairs={{0,32},{32,0},{64,96},{96,64},{128,160},{160,128},{192,224},{224,1... | collective-permute-start | bytes 344072 | tf_op jit(solution)/shard_map/ppermute | solution.py:35
  65.9 1.5 %collective-permute-start.17 = (bf16[4,16,896]{2,1,0:T(8,128)(2,1)S(1)}, bf16[4,16,896]{2,1,0:T(8,128)(2,1)S(1)}, u32[]{:S(2)}, u32[]{:S(2)}) collective-permute-start(bf16[4,16,896]{2,1,0:T(8,128)(2,1)S(1)} %collective-permute-done.13.refs_2_), channel_id=1, source_target_pairs={{0,32},{32,0},{64,96},{96,64},{128,160},{160,128},{192,224},{224,1... | collective-permute-start | bytes 344072 | tf_op jit(solution)/shard_map/ppermute | solution.py:35
  66.6 1.3 %collective-permute-start.16 = (bf16[4,16,896]{2,1,0:T(8,128)(2,1)S(1)}, bf16[4,16,896]{2,1,0:T(8,128)(2,1)S(1)}, u32[]{:S(2)}, u32[]{:S(2)}) collective-permute-start(bf16[4,16,896]{2,1,0:T(8,128)(2,1)S(1)} %collective-permute-done.12.refs_1_), channel_id=1, source_target_pairs={{0,32},{32,0},{64,96},{96,64},{128,160},{160,128},{192,224},{224,1... | collective-permute-start | bytes 344072 | tf_op jit(solution)/shard_map/ppermute | solution.py:35
  66.6 3.7 %copy-start.7 = (bf16[8,16,1024]{2,1,0:T(8,128)(2,1)}, bf16[8,16,1024]{2,1,0:T(8,128)(2,1)S(1)}, u32[]{:S(2)}) copy-start(bf16[8,16,1024]{2,1,0:T(8,128)(2,1)S(1)} %collective-permute-done.19.refs_2_) | copy-start | bytes 786436
  70.3 10.0 %collective-permute-start.21 = (bf16[128,1024]{1,0:T(8,128)(2,1)S(1)}, bf16[128,1024]{1,0:T(8,128)(2,1)S(1)}, u32[]{:S(2)}, u32[]{:S(2)}) collective-permute-start(bf16[128,1024]{1,0:T(8,128)(2,1)S(1)} %get-tuple-element.81), channel_id=1, source_target_pairs={{3,0},{0,1},{1,2},{2,3},{7,4},{4,5},{5,6},{6,7},{11,8},{8,9},{9,10... | collective-permute-start | bytes 786440 | tf_op jit(solution)/shard_map/ppermute | solution.py:31
  70.5 11.9 %collective-permute-start.22 = (bf16[128,1024]{1,0:T(8,128)(2,1)S(1)}, bf16[128,1024]{1,0:T(8,128)(2,1)S(1)}, u32[]{:S(2)}, u32[]{:S(2)}) collective-permute-start(bf16[128,1024]{1,0:T(8,128)(2,1)S(1)} %get-tuple-element.82), channel_id=1, source_target_pairs={{2,0},{3,1},{0,2},{1,3},{6,4},{7,5},{4,6},{5,7},{10,8},{11,9},{8,1... | collective-permute-start | bytes 786440 | tf_op jit(solution)/shard_map/ppermute | solution.py:31
  75.2 12.2 %collective-permute-start.23 = (bf16[128,1024]{1,0:T(8,128)(2,1)S(1)}, bf16[128,1024]{1,0:T(8,128)(2,1)S(1)}, u32[]{:S(2)}, u32[]{:S(2)}) collective-permute-start(bf16[128,1024]{1,0:T(8,128)(2,1)S(1)} %get-tuple-element.83), channel_id=1, source_target_pairs={{1,0},{2,1},{3,2},{0,3},{5,4},{6,5},{7,6},{4,7},{9,8},{10,9},{11,1... | collective-permute-start | bytes 786440 | tf_op jit(solution)/shard_map/ppermute | solution.py:31
  88.2 15.0 %all-to-all-start.1 = ((bf16[8,16,1024]{2,1,0:T(8,128)(2,1)}), bf16[8,16,1024]{2,1,0:T(8,128)(2,1)}, u32[]{:S(2)}, u32[]{:S(2)}) async-start(bf16[8,16,1024]{2,1,0:T(8,128)(2,1)} %bitcast.17), calls=%async_computation.1 | async-start | bytes 524288 | tf_op jit(solution)/shard_map/all_to_all | solution.py:39
  (5 other events, 4.7 us)

commit v3 on v2

--- a/solution.py
+++ b/solution.py
@@ -218,18 +218,18 @@
 
     pre = jnp.stack([own_tokens(gate_pre, tensor % Y), own_tokens(up_pre, tensor % Y)])
     pre = [pre] + [from_x(pre, j) for j in range(1, X)]
-    both, pre = lax.optimization_barrier((both, pre))
+    both, pre = lax.optimization_barrier((both, jnp.stack(pre)))
     grad_z, in_z = both[:, 0], both[:, 1]
     grad_y = [grad_z] + [from_y(grad_z, j) for j in range(1, Y)]
 
-    pre = jnp.stack(pre)
     factors, hidden = gate_terms(pre, swap_core(pre))
+    grad_y, factors, hidden = lax.optimization_barrier((grad_y, factors, hidden))
     theirs, in_z = lax.optimization_barrier((half_dot(1, grad_y, down_weight), in_z))
     theirs = swap_core(theirs)
     dhid, *blocks = half_dot(0, grad_y, down_weight, (theirs,))
     blocks = [from_x(blocks[j - 1], -j) for j in range(1, X)]
     in_y = [in_z] + [from_y(in_z, j) for j in range(1, Y)]
-    blocks, factors, hidden, in_y[1] = lax.optimization_barrier((blocks, factors, hidden, in_y[1]))
+    blocks, in_y[1] = lax.optimization_barrier((blocks, in_y[1]))
     for block in blocks:
         dhid = dhid + block.astype(F32)
 

time: 106 us -> 106 us (level)
  waiting for transfers between devices: 36.6 us -> 41.1 us
  other arithmetic: 4.19 us -> 2.1 us
  local copies, waits for them, and re-layouts: 6.77 us -> 4.79 us
    ppermute x9, waiting for transfers between devices: 3.69 us -> 12.8 us  [from_x(): lax.ppermute(block, 'dp', [((d // C + step) % X * C + d % C, d) for d in...]
    all_to_all x2, waiting for transfers between devices: 10.1 us -> 3.6 us  [exchange_z(): lax.all_to_all(blocks, ('dp', 'tensor'), 0, 0, axis_index_groups=Z_GROUPS)]
    unnamed x22 -> x14, local copies, waits for them, and re-layouts: 4.73 us -> 2.75 us
    ppermute x9, starting transfers between devices: 15 us -> 13.1 us  [from_y(): lax.ppermute(block, 'tensor', [(t // Y * Y + (t % Y + step) % Y, t) for t...]
    ppermute x6, waiting for transfers between devices: 1.31 us -> 2.56 us  [swap_core(): return lax.ppermute(block, 'dp', CORE_SWAP)]
    all_to_all x2, starting transfers between devices: 13.2 us -> 14.4 us  [exchange_z(): lax.all_to_all(blocks, ('dp', 'tensor'), 0, 0, axis_index_groups=Z_GROUPS)]
    another operation x1 -> x2, other arithmetic: 1.3 us -> 0.18 us  [shards(): both, pre = lax.optimization_barrier((both, jnp.stack(pre)))]
    ppermute x9, starting transfers between devices: 16.9 us -> 18 us  [from_x(): lax.ppermute(block, 'dp', [((d // C + step) % X * C + d % C, d) for d in...]
  transfers between devices with their start and end apart: 26 -> 26, of which waited for: 14 -> 17; matrix products, arithmetic and copies ran while one was open for 2% -> 1% of each run, Pallas kernels for 7% -> 7%
where the time goes in v3:
time: 106 us; the launch traced here: 105 us
  starting transfers between devices  46.2 us (44%)
  waiting for transfers between devices  41.1 us (39%)
  Pallas kernels  10.2 us (10%)
  local copies, waits for them, and re-layouts  4.79 us (5%)
  other arithmetic  2.1 us (2%)
    ppermute x9, waiting for transfers between devices, from_y(): lax.ppermute(block, 'tensor', [(t // Y * Y + (t % Y + step) % Y, t) for t...  22.2 us
    ppermute x9, starting transfers between devices, from_x(): lax.ppermute(block, 'dp', [((d // C + step) % X * C + d % C, d) for d in...  18 us
    all_to_all x2, starting transfers between devices, exchange_z(): lax.all_to_all(blocks, ('dp', 'tensor'), 0, 0, axis_index_groups=Z_GROUPS)  14.4 us
    ppermute x9, starting transfers between devices, from_y(): lax.ppermute(block, 'tensor', [(t // Y * Y + (t % Y + step) % Y, t) for t...  13.1 us
    ppermute x9, waiting for transfers between devices, from_x(): lax.ppermute(block, 'dp', [((d // C + step) % X * C + d % C, d) for d in...  12.8 us
    pallas_call x1, Pallas kernels, weight_grads(): pl.pallas_call(weight_kernel, out_shape=[jax.ShapeDtypeStruct((width, col...  4.98 us
    all_to_all x2, waiting for transfers between devices, exchange_z(): lax.all_to_all(blocks, ('dp', 'tensor'), 0, 0, axis_index_groups=Z_GROUPS)  3.6 us
    unnamed x14, local copies, waits for them, and re-layouts  2.75 us
  transfers between devices with their start and end apart: 26, of which 17 were waited for; matrix products, arithmetic and copies ran while one was open for 1% of the time, Pallas kernels for 7%

profile of v3, /device:TPU:40, one launch (start us, length us, event | category | flops | bytes accessed | tf_op | source)
XLA Modules:
  0.0 105.3 jit_solution(15248095358465326859)
XLA Ops:
  2.5 8.6 %all-to-all-start = ((bf16[8,2,4,4,1024]{4,3,2,1,0:T(4,128)(2,1)}), bf16[8,2,4,4,1024]{4,3,2,1,0:T(4,128)(2,1)S(1)}, u32[]{:S(2)}, u32[]{:S(2)}) async-start(bf16[8,2,4,4,1024]{4,3,2,1,0:T(4,128)(2,1)} %broadcast_in_dim.3), calls=%async_computation | async-start | bytes 1048576 | tf_op jit(solution)/shard_map/all_to_all | solution.py:39
  11.5 3.8 %collective-permute-start.1 = (bf16[2,4,16,896]{3,2,1,0:T(8,128)(2,1)S(1)}, bf16[2,4,16,896]{3,2,1,0:T(8,128)(2,1)S(1)}, u32[]{:S(2)}, u32[]{:S(2)}) collective-permute-start(bf16[2,4,16,896]{3,2,1,0:T(8,128)(2,1)S(1)} %get-tuple-element.109), channel_id=1, source_target_pairs={{128,0},{160,32},{192,64},{224,96},{0,128},{32,160},{64,192},{96,2... | collective-permute-start | bytes 688136 | tf_op jit(solution)/shard_map/ppermute | solution.py:27
  15.8 1.6 %collective-permute-start.2 = (bf16[2,4,16,896]{3,2,1,0:T(8,128)(2,1)S(1)}, bf16[2,4,16,896]{3,2,1,0:T(8,128)(2,1)S(1)}, u32[]{:S(2)}, u32[]{:S(2)}) collective-permute-start(bf16[2,4,16,896]{3,2,1,0:T(8,128)(2,1)S(1)} %get-tuple-element.109), channel_id=1, source_target_pairs={{192,0},{224,32},{0,64},{32,96},{64,128},{96,160},{128,192},{160,2... | collective-permute-start | bytes 688136 | tf_op jit(solution)/shard_map/ppermute | solution.py:27
  17.3 4.4 %collective-permute-done.1 = bf16[2,4,16,896]{3,2,1,0:T(8,128)(2,1)S(1)} collective-permute-done((bf16[2,4,16,896]{3,2,1,0:T(8,128)(2,1)S(1)}, bf16[2,4,16,896]{3,2,1,0:T(8,128)(2,1)S(1)}, u32[]{:S(2)}, u32[]{:S(2)}) %collective-permute-start.1) | collective-permute-done | bytes 229408 | tf_op jit(solution)/shard_map/ppermute | solution.py:27
  21.7 3.7 %collective-permute-done = bf16[2,4,16,896]{3,2,1,0:T(8,128)(2,1)S(1)} collective-permute-done((bf16[2,4,16,896]{3,2,1,0:T(8,128)(2,1)S(1)}, bf16[2,4,16,896]{3,2,1,0:T(8,128)(2,1)S(1)}, u32[]{:S(2)}, u32[]{:S(2)}) %collective-permute-start) | collective-permute-done | bytes 229408 | tf_op jit(solution)/shard_map/ppermute | solution.py:27
  26.5 1.7 %collective-permute-start.5 = (bf16[8,16,1024]{2,1,0:T(8,128)(2,1)S(1)}, bf16[8,16,1024]{2,1,0:T(8,128)(2,1)S(1)}, u32[]{:S(2)}, u32[]{:S(2)}) collective-permute-start(bf16[8,16,1024]{2,1,0:T(8,128)(2,1)S(1)} %get-tuple-element.97.refs_0_.refs_4_), channel_id=1, source_target_pairs={{3,0},{0,1},{1,2},{2,3},{7,4},{4,5},{5,6},{6,7},{11,8},{8,9},{9,10... | collective-permute-start | bytes 786440 | tf_op jit(solution)/shard_map/ppermute | solution.py:31
  29.1 2.4 %collective-permute-start.3 = (bf16[8,16,1024]{2,1,0:T(8,128)(2,1)S(1)}, bf16[8,16,1024]{2,1,0:T(8,128)(2,1)S(1)}, u32[]{:S(2)}, u32[]{:S(2)}) collective-permute-start(bf16[8,16,1024]{2,1,0:T(8,128)(2,1)S(1)} %get-tuple-element.97.refs_0_.refs_4_), channel_id=1, source_target_pairs={{1,0},{2,1},{3,2},{0,3},{5,4},{6,5},{7,6},{4,7},{9,8},{10,9},{11,1... | collective-permute-start | bytes 786440 | tf_op jit(solution)/shard_map/ppermute | solution.py:31
  31.5 1.4 %gate_terms.1 = (f32[2,512,896]{2,1,0:T(8,128)S(1)}, bf16[512,896]{1,0:T(8,128)(2,1)S(1)}) custom-call(bf16[4,2,4,16,896]{4,3,2,1,0:T(8,128)(2,1)S(1)} %pad_maximum_fusion.mine_ref, bf16[4,2,4,16,896]{4,3,2,1,0:T(8,128)(2,1)S(1)} %collective-permute-done.6.other_ref), custom_call_target="tpu_custom_call" | custom-call | flops 7340032 | bytes 5505024 | tf_op jit(solution)/shard_map/gate_terms/pallas_call | solution.py:114
  32.9 2.8 %collective-permute-done.5.refs_3_.refs_7_ = bf16[8,16,1024]{2,1,0:T(8,128)(2,1)S(1)} collective-permute-done((bf16[8,16,1024]{2,1,0:T(8,128)(2,1)S(1)}, bf16[8,16,1024]{2,1,0:T(8,128)(2,1)S(1)}, u32[]{:S(2)}, u32[]{:S(2)}) %collective-permute-start.5) | collective-permute-done | bytes 262176 | tf_op jit(solution)/shard_map/ppermute | solution.py:31
  35.6 3.2 %collective-permute-done.4.refs_2_.refs_6_ = bf16[8,16,1024]{2,1,0:T(8,128)(2,1)S(1)} collective-permute-done((bf16[8,16,1024]{2,1,0:T(8,128)(2,1)S(1)}, bf16[8,16,1024]{2,1,0:T(8,128)(2,1)S(1)}, u32[]{:S(2)}, u32[]{:S(2)}) %collective-permute-start.4) | collective-permute-done | bytes 262176 | tf_op jit(solution)/shard_map/ppermute | solution.py:31
  38.8 4.2 %collective-permute-done.3.refs_1_.refs_5_ = bf16[8,16,1024]{2,1,0:T(8,128)(2,1)S(1)} collective-permute-done((bf16[8,16,1024]{2,1,0:T(8,128)(2,1)S(1)}, bf16[8,16,1024]{2,1,0:T(8,128)(2,1)S(1)}, u32[]{:S(2)}, u32[]{:S(2)}) %collective-permute-start.3) | collective-permute-done | bytes 262176 | tf_op jit(solution)/shard_map/ppermute | solution.py:31
  44.7 1.6 %collective-permute-done.7.refs_5_ = f32[256,896]{1,0:T(8,128)S(1)} collective-permute-done((f32[256,896]{1,0:T(8,128)S(1)}, f32[256,896]{1,0:T(8,128)S(1)}, u32[]{:S(2)}, u32[]{:S(2)}) %collective-permute-start.7) | collective-permute-done | bytes 917536 | tf_op jit(solution)/shard_map/ppermute | solution.py:35
  47.0 2.1 %collective-permute-start.8 = (bf16[4,16,896]{2,1,0:T(8,128)(2,1)S(1)}, bf16[4,16,896]{2,1,0:T(8,128)(2,1)S(1)}, u32[]{:S(2)}, u32[]{:S(2)}) collective-permute-start(bf16[4,16,896]{2,1,0:T(8,128)(2,1)S(1)} %get-tuple-element.65), channel_id=1, source_target_pairs={{192,0},{224,32},{0,64},{32,96},{64,128},{96,160},{128,192},{160,2... | collective-permute-start | bytes 344072 | tf_op jit(solution)/shard_map/ppermute | solution.py:27
  49.1 1.6 %collective-permute-start.9 = (bf16[4,16,896]{2,1,0:T(8,128)(2,1)S(1)}, bf16[4,16,896]{2,1,0:T(8,128)(2,1)S(1)}, u32[]{:S(2)}, u32[]{:S(2)}) collective-permute-start(bf16[4,16,896]{2,1,0:T(8,128)(2,1)S(1)} %get-tuple-element.66), channel_id=1, source_target_pairs={{128,0},{160,32},{192,64},{224,96},{0,128},{32,160},{64,192},{96,2... | collective-permute-start | bytes 344072 | tf_op jit(solution)/shard_map/ppermute | solution.py:27
  50.7 2.2 %collective-permute-start.10 = (bf16[4,16,896]{2,1,0:T(8,128)(2,1)S(1)}, bf16[4,16,896]{2,1,0:T(8,128)(2,1)S(1)}, u32[]{:S(2)}, u32[]{:S(2)}) collective-permute-start(bf16[4,16,896]{2,1,0:T(8,128)(2,1)S(1)} %get-tuple-element.67), channel_id=1, source_target_pairs={{64,0},{96,32},{128,64},{160,96},{192,128},{224,160},{0,192},{32,2... | collective-permute-start | bytes 344072 | tf_op jit(solution)/shard_map/ppermute | solution.py:27
  53.0 1.3 %collective-permute-start.20 = (bf16[8,16,1024]{2,1,0:T(8,128)(2,1)S(1)}, bf16[8,16,1024]{2,1,0:T(8,128)(2,1)S(1)}, u32[]{:S(2)}, u32[]{:S(2)}) collective-permute-start(bf16[8,16,1024]{2,1,0:T(8,128)(2,1)S(1)} %get-tuple-element.93.refs_0_), channel_id=1, source_target_pairs={{3,0},{0,1},{1,2},{2,3},{7,4},{4,5},{5,6},{6,7},{11,8},{8,9},{9,10... | collective-permute-start | bytes 786440 | tf_op jit(solution)/shard_map/ppermute | solution.py:31
  54.3 1.6 %collective-permute-start.19 = (bf16[8,16,1024]{2,1,0:T(8,128)(2,1)S(1)}, bf16[8,16,1024]{2,1,0:T(8,128)(2,1)S(1)}, u32[]{:S(2)}, u32[]{:S(2)}) collective-permute-start(bf16[8,16,1024]{2,1,0:T(8,128)(2,1)S(1)} %get-tuple-element.93.refs_0_), channel_id=1, source_target_pairs={{2,0},{3,1},{0,2},{1,3},{6,4},{7,5},{4,6},{5,7},{10,8},{11,9},{8,1... | collective-permute-start | bytes 786440 | tf_op jit(solution)/shard_map/ppermute | solution.py:31
  56.6 2.0 %collective-permute-start.14 = (bf16[4,16,896]{2,1,0:T(8,128)(2,1)S(1)}, bf16[4,16,896]{2,1,0:T(8,128)(2,1)S(1)}, u32[]{:S(2)}, u32[]{:S(2)}) collective-permute-start(bf16[4,16,896]{2,1,0:T(8,128)(2,1)S(1)} %add_convert_fusion.1.refs_0_), channel_id=1, source_target_pairs={{192,0},{224,32},{0,64},{32,96},{64,128},{96,160},{128,192},{160,2... | collective-permute-start | bytes 344072 | tf_op jit(solution)/shard_map/ppermute | solution.py:27
  58.6 2.8 %collective-permute-start.13 = (bf16[4,16,896]{2,1,0:T(8,128)(2,1)S(1)}, bf16[4,16,896]{2,1,0:T(8,128)(2,1)S(1)}, u32[]{:S(2)}, u32[]{:S(2)}) collective-permute-start(bf16[4,16,896]{2,1,0:T(8,128)(2,1)S(1)} %add_convert_fusion.1.refs_0_), channel_id=1, source_target_pairs={{128,0},{160,32},{192,64},{224,96},{0,128},{32,160},{64,192},{96,2... | collective-permute-start | bytes 344072 | tf_op jit(solution)/shard_map/ppermute | solution.py:27
  61.3 1.4 %collective-permute-start.12 = (bf16[4,16,896]{2,1,0:T(8,128)(2,1)S(1)}, bf16[4,16,896]{2,1,0:T(8,128)(2,1)S(1)}, u32[]{:S(2)}, u32[]{:S(2)}) collective-permute-start(bf16[4,16,896]{2,1,0:T(8,128)(2,1)S(1)} %add_convert_fusion.1.refs_0_), channel_id=1, source_target_pairs={{64,0},{96,32},{128,64},{160,96},{192,128},{224,160},{0,192},{32,2... | collective-permute-start | bytes 344072 | tf_op jit(solution)/shard_map/ppermute | solution.py:27
  63.6 2.6 %collective-permute-done.13.refs_2_ = bf16[4,16,896]{2,1,0:T(8,128)(2,1)S(1)} collective-permute-done((bf16[4,16,896]{2,1,0:T(8,128)(2,1)S(1)}, bf16[4,16,896]{2,1,0:T(8,128)(2,1)S(1)}, u32[]{:S(2)}, u32[]{:S(2)}) %collective-permute-start.13) | collective-permute-done | bytes 114720 | tf_op jit(solution)/shard_map/ppermute | solution.py:27
  67.7 2.4 %input_terms.1 = (bf16[2,512,896]{2,1,0:T(8,128)(2,1)S(1)}, f32[128,1024]{1,0:T(8,128)S(1)}, bf16[128,1024]{1,0:T(8,128)(2,1)S(1)}, bf16[128,1024]{1,0:T(8,128)(2,1)S(1)}, bf16[128,1024]{1,0:T(8,128)(2,1)S(1)}) custom-call(bf16[4,16,896]{2,1,0:T(8,128)(2,1)S(1)} %add_convert_fusion.1.refs_0_, bf16[4,16,896]{2,1,0:T(8,128)(2,1)S(1)} %collective-permute-done.12.refs_1_, ...), custom_call_target="tpu_custom_call" | custom-call | flops 1879048192 | bytes 3670016 | tf_op jit(solution)/shard_map/input_terms/pallas_call | solution.py:151
  71.3 1.3 %collective-permute-start.21 = (bf16[128,1024]{1,0:T(8,128)(2,1)S(1)}, bf16[128,1024]{1,0:T(8,128)(2,1)S(1)}, u32[]{:S(2)}, u32[]{:S(2)}) collective-permute-start(bf16[128,1024]{1,0:T(8,128)(2,1)S(1)} %get-tuple-element.83), channel_id=1, source_target_pairs={{3,0},{0,1},{1,2},{2,3},{7,4},{4,5},{5,6},{6,7},{11,8},{8,9},{9,10... | collective-permute-start | bytes 786440 | tf_op jit(solution)/shard_map/ppermute | solution.py:31
  72.6 1.6 %collective-permute-start.22 = (bf16[128,1024]{1,0:T(8,128)(2,1)S(1)}, bf16[128,1024]{1,0:T(8,128)(2,1)S(1)}, u32[]{:S(2)}, u32[]{:S(2)}) collective-permute-start(bf16[128,1024]{1,0:T(8,128)(2,1)S(1)} %get-tuple-element.84), channel_id=1, source_target_pairs={{2,0},{3,1},{0,2},{1,3},{6,4},{7,5},{4,6},{5,7},{10,8},{11,9},{8,1... | collective-permute-start | bytes 786440 | tf_op jit(solution)/shard_map/ppermute | solution.py:31
  74.3 1.5 %collective-permute-start.23 = (bf16[128,1024]{1,0:T(8,128)(2,1)S(1)}, bf16[128,1024]{1,0:T(8,128)(2,1)S(1)}, u32[]{:S(2)}, u32[]{:S(2)}) collective-permute-start(bf16[128,1024]{1,0:T(8,128)(2,1)S(1)} %get-tuple-element.85), channel_id=1, source_target_pairs={{1,0},{2,1},{3,2},{0,3},{5,4},{6,5},{7,6},{4,7},{9,8},{10,9},{11,1... | collective-permute-start | bytes 786440 | tf_op jit(solution)/shard_map/ppermute | solution.py:31
  75.8 4.7 %collective-permute-done.21 = bf16[128,1024]{1,0:T(8,128)(2,1)S(1)} collective-permute-done((bf16[128,1024]{1,0:T(8,128)(2,1)S(1)}, bf16[128,1024]{1,0:T(8,128)(2,1)S(1)}, u32[]{:S(2)}, u32[]{:S(2)}) %collective-permute-start.21) | collective-permute-done | bytes 262176 | tf_op jit(solution)/shard_map/ppermute | solution.py:31
  80.5 2.9 %collective-permute-done.22 = bf16[128,1024]{1,0:T(8,128)(2,1)S(1)} collective-permute-done((bf16[128,1024]{1,0:T(8,128)(2,1)S(1)}, bf16[128,1024]{1,0:T(8,128)(2,1)S(1)}, u32[]{:S(2)}, u32[]{:S(2)}) %collective-permute-start.22) | collective-permute-done | bytes 262176 | tf_op jit(solution)/shard_map/ppermute | solution.py:31
  83.4 4.5 %collective-permute-done.23 = bf16[128,1024]{1,0:T(8,128)(2,1)S(1)} collective-permute-done((bf16[128,1024]{1,0:T(8,128)(2,1)S(1)}, bf16[128,1024]{1,0:T(8,128)(2,1)S(1)}, u32[]{:S(2)}, u32[]{:S(2)}) %collective-permute-start.23) | collective-permute-done | bytes 262176 | tf_op jit(solution)/shard_map/ppermute | solution.py:31
  88.7 5.9 %all-to-all-start.1 = ((bf16[8,16,1024]{2,1,0:T(8,128)(2,1)}), bf16[8,16,1024]{2,1,0:T(8,128)(2,1)S(1)}, u32[]{:S(2)}, u32[]{:S(2)}) async-start(bf16[8,16,1024]{2,1,0:T(8,128)(2,1)} %bitcast.12), calls=%async_computation.1 | async-start | bytes 524288 | tf_op jit(solution)/shard_map/all_to_all | solution.py:39
  94.5 1.5 %copy-done.4 = bf16[2,512,896]{2,1,0:T(8,128)(2,1)S(1)} copy-done((bf16[2,512,896]{2,1,0:T(8,128)(2,1)S(1)}, bf16[2,512,896]{2,1,0:T(8,128)(2,1)}, u32[]{:S(2)}) %copy-start.4) | copy-done | bytes 1835032
  96.0 5.0 %weight_grads.1 = (bf16[1024,896]{1,0:T(8,128)(2,1)}, bf16[1024,896]{1,0:T(8,128)(2,1)}, bf16[1024,896]{1,0:T(8,128)(2,1)}) custom-call(bf16[8,16,1024]{2,1,0:T(8,128)(2,1)S(1)} %get-tuple-element.93.refs_0_, bf16[8,16,1024]{2,1,0:T(8,128)(2,1)S(1)} %collective-permute-done.11.refs_1_, bf16[8,16,1024]{2,1,0:T(8,128)(2,1)S(1)} %collective-permute-done.19.refs_2_, ...), custom_call_target="tpu_custom_call" | custom-call | flops 2818572288 | bytes 5505024 | tf_op jit(solution)/shard_map/weight_grads/pallas_call | solution.py:196
  101.0 3.6 %all-to-all-done.1 = bf16[8,16,1024]{2,1,0:T(8,128)(2,1)S(1)} async-done(((bf16[8,16,1024]{2,1,0:T(8,128)(2,1)}), bf16[8,16,1024]{2,1,0:T(8,128)(2,1)S(1)}, u32[]{:S(2)}, u32[]{:S(2)}) %all-to-all-start.1) | async-done | bytes 262176 | tf_op jit(solution)/shard_map/all_to_all | solution.py:39
  (57 shorter events, 12.9 us)
Async XLA Ops:
  0.6 10.5 %copy-start.5 = (bf16[4,16,896]{2,1,0:T(8,128)(2,1)S(1)}, bf16[4,16,896]{2,1,0:T(8,128)(2,1)}, u32[]{:S(2)}) copy-start(bf16[4,16,896]{2,1,0:T(8,128)(2,1)} %param.9) | copy-start | bytes 344068
  0.6 10.6 %copy-start.6 = (bf16[4,16,896]{2,1,0:T(8,128)(2,1)S(1)}, bf16[4,16,896]{2,1,0:T(8,128)(2,1)}, u32[]{:S(2)}) copy-start(bf16[4,16,896]{2,1,0:T(8,128)(2,1)} %param.10) | copy-start | bytes 344068
  2.5 23.6 %all-to-all-start = ((bf16[8,2,4,4,1024]{4,3,2,1,0:T(4,128)(2,1)}), bf16[8,2,4,4,1024]{4,3,2,1,0:T(4,128)(2,1)S(1)}, u32[]{:S(2)}, u32[]{:S(2)}) async-start(bf16[8,2,4,4,1024]{4,3,2,1,0:T(4,128)(2,1)} %broadcast_in_dim.3), calls=%async_computation | async-start | bytes 1048576 | tf_op jit(solution)/shard_map/all_to_all | solution.py:39
  11.5 10.2 %collective-permute-start.1 = (bf16[2,4,16,896]{3,2,1,0:T(8,128)(2,1)S(1)}, bf16[2,4,16,896]{3,2,1,0:T(8,128)(2,1)S(1)}, u32[]{:S(2)}, u32[]{:S(2)}) collective-permute-start(bf16[2,4,16,896]{3,2,1,0:T(8,128)(2,1)S(1)} %get-tuple-element.109), channel_id=1, source_target_pairs={{128,0},{160,32},{192,64},{224,96},{0,128},{32,160},{64,192},{96,2... | collective-permute-start | bytes 688136 | tf_op jit(solution)/shard_map/ppermute | solution.py:27
  15.3 10.1 %collective-permute-start = (bf16[2,4,16,896]{3,2,1,0:T(8,128)(2,1)S(1)}, bf16[2,4,16,896]{3,2,1,0:T(8,128)(2,1)S(1)}, u32[]{:S(2)}, u32[]{:S(2)}) collective-permute-start(bf16[2,4,16,896]{3,2,1,0:T(8,128)(2,1)S(1)} %get-tuple-element.109), channel_id=1, source_target_pairs={{64,0},{96,32},{128,64},{160,96},{192,128},{224,160},{0,192},{32,2... | collective-permute-start | bytes 688136 | tf_op jit(solution)/shard_map/ppermute | solution.py:27
  15.8 10.2 %collective-permute-start.2 = (bf16[2,4,16,896]{3,2,1,0:T(8,128)(2,1)S(1)}, bf16[2,4,16,896]{3,2,1,0:T(8,128)(2,1)S(1)}, u32[]{:S(2)}, u32[]{:S(2)}) collective-permute-start(bf16[2,4,16,896]{3,2,1,0:T(8,128)(2,1)S(1)} %get-tuple-element.109), channel_id=1, source_target_pairs={{192,0},{224,32},{0,64},{32,96},{64,128},{96,160},{128,192},{160,2... | collective-permute-start | bytes 688136 | tf_op jit(solution)/shard_map/ppermute | solution.py:27
  26.3 16.7 %copy-start = (bf16[1024,896]{1,0:T(8,128)(2,1)S(1)}, bf16[1024,896]{1,0:T(8,128)(2,1)}, u32[]{:S(2)}) copy-start(bf16[1024,896]{1,0:T(8,128)(2,1)} %refs_4_.3) | copy-start | bytes 5505028
  26.3 5.2 %collective-permute-start.6 = (bf16[4,2,4,16,896]{4,3,2,1,0:T(8,128)(2,1)S(1)}, bf16[4,2,4,16,896]{4,3,2,1,0:T(8,128)(2,1)S(1)}, u32[]{:S(2)}, u32[]{:S(2)}) collective-permute-start(bf16[4,2,4,16,896]{4,3,2,1,0:T(8,128)(2,1)S(1)} %pad_maximum_fusion.mine_ref), channel_id=1, source_target_pairs={{0,32},{32,0},{64,96},{96,64},{128,160},{160,128},{192,224},{224,1... | collective-permute-start | bytes 2752520 | tf_op jit(solution)/shard_map/ppermute | solution.py:35
  26.5 9.2 %collective-permute-start.5 = (bf16[8,16,1024]{2,1,0:T(8,128)(2,1)S(1)}, bf16[8,16,1024]{2,1,0:T(8,128)(2,1)S(1)}, u32[]{:S(2)}, u32[]{:S(2)}) collective-permute-start(bf16[8,16,1024]{2,1,0:T(8,128)(2,1)S(1)} %get-tuple-element.97.refs_0_.refs_4_), channel_id=1, source_target_pairs={{3,0},{0,1},{1,2},{2,3},{7,4},{4,5},{5,6},{6,7},{11,8},{8,9},{9,10... | collective-permute-start | bytes 786440 | tf_op jit(solution)/shard_map/ppermute | solution.py:31
  28.1 10.7 %collective-permute-start.4 = (bf16[8,16,1024]{2,1,0:T(8,128)(2,1)S(1)}, bf16[8,16,1024]{2,1,0:T(8,128)(2,1)S(1)}, u32[]{:S(2)}, u32[]{:S(2)}) collective-permute-start(bf16[8,16,1024]{2,1,0:T(8,128)(2,1)S(1)} %get-tuple-element.97.refs_0_.refs_4_), channel_id=1, source_target_pairs={{2,0},{3,1},{0,2},{1,3},{6,4},{7,5},{4,6},{5,7},{10,8},{11,9},{8,1... | collective-permute-start | bytes 786440 | tf_op jit(solution)/shard_map/ppermute | solution.py:31
  29.1 13.9 %collective-permute-start.3 = (bf16[8,16,1024]{2,1,0:T(8,128)(2,1)S(1)}, bf16[8,16,1024]{2,1,0:T(8,128)(2,1)S(1)}, u32[]{:S(2)}, u32[]{:S(2)}) collective-permute-start(bf16[8,16,1024]{2,1,0:T(8,128)(2,1)S(1)} %get-tuple-element.97.refs_0_.refs_4_), channel_id=1, source_target_pairs={{1,0},{2,1},{3,2},{0,3},{5,4},{6,5},{7,6},{4,7},{9,8},{10,9},{11,1... | collective-permute-start | bytes 786440 | tf_op jit(solution)/shard_map/ppermute | solution.py:31
  43.7 24.0 %copy-start.1 = (bf16[1024,896]{1,0:T(8,128)(2,1)S(1)}, bf16[1024,896]{1,0:T(8,128)(2,1)}, u32[]{:S(2)}) copy-start(bf16[1024,896]{1,0:T(8,128)(2,1)} %refs_9_.1) | copy-start | bytes 5505028
  43.7 24.0 %copy-start.2 = (bf16[1024,896]{1,0:T(8,128)(2,1)S(1)}, bf16[1024,896]{1,0:T(8,128)(2,1)}, u32[]{:S(2)}) copy-start(bf16[1024,896]{1,0:T(8,128)(2,1)} %refs_10_.1) | copy-start | bytes 5505028
  43.7 2.6 %collective-permute-start.7 = (f32[256,896]{1,0:T(8,128)S(1)}, f32[256,896]{1,0:T(8,128)S(1)}, u32[]{:S(2)}, u32[]{:S(2)}) collective-permute-start(f32[256,896]{1,0:T(8,128)S(1)} %half_1.1), channel_id=1, source_target_pairs={{0,32},{32,0},{64,96},{96,64},{128,160},{160,128},{192,224},{224,1... | collective-permute-start | bytes 2752520 | tf_op jit(solution)/shard_map/ppermute | solution.py:35
  43.8 10.4 %collective-permute-start.11 = (bf16[8,16,1024]{2,1,0:T(8,128)(2,1)S(1)}, bf16[8,16,1024]{2,1,0:T(8,128)(2,1)S(1)}, u32[]{:S(2)}, u32[]{:S(2)}) collective-permute-start(bf16[8,16,1024]{2,1,0:T(8,128)(2,1)S(1)} %get-tuple-element.93.refs_0_), channel_id=1, source_target_pairs={{1,0},{2,1},{3,2},{0,3},{5,4},{6,5},{7,6},{4,7},{9,8},{10,9},{11,1... | collective-permute-start | bytes 786440 | tf_op jit(solution)/shard_map/ppermute | solution.py:31
  47.0 8.8 %collective-permute-start.8 = (bf16[4,16,896]{2,1,0:T(8,128)(2,1)S(1)}, bf16[4,16,896]{2,1,0:T(8,128)(2,1)S(1)}, u32[]{:S(2)}, u32[]{:S(2)}) collective-permute-start(bf16[4,16,896]{2,1,0:T(8,128)(2,1)S(1)} %get-tuple-element.65), channel_id=1, source_target_pairs={{192,0},{224,32},{0,64},{32,96},{64,128},{96,160},{128,192},{160,2... | collective-permute-start | bytes 344072 | tf_op jit(solution)/shard_map/ppermute | solution.py:27
  49.1 7.2 %collective-permute-start.9 = (bf16[4,16,896]{2,1,0:T(8,128)(2,1)S(1)}, bf16[4,16,896]{2,1,0:T(8,128)(2,1)S(1)}, u32[]{:S(2)}, u32[]{:S(2)}) collective-permute-start(bf16[4,16,896]{2,1,0:T(8,128)(2,1)S(1)} %get-tuple-element.66), channel_id=1, source_target_pairs={{128,0},{160,32},{192,64},{224,96},{0,128},{32,160},{64,192},{96,2... | collective-permute-start | bytes 344072 | tf_op jit(solution)/shard_map/ppermute | solution.py:27
  50.7 5.8 %collective-permute-start.10 = (bf16[4,16,896]{2,1,0:T(8,128)(2,1)S(1)}, bf16[4,16,896]{2,1,0:T(8,128)(2,1)S(1)}, u32[]{:S(2)}, u32[]{:S(2)}) collective-permute-start(bf16[4,16,896]{2,1,0:T(8,128)(2,1)S(1)} %get-tuple-element.67), channel_id=1, source_target_pairs={{64,0},{96,32},{128,64},{160,96},{192,128},{224,160},{0,192},{32,2... | collective-permute-start | bytes 344072 | tf_op jit(solution)/shard_map/ppermute | solution.py:27
  53.0 9.8 %collective-permute-start.20 = (bf16[8,16,1024]{2,1,0:T(8,128)(2,1)S(1)}, bf16[8,16,1024]{2,1,0:T(8,128)(2,1)S(1)}, u32[]{:S(2)}, u32[]{:S(2)}) collective-permute-start(bf16[8,16,1024]{2,1,0:T(8,128)(2,1)S(1)} %get-tuple-element.93.refs_0_), channel_id=1, source_target_pairs={{3,0},{0,1},{1,2},{2,3},{7,4},{4,5},{5,6},{6,7},{11,8},{8,9},{9,10... | collective-permute-start | bytes 786440 | tf_op jit(solution)/shard_map/ppermute | solution.py:31
  54.3 12.4 %collective-permute-start.19 = (bf16[8,16,1024]{2,1,0:T(8,128)(2,1)S(1)}, bf16[8,16,1024]{2,1,0:T(8,128)(2,1)S(1)}, u32[]{:S(2)}, u32[]{:S(2)}) collective-permute-start(bf16[8,16,1024]{2,1,0:T(8,128)(2,1)S(1)} %get-tuple-element.93.refs_0_), channel_id=1, source_target_pairs={{2,0},{3,1},{0,2},{1,3},{6,4},{7,5},{4,6},{5,7},{10,8},{11,9},{8,1... | collective-permute-start | bytes 786440 | tf_op jit(solution)/shard_map/ppermute | solution.py:31
  56.6 7.0 %collective-permute-start.14 = (bf16[4,16,896]{2,1,0:T(8,128)(2,1)S(1)}, bf16[4,16,896]{2,1,0:T(8,128)(2,1)S(1)}, u32[]{:S(2)}, u32[]{:S(2)}) collective-permute-start(bf16[4,16,896]{2,1,0:T(8,128)(2,1)S(1)} %add_convert_fusion.1.refs_0_), channel_id=1, source_target_pairs={{192,0},{224,32},{0,64},{32,96},{64,128},{96,160},{128,192},{160,2... | collective-permute-start | bytes 344072 | tf_op jit(solution)/shard_map/ppermute | solution.py:27
  58.6 7.6 %collective-permute-start.13 = (bf16[4,16,896]{2,1,0:T(8,128)(2,1)S(1)}, bf16[4,16,896]{2,1,0:T(8,128)(2,1)S(1)}, u32[]{:S(2)}, u32[]{:S(2)}) collective-permute-start(bf16[4,16,896]{2,1,0:T(8,128)(2,1)S(1)} %add_convert_fusion.1.refs_0_), channel_id=1, source_target_pairs={{128,0},{160,32},{192,64},{224,96},{0,128},{32,160},{64,192},{96,2... | collective-permute-start | bytes 344072 | tf_op jit(solution)/shard_map/ppermute | solution.py:27
  61.3 4.9 %collective-permute-start.12 = (bf16[4,16,896]{2,1,0:T(8,128)(2,1)S(1)}, bf16[4,16,896]{2,1,0:T(8,128)(2,1)S(1)}, u32[]{:S(2)}, u32[]{:S(2)}) collective-permute-start(bf16[4,16,896]{2,1,0:T(8,128)(2,1)S(1)} %add_convert_fusion.1.refs_0_), channel_id=1, source_target_pairs={{64,0},{96,32},{128,64},{160,96},{192,128},{224,160},{0,192},{32,2... | collective-permute-start | bytes 344072 | tf_op jit(solution)/shard_map/ppermute | solution.py:27
  62.8 4.0 %collective-permute-start.15 = (bf16[4,16,896]{2,1,0:T(8,128)(2,1)S(1)}, bf16[4,16,896]{2,1,0:T(8,128)(2,1)S(1)}, u32[]{:S(2)}, u32[]{:S(2)}) collective-permute-start(bf16[4,16,896]{2,1,0:T(8,128)(2,1)S(1)} %add_convert_fusion.1.refs_0_), channel_id=1, source_target_pairs={{0,32},{32,0},{64,96},{96,64},{128,160},{160,128},{192,224},{224,1... | collective-permute-start | bytes 344072 | tf_op jit(solution)/shard_map/ppermute | solution.py:35
  63.6 3.1 %collective-permute-start.18 = (bf16[4,16,896]{2,1,0:T(8,128)(2,1)S(1)}, bf16[4,16,896]{2,1,0:T(8,128)(2,1)S(1)}, u32[]{:S(2)}, u32[]{:S(2)}) collective-permute-start(bf16[4,16,896]{2,1,0:T(8,128)(2,1)S(1)} %collective-permute-done.14.refs_3_), channel_id=1, source_target_pairs={{0,32},{32,0},{64,96},{96,64},{128,160},{160,128},{192,224},{224,1... | collective-permute-start | bytes 344072 | tf_op jit(solution)/shard_map/ppermute | solution.py:35
  66.2 1.3 %collective-permute-start.17 = (bf16[4,16,896]{2,1,0:T(8,128)(2,1)S(1)}, bf16[4,16,896]{2,1,0:T(8,128)(2,1)S(1)}, u32[]{:S(2)}, u32[]{:S(2)}) collective-permute-start(bf16[4,16,896]{2,1,0:T(8,128)(2,1)S(1)} %collective-permute-done.13.refs_2_), channel_id=1, source_target_pairs={{0,32},{32,0},{64,96},{96,64},{128,160},{160,128},{192,224},{224,1... | collective-permute-start | bytes 344072 | tf_op jit(solution)/shard_map/ppermute | solution.py:35
  66.2 1.5 %collective-permute-start.16 = (bf16[4,16,896]{2,1,0:T(8,128)(2,1)S(1)}, bf16[4,16,896]{2,1,0:T(8,128)(2,1)S(1)}, u32[]{:S(2)}, u32[]{:S(2)}) collective-permute-start(bf16[4,16,896]{2,1,0:T(8,128)(2,1)S(1)} %collective-permute-done.12.refs_1_), channel_id=1, source_target_pairs={{0,32},{32,0},{64,96},{96,64},{128,160},{160,128},{192,224},{224,1... | collective-permute-start | bytes 344072 | tf_op jit(solution)/shard_map/ppermute | solution.py:35
  71.3 9.1 %collective-permute-start.21 = (bf16[128,1024]{1,0:T(8,128)(2,1)S(1)}, bf16[128,1024]{1,0:T(8,128)(2,1)S(1)}, u32[]{:S(2)}, u32[]{:S(2)}) collective-permute-start(bf16[128,1024]{1,0:T(8,128)(2,1)S(1)} %get-tuple-element.83), channel_id=1, source_target_pairs={{3,0},{0,1},{1,2},{2,3},{7,4},{4,5},{5,6},{6,7},{11,8},{8,9},{9,10... | collective-permute-start | bytes 786440 | tf_op jit(solution)/shard_map/ppermute | solution.py:31
  72.6 10.7 %collective-permute-start.22 = (bf16[128,1024]{1,0:T(8,128)(2,1)S(1)}, bf16[128,1024]{1,0:T(8,128)(2,1)S(1)}, u32[]{:S(2)}, u32[]{:S(2)}) collective-permute-start(bf16[128,1024]{1,0:T(8,128)(2,1)S(1)} %get-tuple-element.84), channel_id=1, source_target_pairs={{2,0},{3,1},{0,2},{1,3},{6,4},{7,5},{4,6},{5,7},{10,8},{11,9},{8,1... | collective-permute-start | bytes 786440 | tf_op jit(solution)/shard_map/ppermute | solution.py:31
  74.3 13.6 %collective-permute-start.23 = (bf16[128,1024]{1,0:T(8,128)(2,1)S(1)}, bf16[128,1024]{1,0:T(8,128)(2,1)S(1)}, u32[]{:S(2)}, u32[]{:S(2)}) collective-permute-start(bf16[128,1024]{1,0:T(8,128)(2,1)S(1)} %get-tuple-element.85), channel_id=1, source_target_pairs={{1,0},{2,1},{3,2},{0,3},{5,4},{6,5},{7,6},{4,7},{9,8},{10,9},{11,1... | collective-permute-start | bytes 786440 | tf_op jit(solution)/shard_map/ppermute | solution.py:31
  88.7 15.9 %all-to-all-start.1 = ((bf16[8,16,1024]{2,1,0:T(8,128)(2,1)}), bf16[8,16,1024]{2,1,0:T(8,128)(2,1)S(1)}, u32[]{:S(2)}, u32[]{:S(2)}) async-start(bf16[8,16,1024]{2,1,0:T(8,128)(2,1)} %bitcast.12), calls=%async_computation.1 | async-start | bytes 524288 | tf_op jit(solution)/shard_map/all_to_all | solution.py:39
  94.5 1.5 %copy-start.4 = (bf16[2,512,896]{2,1,0:T(8,128)(2,1)S(1)}, bf16[2,512,896]{2,1,0:T(8,128)(2,1)}, u32[]{:S(2)}) copy-start(bf16[2,512,896]{2,1,0:T(8,128)(2,1)} %copy-done.3) | copy-start | bytes 5505028
  (1 other events, 1.2 us)

commit v4 on v3

--- a/solution.py
+++ b/solution.py
@@ -229,14 +229,13 @@
     dhid, *blocks = half_dot(0, grad_y, down_weight, (theirs,))
     blocks = [from_x(blocks[j - 1], -j) for j in range(1, X)]
     in_y = [in_z] + [from_y(in_z, j) for j in range(1, Y)]
-    blocks, in_y[1] = lax.optimization_barrier((blocks, in_y[1]))
     for block in blocks:
         dhid = dhid + block.astype(F32)
 
     d_own = dhid.astype(BF)
     d_x = [d_own] + [from_x(d_own, j) for j in range(1, X)]
+    d_x[1], in_y = lax.optimization_barrier((d_x[1], in_y))
     d_other = [swap_core(d) for d in d_x]
-    d_other, in_y = lax.optimization_barrier((d_other, in_y))
 
     rows, own, *sent = input_terms(d_x + d_other, factors, gate_weight, up_weight)
     sent, hidden = lax.optimization_barrier((sent, hidden))

time: 106 us -> 107 us (level)
  waiting for transfers between devices: 41.1 us -> 46.2 us
  starting transfers between devices: 46.2 us -> 42.8 us
    ppermute x9, waiting for transfers between devices: 22.2 us -> 30.2 us  [from_y(): lax.ppermute(block, 'tensor', [(t // Y * Y + (t % Y + step) % Y, t) for t...]
    ppermute x9, waiting for transfers between devices: 12.8 us -> 8.75 us  [from_x(): lax.ppermute(block, 'dp', [((d // C + step) % X * C + d % C, d) for d in...]
    ppermute x9, starting transfers between devices: 18 us -> 14.5 us  [from_x(): lax.ppermute(block, 'dp', [((d // C + step) % X * C + d % C, d) for d in...]
    ppermute x6, waiting for transfers between devices: 2.56 us -> 3.68 us  [swap_core(): return lax.ppermute(block, 'dp', CORE_SWAP)]
  transfers between devices with their start and end apart: 26 -> 26, of which waited for: 17 -> 18; matrix products, arithmetic and copies ran while one was open for 1% -> 1% of each run, Pallas kernels for 7% -> 6%
where the time goes in v4:
time: 107 us
  waiting for transfers between devices  46.2 us (43%)
  starting transfers between devices  42.8 us (40%)
  Pallas kernels  10.2 us (10%)
  local copies, waits for them, and re-layouts  4.79 us (4%)
  other arithmetic  2.1 us (2%)
    ppermute x9, waiting for transfers between devices, from_y(): lax.ppermute(block, 'tensor', [(t // Y * Y + (t % Y + step) % Y, t) for t...  30.2 us
    ppermute x9, starting transfers between devices, from_x(): lax.ppermute(block, 'dp', [((d // C + step) % X * C + d % C, d) for d in...  14.5 us
    ppermute x9, starting transfers between devices, from_y(): lax.ppermute(block, 'tensor', [(t // Y * Y + (t % Y + step) % Y, t) for t...  13.8 us
    all_to_all x2, starting transfers between devices, exchange_z(): lax.all_to_all(blocks, ('dp', 'tensor'), 0, 0, axis_index_groups=Z_GROUPS)  13.7 us
    ppermute x9, waiting for transfers between devices, from_x(): lax.ppermute(block, 'dp', [((d // C + step) % X * C + d % C, d) for d in...  8.75 us
    pallas_call x1, Pallas kernels, weight_grads(): pl.pallas_call(weight_kernel, out_shape=[jax.ShapeDtypeStruct((width, col...  4.98 us
    ppermute x6, waiting for transfers between devices, swap_core(): return lax.ppermute(block, 'dp', CORE_SWAP)  3.68 us
    all_to_all x2, waiting for transfers between devices, exchange_z(): lax.all_to_all(blocks, ('dp', 'tensor'), 0, 0, axis_index_groups=Z_GROUPS)  3.59 us
  transfers between devices with their start and end apart: 26, of which 18 were waited for; matrix products, arithmetic and copies ran while one was open for 1% of the time, Pallas kernels for 6%

profile of v4, /device:TPU:40, one launch (start us, length us, event | category | flops | bytes accessed | tf_op | source)
XLA Modules:
  0.0 107.0 jit_solution(2093701862336050017)
XLA Ops:
  2.5 8.6 %all-to-all-start = ((bf16[8,2,4,4,1024]{4,3,2,1,0:T(4,128)(2,1)}), bf16[8,2,4,4,1024]{4,3,2,1,0:T(4,128)(2,1)S(1)}, u32[]{:S(2)}, u32[]{:S(2)}) async-start(bf16[8,2,4,4,1024]{4,3,2,1,0:T(4,128)(2,1)} %broadcast_in_dim.3), calls=%async_computation | async-start | bytes 1048576 | tf_op jit(solution)/shard_map/all_to_all | solution.py:39
  11.5 3.8 %collective-permute-start.1 = (bf16[2,4,16,896]{3,2,1,0:T(8,128)(2,1)S(1)}, bf16[2,4,16,896]{3,2,1,0:T(8,128)(2,1)S(1)}, u32[]{:S(2)}, u32[]{:S(2)}) collective-permute-start(bf16[2,4,16,896]{3,2,1,0:T(8,128)(2,1)S(1)} %get-tuple-element.95), channel_id=1, source_target_pairs={{128,0},{160,32},{192,64},{224,96},{0,128},{32,160},{64,192},{96,2... | collective-permute-start | bytes 688136 | tf_op jit(solution)/shard_map/ppermute | solution.py:27
  15.8 1.6 %collective-permute-start.2 = (bf16[2,4,16,896]{3,2,1,0:T(8,128)(2,1)S(1)}, bf16[2,4,16,896]{3,2,1,0:T(8,128)(2,1)S(1)}, u32[]{:S(2)}, u32[]{:S(2)}) collective-permute-start(bf16[2,4,16,896]{3,2,1,0:T(8,128)(2,1)S(1)} %get-tuple-element.95), channel_id=1, source_target_pairs={{192,0},{224,32},{0,64},{32,96},{64,128},{96,160},{128,192},{160,2... | collective-permute-start | bytes 688136 | tf_op jit(solution)/shard_map/ppermute | solution.py:27
  17.3 4.4 %collective-permute-done.1 = bf16[2,4,16,896]{3,2,1,0:T(8,128)(2,1)S(1)} collective-permute-done((bf16[2,4,16,896]{3,2,1,0:T(8,128)(2,1)S(1)}, bf16[2,4,16,896]{3,2,1,0:T(8,128)(2,1)S(1)}, u32[]{:S(2)}, u32[]{:S(2)}) %collective-permute-start.1) | collective-permute-done | bytes 229408 | tf_op jit(solution)/shard_map/ppermute | solution.py:27
  21.7 3.7 %collective-permute-done = bf16[2,4,16,896]{3,2,1,0:T(8,128)(2,1)S(1)} collective-permute-done((bf16[2,4,16,896]{3,2,1,0:T(8,128)(2,1)S(1)}, bf16[2,4,16,896]{3,2,1,0:T(8,128)(2,1)S(1)}, u32[]{:S(2)}, u32[]{:S(2)}) %collective-permute-start) | collective-permute-done | bytes 229408 | tf_op jit(solution)/shard_map/ppermute | solution.py:27
  26.5 1.7 %collective-permute-start.5 = (bf16[8,16,1024]{2,1,0:T(8,128)(2,1)S(1)}, bf16[8,16,1024]{2,1,0:T(8,128)(2,1)S(1)}, u32[]{:S(2)}, u32[]{:S(2)}) collective-permute-start(bf16[8,16,1024]{2,1,0:T(8,128)(2,1)S(1)} %get-tuple-element.83.refs_0_.refs_4_), channel_id=1, source_target_pairs={{3,0},{0,1},{1,2},{2,3},{7,4},{4,5},{5,6},{6,7},{11,8},{8,9},{9,10... | collective-permute-start | bytes 786440 | tf_op jit(solution)/shard_map/ppermute | solution.py:31
  29.1 2.4 %collective-permute-start.3 = (bf16[8,16,1024]{2,1,0:T(8,128)(2,1)S(1)}, bf16[8,16,1024]{2,1,0:T(8,128)(2,1)S(1)}, u32[]{:S(2)}, u32[]{:S(2)}) collective-permute-start(bf16[8,16,1024]{2,1,0:T(8,128)(2,1)S(1)} %get-tuple-element.83.refs_0_.refs_4_), channel_id=1, source_target_pairs={{1,0},{2,1},{3,2},{0,3},{5,4},{6,5},{7,6},{4,7},{9,8},{10,9},{11,1... | collective-permute-start | bytes 786440 | tf_op jit(solution)/shard_map/ppermute | solution.py:31
  31.5 1.4 %gate_terms.1 = (f32[2,512,896]{2,1,0:T(8,128)S(1)}, bf16[512,896]{1,0:T(8,128)(2,1)S(1)}) custom-call(bf16[4,2,4,16,896]{4,3,2,1,0:T(8,128)(2,1)S(1)} %pad_maximum_fusion.mine_ref, bf16[4,2,4,16,896]{4,3,2,1,0:T(8,128)(2,1)S(1)} %collective-permute-done.6.other_ref), custom_call_target="tpu_custom_call" | custom-call | flops 7340032 | bytes 5505024 | tf_op jit(solution)/shard_map/gate_terms/pallas_call | solution.py:114
  32.9 2.8 %collective-permute-done.5.refs_3_.refs_7_ = bf16[8,16,1024]{2,1,0:T(8,128)(2,1)S(1)} collective-permute-done((bf16[8,16,1024]{2,1,0:T(8,128)(2,1)S(1)}, bf16[8,16,1024]{2,1,0:T(8,128)(2,1)S(1)}, u32[]{:S(2)}, u32[]{:S(2)}) %collective-permute-start.5) | collective-permute-done | bytes 262176 | tf_op jit(solution)/shard_map/ppermute | solution.py:31
  35.6 3.2 %collective-permute-done.4.refs_2_.refs_6_ = bf16[8,16,1024]{2,1,0:T(8,128)(2,1)S(1)} collective-permute-done((bf16[8,16,1024]{2,1,0:T(8,128)(2,1)S(1)}, bf16[8,16,1024]{2,1,0:T(8,128)(2,1)S(1)}, u32[]{:S(2)}, u32[]{:S(2)}) %collective-permute-start.4) | collective-permute-done | bytes 262176 | tf_op jit(solution)/shard_map/ppermute | solution.py:31
  38.8 4.2 %collective-permute-done.3.refs_1_.refs_5_ = bf16[8,16,1024]{2,1,0:T(8,128)(2,1)S(1)} collective-permute-done((bf16[8,16,1024]{2,1,0:T(8,128)(2,1)S(1)}, bf16[8,16,1024]{2,1,0:T(8,128)(2,1)S(1)}, u32[]{:S(2)}, u32[]{:S(2)}) %collective-permute-start.3) | collective-permute-done | bytes 262176 | tf_op jit(solution)/shard_map/ppermute | solution.py:31
  43.8 2.5 %collective-permute-done.7.refs_5_ = f32[256,896]{1,0:T(8,128)S(1)} collective-permute-done((f32[256,896]{1,0:T(8,128)S(1)}, f32[256,896]{1,0:T(8,128)S(1)}, u32[]{:S(2)}, u32[]{:S(2)}) %collective-permute-start.7) | collective-permute-done | bytes 917536 | tf_op jit(solution)/shard_map/ppermute | solution.py:35
  47.0 2.1 %collective-permute-start.8 = (bf16[4,16,896]{2,1,0:T(8,128)(2,1)S(1)}, bf16[4,16,896]{2,1,0:T(8,128)(2,1)S(1)}, u32[]{:S(2)}, u32[]{:S(2)}) collective-permute-start(bf16[4,16,896]{2,1,0:T(8,128)(2,1)S(1)} %get-tuple-element.58), channel_id=1, source_target_pairs={{192,0},{224,32},{0,64},{32,96},{64,128},{96,160},{128,192},{160,2... | collective-permute-start | bytes 344072 | tf_op jit(solution)/shard_map/ppermute | solution.py:27
  49.1 1.6 %collective-permute-start.9 = (bf16[4,16,896]{2,1,0:T(8,128)(2,1)S(1)}, bf16[4,16,896]{2,1,0:T(8,128)(2,1)S(1)}, u32[]{:S(2)}, u32[]{:S(2)}) collective-permute-start(bf16[4,16,896]{2,1,0:T(8,128)(2,1)S(1)} %get-tuple-element.59), channel_id=1, source_target_pairs={{128,0},{160,32},{192,64},{224,96},{0,128},{32,160},{64,192},{96,2... | collective-permute-start | bytes 344072 | tf_op jit(solution)/shard_map/ppermute | solution.py:27
  50.7 2.2 %collective-permute-start.10 = (bf16[4,16,896]{2,1,0:T(8,128)(2,1)S(1)}, bf16[4,16,896]{2,1,0:T(8,128)(2,1)S(1)}, u32[]{:S(2)}, u32[]{:S(2)}) collective-permute-start(bf16[4,16,896]{2,1,0:T(8,128)(2,1)S(1)} %get-tuple-element.60), channel_id=1, source_target_pairs={{64,0},{96,32},{128,64},{160,96},{192,128},{224,160},{0,192},{32,2... | collective-permute-start | bytes 344072 | tf_op jit(solution)/shard_map/ppermute | solution.py:27
  53.0 1.3 %collective-permute-start.14 = (bf16[8,16,1024]{2,1,0:T(8,128)(2,1)S(1)}, bf16[8,16,1024]{2,1,0:T(8,128)(2,1)S(1)}, u32[]{:S(2)}, u32[]{:S(2)}) collective-permute-start(bf16[8,16,1024]{2,1,0:T(8,128)(2,1)S(1)} %get-tuple-element.79.refs_0_), channel_id=1, source_target_pairs={{3,0},{0,1},{1,2},{2,3},{7,4},{4,5},{5,6},{6,7},{11,8},{8,9},{9,10... | collective-permute-start | bytes 786440 | tf_op jit(solution)/shard_map/ppermute | solution.py:31
  54.3 1.6 %collective-permute-start.13 = (bf16[8,16,1024]{2,1,0:T(8,128)(2,1)S(1)}, bf16[8,16,1024]{2,1,0:T(8,128)(2,1)S(1)}, u32[]{:S(2)}, u32[]{:S(2)}) collective-permute-start(bf16[8,16,1024]{2,1,0:T(8,128)(2,1)S(1)} %get-tuple-element.79.refs_0_), channel_id=1, source_target_pairs={{2,0},{3,1},{0,2},{1,3},{6,4},{7,5},{4,6},{5,7},{10,8},{11,9},{8,1... | collective-permute-start | bytes 786440 | tf_op jit(solution)/shard_map/ppermute | solution.py:31
  55.8 1.6 %collective-permute-start.12 = (bf16[8,16,1024]{2,1,0:T(8,128)(2,1)S(1)}, bf16[8,16,1024]{2,1,0:T(8,128)(2,1)S(1)}, u32[]{:S(2)}, u32[]{:S(2)}) collective-permute-start(bf16[8,16,1024]{2,1,0:T(8,128)(2,1)S(1)} %get-tuple-element.79.refs_0_), channel_id=1, source_target_pairs={{1,0},{2,1},{3,2},{0,3},{5,4},{6,5},{7,6},{4,7},{9,8},{10,9},{11,1... | collective-permute-start | bytes 786440 | tf_op jit(solution)/shard_map/ppermute | solution.py:31
  57.5 2.4 %collective-permute-start.11 = (bf16[4,16,896]{2,1,0:T(8,128)(2,1)S(1)}, bf16[4,16,896]{2,1,0:T(8,128)(2,1)S(1)}, u32[]{:S(2)}, u32[]{:S(2)}) collective-permute-start(bf16[4,16,896]{2,1,0:T(8,128)(2,1)S(1)} %add_convert_fusion.1.refs_0_), channel_id=1, source_target_pairs={{64,0},{96,32},{128,64},{160,96},{192,128},{224,160},{0,192},{32,2... | collective-permute-start | bytes 344072 | tf_op jit(solution)/shard_map/ppermute | solution.py:27
  59.9 2.3 %collective-permute-done.14.refs_3_ = bf16[8,16,1024]{2,1,0:T(8,128)(2,1)S(1)} collective-permute-done((bf16[8,16,1024]{2,1,0:T(8,128)(2,1)S(1)}, bf16[8,16,1024]{2,1,0:T(8,128)(2,1)S(1)}, u32[]{:S(2)}, u32[]{:S(2)}) %collective-permute-start.14) | collective-permute-done | bytes 262176 | tf_op jit(solution)/shard_map/ppermute | solution.py:31
  62.5 2.5 %collective-permute-done.13.refs_2_ = bf16[8,16,1024]{2,1,0:T(8,128)(2,1)S(1)} collective-permute-done((bf16[8,16,1024]{2,1,0:T(8,128)(2,1)S(1)}, bf16[8,16,1024]{2,1,0:T(8,128)(2,1)S(1)}, u32[]{:S(2)}, u32[]{:S(2)}) %collective-permute-start.13) | collective-permute-done | bytes 262176 | tf_op jit(solution)/shard_map/ppermute | solution.py:31
  65.0 3.4 %collective-permute-done.12.refs_1_ = bf16[8,16,1024]{2,1,0:T(8,128)(2,1)S(1)} collective-permute-done((bf16[8,16,1024]{2,1,0:T(8,128)(2,1)S(1)}, bf16[8,16,1024]{2,1,0:T(8,128)(2,1)S(1)}, u32[]{:S(2)}, u32[]{:S(2)}) %collective-permute-start.12) | collective-permute-done | bytes 262176 | tf_op jit(solution)/shard_map/ppermute | solution.py:31
  70.2 2.4 %input_terms.1 = (bf16[2,512,896]{2,1,0:T(8,128)(2,1)S(1)}, f32[128,1024]{1,0:T(8,128)S(1)}, bf16[128,1024]{1,0:T(8,128)(2,1)S(1)}, bf16[128,1024]{1,0:T(8,128)(2,1)S(1)}, bf16[128,1024]{1,0:T(8,128)(2,1)S(1)}) custom-call(bf16[4,16,896]{2,1,0:T(8,128)(2,1)S(1)} %add_convert_fusion.1.refs_0_, bf16[4,16,896]{2,1,0:T(8,128)(2,1)S(1)} %collective-permute-done.11.refs_1_, ...), custom_call_target="tpu_custom_call" | custom-call | flops 1879048192 | bytes 3670016 | tf_op jit(solution)/shard_map/input_terms/pallas_call | solution.py:151
  72.7 1.2 %copy-done.3 = bf16[2,512,896]{2,1,0:T(8,128)(2,1)} copy-done((bf16[2,512,896]{2,1,0:T(8,128)(2,1)}, bf16[2,512,896]{2,1,0:T(8,128)(2,1)S(1)}, u32[]{:S(2)}) %copy-start.3) | copy-done | bytes 1835032
  74.8 2.6 %collective-permute-start.22 = (bf16[128,1024]{1,0:T(8,128)(2,1)S(1)}, bf16[128,1024]{1,0:T(8,128)(2,1)S(1)}, u32[]{:S(2)}, u32[]{:S(2)}) collective-permute-start(bf16[128,1024]{1,0:T(8,128)(2,1)S(1)} %get-tuple-element.70), channel_id=1, source_target_pairs={{2,0},{3,1},{0,2},{1,3},{6,4},{7,5},{4,6},{5,7},{10,8},{11,9},{8,1... | collective-permute-start | bytes 786440 | tf_op jit(solution)/shard_map/ppermute | solution.py:31
  78.3 4.7 %collective-permute-done.21 = bf16[128,1024]{1,0:T(8,128)(2,1)S(1)} collective-permute-done((bf16[128,1024]{1,0:T(8,128)(2,1)S(1)}, bf16[128,1024]{1,0:T(8,128)(2,1)S(1)}, u32[]{:S(2)}, u32[]{:S(2)}) %collective-permute-start.21) | collective-permute-done | bytes 262176 | tf_op jit(solution)/shard_map/ppermute | solution.py:31
  83.1 2.4 %collective-permute-done.22 = bf16[128,1024]{1,0:T(8,128)(2,1)S(1)} collective-permute-done((bf16[128,1024]{1,0:T(8,128)(2,1)S(1)}, bf16[128,1024]{1,0:T(8,128)(2,1)S(1)}, u32[]{:S(2)}, u32[]{:S(2)}) %collective-permute-start.22) | collective-permute-done | bytes 262176 | tf_op jit(solution)/shard_map/ppermute | solution.py:31
  85.5 4.7 %collective-permute-done.23 = bf16[128,1024]{1,0:T(8,128)(2,1)S(1)} collective-permute-done((bf16[128,1024]{1,0:T(8,128)(2,1)S(1)}, bf16[128,1024]{1,0:T(8,128)(2,1)S(1)}, u32[]{:S(2)}, u32[]{:S(2)}) %collective-permute-start.23) | collective-permute-done | bytes 262176 | tf_op jit(solution)/shard_map/ppermute | solution.py:31
  91.0 5.2 %all-to-all-start.1 = ((bf16[8,16,1024]{2,1,0:T(8,128)(2,1)}), bf16[8,16,1024]{2,1,0:T(8,128)(2,1)S(1)}, u32[]{:S(2)}, u32[]{:S(2)}) async-start(bf16[8,16,1024]{2,1,0:T(8,128)(2,1)} %bitcast.12), calls=%async_computation.1 | async-start | bytes 524288 | tf_op jit(solution)/shard_map/all_to_all | solution.py:39
  96.2 1.5 %copy-done.4 = bf16[2,512,896]{2,1,0:T(8,128)(2,1)S(1)} copy-done((bf16[2,512,896]{2,1,0:T(8,128)(2,1)S(1)}, bf16[2,512,896]{2,1,0:T(8,128)(2,1)}, u32[]{:S(2)}) %copy-start.4) | copy-done | bytes 1835032
  97.7 5.0 %weight_grads.1 = (bf16[1024,896]{1,0:T(8,128)(2,1)}, bf16[1024,896]{1,0:T(8,128)(2,1)}, bf16[1024,896]{1,0:T(8,128)(2,1)}) custom-call(bf16[8,16,1024]{2,1,0:T(8,128)(2,1)S(1)} %get-tuple-element.79.refs_0_, bf16[8,16,1024]{2,1,0:T(8,128)(2,1)S(1)} %collective-permute-done.12.refs_1_, bf16[8,16,1024]{2,1,0:T(8,128)(2,1)S(1)} %collective-permute-done.13.refs_2_, ...), custom_call_target="tpu_custom_call" | custom-call | flops 2818572288 | bytes 5505024 | tf_op jit(solution)/shard_map/weight_grads/pallas_call | solution.py:196
  102.7 3.6 %all-to-all-done.1 = bf16[8,16,1024]{2,1,0:T(8,128)(2,1)S(1)} async-done(((bf16[8,16,1024]{2,1,0:T(8,128)(2,1)}), bf16[8,16,1024]{2,1,0:T(8,128)(2,1)S(1)}, u32[]{:S(2)}, u32[]{:S(2)}) %all-to-all-start.1) | async-done | bytes 262176 | tf_op jit(solution)/shard_map/all_to_all | solution.py:39
  (57 shorter events, 11.8 us)
Async XLA Ops:
  0.6 10.5 %copy-start.5 = (bf16[4,16,896]{2,1,0:T(8,128)(2,1)S(1)}, bf16[4,16,896]{2,1,0:T(8,128)(2,1)}, u32[]{:S(2)}) copy-start(bf16[4,16,896]{2,1,0:T(8,128)(2,1)} %param.9) | copy-start | bytes 344068
  0.6 10.6 %copy-start.6 = (bf16[4,16,896]{2,1,0:T(8,128)(2,1)S(1)}, bf16[4,16,896]{2,1,0:T(8,128)(2,1)}, u32[]{:S(2)}) copy-start(bf16[4,16,896]{2,1,0:T(8,128)(2,1)} %param.10) | copy-start | bytes 344068
  2.5 23.6 %all-to-all-start = ((bf16[8,2,4,4,1024]{4,3,2,1,0:T(4,128)(2,1)}), bf16[8,2,4,4,1024]{4,3,2,1,0:T(4,128)(2,1)S(1)}, u32[]{:S(2)}, u32[]{:S(2)}) async-start(bf16[8,2,4,4,1024]{4,3,2,1,0:T(4,128)(2,1)} %broadcast_in_dim.3), calls=%async_computation | async-start | bytes 1048576 | tf_op jit(solution)/shard_map/all_to_all | solution.py:39
  11.5 10.2 %collective-permute-start.1 = (bf16[2,4,16,896]{3,2,1,0:T(8,128)(2,1)S(1)}, bf16[2,4,16,896]{3,2,1,0:T(8,128)(2,1)S(1)}, u32[]{:S(2)}, u32[]{:S(2)}) collective-permute-start(bf16[2,4,16,896]{3,2,1,0:T(8,128)(2,1)S(1)} %get-tuple-element.95), channel_id=1, source_target_pairs={{128,0},{160,32},{192,64},{224,96},{0,128},{32,160},{64,192},{96,2... | collective-permute-start | bytes 688136 | tf_op jit(solution)/shard_map/ppermute | solution.py:27
  15.3 10.1 %collective-permute-start = (bf16[2,4,16,896]{3,2,1,0:T(8,128)(2,1)S(1)}, bf16[2,4,16,896]{3,2,1,0:T(8,128)(2,1)S(1)}, u32[]{:S(2)}, u32[]{:S(2)}) collective-permute-start(bf16[2,4,16,896]{3,2,1,0:T(8,128)(2,1)S(1)} %get-tuple-element.95), channel_id=1, source_target_pairs={{64,0},{96,32},{128,64},{160,96},{192,128},{224,160},{0,192},{32,2... | collective-permute-start | bytes 688136 | tf_op jit(solution)/shard_map/ppermute | solution.py:27
  15.8 10.2 %collective-permute-start.2 = (bf16[2,4,16,896]{3,2,1,0:T(8,128)(2,1)S(1)}, bf16[2,4,16,896]{3,2,1,0:T(8,128)(2,1)S(1)}, u32[]{:S(2)}, u32[]{:S(2)}) collective-permute-start(bf16[2,4,16,896]{3,2,1,0:T(8,128)(2,1)S(1)} %get-tuple-element.95), channel_id=1, source_target_pairs={{192,0},{224,32},{0,64},{32,96},{64,128},{96,160},{128,192},{160,2... | collective-permute-start | bytes 688136 | tf_op jit(solution)/shard_map/ppermute | solution.py:27
  26.3 16.7 %copy-start = (bf16[1024,896]{1,0:T(8,128)(2,1)S(1)}, bf16[1024,896]{1,0:T(8,128)(2,1)}, u32[]{:S(2)}) copy-start(bf16[1024,896]{1,0:T(8,128)(2,1)} %refs_4_.3) | copy-start | bytes 5505028
  26.3 5.2 %collective-permute-start.6 = (bf16[4,2,4,16,896]{4,3,2,1,0:T(8,128)(2,1)S(1)}, bf16[4,2,4,16,896]{4,3,2,1,0:T(8,128)(2,1)S(1)}, u32[]{:S(2)}, u32[]{:S(2)}) collective-permute-start(bf16[4,2,4,16,896]{4,3,2,1,0:T(8,128)(2,1)S(1)} %pad_maximum_fusion.mine_ref), channel_id=1, source_target_pairs={{0,32},{32,0},{64,96},{96,64},{128,160},{160,128},{192,224},{224,1... | collective-permute-start | bytes 2752520 | tf_op jit(solution)/shard_map/ppermute | solution.py:35
  26.5 9.2 %collective-permute-start.5 = (bf16[8,16,1024]{2,1,0:T(8,128)(2,1)S(1)}, bf16[8,16,1024]{2,1,0:T(8,128)(2,1)S(1)}, u32[]{:S(2)}, u32[]{:S(2)}) collective-permute-start(bf16[8,16,1024]{2,1,0:T(8,128)(2,1)S(1)} %get-tuple-element.83.refs_0_.refs_4_), channel_id=1, source_target_pairs={{3,0},{0,1},{1,2},{2,3},{7,4},{4,5},{5,6},{6,7},{11,8},{8,9},{9,10... | collective-permute-start | bytes 786440 | tf_op jit(solution)/shard_map/ppermute | solution.py:31
  28.1 10.7 %collective-permute-start.4 = (bf16[8,16,1024]{2,1,0:T(8,128)(2,1)S(1)}, bf16[8,16,1024]{2,1,0:T(8,128)(2,1)S(1)}, u32[]{:S(2)}, u32[]{:S(2)}) collective-permute-start(bf16[8,16,1024]{2,1,0:T(8,128)(2,1)S(1)} %get-tuple-element.83.refs_0_.refs_4_), channel_id=1, source_target_pairs={{2,0},{3,1},{0,2},{1,3},{6,4},{7,5},{4,6},{5,7},{10,8},{11,9},{8,1... | collective-permute-start | bytes 786440 | tf_op jit(solution)/shard_map/ppermute | solution.py:31
  29.1 13.9 %collective-permute-start.3 = (bf16[8,16,1024]{2,1,0:T(8,128)(2,1)S(1)}, bf16[8,16,1024]{2,1,0:T(8,128)(2,1)S(1)}, u32[]{:S(2)}, u32[]{:S(2)}) collective-permute-start(bf16[8,16,1024]{2,1,0:T(8,128)(2,1)S(1)} %get-tuple-element.83.refs_0_.refs_4_), channel_id=1, source_target_pairs={{1,0},{2,1},{3,2},{0,3},{5,4},{6,5},{7,6},{4,7},{9,8},{10,9},{11,1... | collective-permute-start | bytes 786440 | tf_op jit(solution)/shard_map/ppermute | solution.py:31
  43.7 26.5 %copy-start.1 = (bf16[1024,896]{1,0:T(8,128)(2,1)S(1)}, bf16[1024,896]{1,0:T(8,128)(2,1)}, u32[]{:S(2)}) copy-start(bf16[1024,896]{1,0:T(8,128)(2,1)} %refs_9_.1) | copy-start | bytes 5505028
  43.7 26.5 %copy-start.2 = (bf16[1024,896]{1,0:T(8,128)(2,1)S(1)}, bf16[1024,896]{1,0:T(8,128)(2,1)}, u32[]{:S(2)}) copy-start(bf16[1024,896]{1,0:T(8,128)(2,1)} %refs_10_.1) | copy-start | bytes 5505028
  43.7 2.6 %collective-permute-start.7 = (f32[256,896]{1,0:T(8,128)S(1)}, f32[256,896]{1,0:T(8,128)S(1)}, u32[]{:S(2)}, u32[]{:S(2)}) collective-permute-start(f32[256,896]{1,0:T(8,128)S(1)} %half_1.1), channel_id=1, source_target_pairs={{0,32},{32,0},{64,96},{96,64},{128,160},{160,128},{192,224},{224,1... | collective-permute-start | bytes 2752520 | tf_op jit(solution)/shard_map/ppermute | solution.py:35
  47.0 8.8 %collective-permute-start.8 = (bf16[4,16,896]{2,1,0:T(8,128)(2,1)S(1)}, bf16[4,16,896]{2,1,0:T(8,128)(2,1)S(1)}, u32[]{:S(2)}, u32[]{:S(2)}) collective-permute-start(bf16[4,16,896]{2,1,0:T(8,128)(2,1)S(1)} %get-tuple-element.58), channel_id=1, source_target_pairs={{192,0},{224,32},{0,64},{32,96},{64,128},{96,160},{128,192},{160,2... | collective-permute-start | bytes 344072 | tf_op jit(solution)/shard_map/ppermute | solution.py:27
  49.1 8.3 %collective-permute-start.9 = (bf16[4,16,896]{2,1,0:T(8,128)(2,1)S(1)}, bf16[4,16,896]{2,1,0:T(8,128)(2,1)S(1)}, u32[]{:S(2)}, u32[]{:S(2)}) collective-permute-start(bf16[4,16,896]{2,1,0:T(8,128)(2,1)S(1)} %get-tuple-element.59), channel_id=1, source_target_pairs={{128,0},{160,32},{192,64},{224,96},{0,128},{32,160},{64,192},{96,2... | collective-permute-start | bytes 344072 | tf_op jit(solution)/shard_map/ppermute | solution.py:27
  50.7 6.7 %collective-permute-start.10 = (bf16[4,16,896]{2,1,0:T(8,128)(2,1)S(1)}, bf16[4,16,896]{2,1,0:T(8,128)(2,1)S(1)}, u32[]{:S(2)}, u32[]{:S(2)}) collective-permute-start(bf16[4,16,896]{2,1,0:T(8,128)(2,1)S(1)} %get-tuple-element.60), channel_id=1, source_target_pairs={{64,0},{96,32},{128,64},{160,96},{192,128},{224,160},{0,192},{32,2... | collective-permute-start | bytes 344072 | tf_op jit(solution)/shard_map/ppermute | solution.py:27
  53.0 9.2 %collective-permute-start.14 = (bf16[8,16,1024]{2,1,0:T(8,128)(2,1)S(1)}, bf16[8,16,1024]{2,1,0:T(8,128)(2,1)S(1)}, u32[]{:S(2)}, u32[]{:S(2)}) collective-permute-start(bf16[8,16,1024]{2,1,0:T(8,128)(2,1)S(1)} %get-tuple-element.79.refs_0_), channel_id=1, source_target_pairs={{3,0},{0,1},{1,2},{2,3},{7,4},{4,5},{5,6},{6,7},{11,8},{8,9},{9,10... | collective-permute-start | bytes 786440 | tf_op jit(solution)/shard_map/ppermute | solution.py:31
  54.3 10.7 %collective-permute-start.13 = (bf16[8,16,1024]{2,1,0:T(8,128)(2,1)S(1)}, bf16[8,16,1024]{2,1,0:T(8,128)(2,1)S(1)}, u32[]{:S(2)}, u32[]{:S(2)}) collective-permute-start(bf16[8,16,1024]{2,1,0:T(8,128)(2,1)S(1)} %get-tuple-element.79.refs_0_), channel_id=1, source_target_pairs={{2,0},{3,1},{0,2},{1,3},{6,4},{7,5},{4,6},{5,7},{10,8},{11,9},{8,1... | collective-permute-start | bytes 786440 | tf_op jit(solution)/shard_map/ppermute | solution.py:31
  55.8 12.6 %collective-permute-start.12 = (bf16[8,16,1024]{2,1,0:T(8,128)(2,1)S(1)}, bf16[8,16,1024]{2,1,0:T(8,128)(2,1)S(1)}, u32[]{:S(2)}, u32[]{:S(2)}) collective-permute-start(bf16[8,16,1024]{2,1,0:T(8,128)(2,1)S(1)} %get-tuple-element.79.refs_0_), channel_id=1, source_target_pairs={{1,0},{2,1},{3,2},{0,3},{5,4},{6,5},{7,6},{4,7},{9,8},{10,9},{11,1... | collective-permute-start | bytes 786440 | tf_op jit(solution)/shard_map/ppermute | solution.py:31
  57.5 10.9 %collective-permute-start.11 = (bf16[4,16,896]{2,1,0:T(8,128)(2,1)S(1)}, bf16[4,16,896]{2,1,0:T(8,128)(2,1)S(1)}, u32[]{:S(2)}, u32[]{:S(2)}) collective-permute-start(bf16[4,16,896]{2,1,0:T(8,128)(2,1)S(1)} %add_convert_fusion.1.refs_0_), channel_id=1, source_target_pairs={{64,0},{96,32},{128,64},{160,96},{192,128},{224,160},{0,192},{32,2... | collective-permute-start | bytes 344072 | tf_op jit(solution)/shard_map/ppermute | solution.py:27
  59.9 8.5 %collective-permute-start.16 = (bf16[4,16,896]{2,1,0:T(8,128)(2,1)S(1)}, bf16[4,16,896]{2,1,0:T(8,128)(2,1)S(1)}, u32[]{:S(2)}, u32[]{:S(2)}) collective-permute-start(bf16[4,16,896]{2,1,0:T(8,128)(2,1)S(1)} %add_convert_fusion.1.refs_0_), channel_id=1, source_target_pairs={{192,0},{224,32},{0,64},{32,96},{64,128},{96,160},{128,192},{160,2... | collective-permute-start | bytes 344072 | tf_op jit(solution)/shard_map/ppermute | solution.py:27
  62.2 6.3 %collective-permute-start.15 = (bf16[4,16,896]{2,1,0:T(8,128)(2,1)S(1)}, bf16[4,16,896]{2,1,0:T(8,128)(2,1)S(1)}, u32[]{:S(2)}, u32[]{:S(2)}) collective-permute-start(bf16[4,16,896]{2,1,0:T(8,128)(2,1)S(1)} %add_convert_fusion.1.refs_0_), channel_id=1, source_target_pairs={{128,0},{160,32},{192,64},{224,96},{0,128},{32,160},{64,192},{96,2... | collective-permute-start | bytes 344072 | tf_op jit(solution)/shard_map/ppermute | solution.py:27
  65.0 4.0 %collective-permute-start.17 = (bf16[4,16,896]{2,1,0:T(8,128)(2,1)S(1)}, bf16[4,16,896]{2,1,0:T(8,128)(2,1)S(1)}, u32[]{:S(2)}, u32[]{:S(2)}) collective-permute-start(bf16[4,16,896]{2,1,0:T(8,128)(2,1)S(1)} %add_convert_fusion.1.refs_0_), channel_id=1, source_target_pairs={{0,32},{32,0},{64,96},{96,64},{128,160},{160,128},{192,224},{224,1... | collective-permute-start | bytes 344072 | tf_op jit(solution)/shard_map/ppermute | solution.py:35
  68.4 1.3 %collective-permute-start.20 = (bf16[4,16,896]{2,1,0:T(8,128)(2,1)S(1)}, bf16[4,16,896]{2,1,0:T(8,128)(2,1)S(1)}, u32[]{:S(2)}, u32[]{:S(2)}) collective-permute-start(bf16[4,16,896]{2,1,0:T(8,128)(2,1)S(1)} %collective-permute-done.16.refs_3_), channel_id=1, source_target_pairs={{0,32},{32,0},{64,96},{96,64},{128,160},{160,128},{192,224},{224,1... | collective-permute-start | bytes 344072 | tf_op jit(solution)/shard_map/ppermute | solution.py:35
  68.5 1.4 %collective-permute-start.19 = (bf16[4,16,896]{2,1,0:T(8,128)(2,1)S(1)}, bf16[4,16,896]{2,1,0:T(8,128)(2,1)S(1)}, u32[]{:S(2)}, u32[]{:S(2)}) collective-permute-start(bf16[4,16,896]{2,1,0:T(8,128)(2,1)S(1)} %collective-permute-done.15.refs_2_), channel_id=1, source_target_pairs={{0,32},{32,0},{64,96},{96,64},{128,160},{160,128},{192,224},{224,1... | collective-permute-start | bytes 344072 | tf_op jit(solution)/shard_map/ppermute | solution.py:35
  68.9 1.3 %collective-permute-start.18 = (bf16[4,16,896]{2,1,0:T(8,128)(2,1)S(1)}, bf16[4,16,896]{2,1,0:T(8,128)(2,1)S(1)}, u32[]{:S(2)}, u32[]{:S(2)}) collective-permute-start(bf16[4,16,896]{2,1,0:T(8,128)(2,1)S(1)} %collective-permute-done.11.refs_1_), channel_id=1, source_target_pairs={{0,32},{32,0},{64,96},{96,64},{128,160},{160,128},{192,224},{224,1... | collective-permute-start | bytes 344072 | tf_op jit(solution)/shard_map/ppermute | solution.py:35
  73.9 9.1 %collective-permute-start.21 = (bf16[128,1024]{1,0:T(8,128)(2,1)S(1)}, bf16[128,1024]{1,0:T(8,128)(2,1)S(1)}, u32[]{:S(2)}, u32[]{:S(2)}) collective-permute-start(bf16[128,1024]{1,0:T(8,128)(2,1)S(1)} %get-tuple-element.69), channel_id=1, source_target_pairs={{3,0},{0,1},{1,2},{2,3},{7,4},{4,5},{5,6},{6,7},{11,8},{8,9},{9,10... | collective-permute-start | bytes 786440 | tf_op jit(solution)/shard_map/ppermute | solution.py:31
  74.8 10.7 %collective-permute-start.22 = (bf16[128,1024]{1,0:T(8,128)(2,1)S(1)}, bf16[128,1024]{1,0:T(8,128)(2,1)S(1)}, u32[]{:S(2)}, u32[]{:S(2)}) collective-permute-start(bf16[128,1024]{1,0:T(8,128)(2,1)S(1)} %get-tuple-element.70), channel_id=1, source_target_pairs={{2,0},{3,1},{0,2},{1,3},{6,4},{7,5},{4,6},{5,7},{10,8},{11,9},{8,1... | collective-permute-start | bytes 786440 | tf_op jit(solution)/shard_map/ppermute | solution.py:31
  77.3 12.8 %collective-permute-start.23 = (bf16[128,1024]{1,0:T(8,128)(2,1)S(1)}, bf16[128,1024]{1,0:T(8,128)(2,1)S(1)}, u32[]{:S(2)}, u32[]{:S(2)}) collective-permute-start(bf16[128,1024]{1,0:T(8,128)(2,1)S(1)} %get-tuple-element.71), channel_id=1, source_target_pairs={{1,0},{2,1},{3,2},{0,3},{5,4},{6,5},{7,6},{4,7},{9,8},{10,9},{11,1... | collective-permute-start | bytes 786440 | tf_op jit(solution)/shard_map/ppermute | solution.py:31
  91.0 15.2 %all-to-all-start.1 = ((bf16[8,16,1024]{2,1,0:T(8,128)(2,1)}), bf16[8,16,1024]{2,1,0:T(8,128)(2,1)S(1)}, u32[]{:S(2)}, u32[]{:S(2)}) async-start(bf16[8,16,1024]{2,1,0:T(8,128)(2,1)} %bitcast.12), calls=%async_computation.1 | async-start | bytes 524288 | tf_op jit(solution)/shard_map/all_to_all | solution.py:39
  96.2 1.5 %copy-start.4 = (bf16[2,512,896]{2,1,0:T(8,128)(2,1)S(1)}, bf16[2,512,896]{2,1,0:T(8,128)(2,1)}, u32[]{:S(2)}) copy-start(bf16[2,512,896]{2,1,0:T(8,128)(2,1)} %copy-done.3) | copy-start | bytes 5505028
  (1 other events, 1.2 us)
